TPU v7x, 32 devices: a whole 2x2x4 slice. The times are simulated.
32 devices in a mesh: fsdp: 8 (over y, x, core), dp: 4 (over z).
Axes of the slice: x: 2, y: 2, z: 4, core: 2. Of those that a mesh axis runs over, the one named last changes fastest.
Arguments:
- enc_input: bfloat16 [64, 512, 512], P(('fsdp', 'dp')), may hold values from -6 to 6
- segments: int32 [64, 512], P(('fsdp', 'dp')), may hold values from 0 to 3, never falling along the last dimension, each value on 1 to 256 neighbouring positions
- targets: int32 [64, 64], P(('fsdp', 'dp')), may hold values from 0 to 4095
- enc_cot: bfloat16 [64, 512, 512], P(('fsdp', 'dp')), may hold values from -6 to 6
- dec_cot: bfloat16 [64, 64, 512], P(('fsdp', 'dp')), may hold values from -6 to 6
- enc_gains: bfloat16 [2, 512], P(None, 'fsdp'), may hold values from 0.5 to 1.5
- enc_attn: bfloat16 [4, 512, 512], P(None, 'fsdp'), may hold values from -0.375 to 0.375
- enc_table: bfloat16 [256], P('fsdp'), may hold values from -4 to 4
- enc_up: bfloat16 [512, 2048], P('fsdp'), may hold values from -0.25 to 0.25
- enc_down: bfloat16 [2048, 512], P('fsdp'), may hold values from -0.125 to 0.125
- embed: bfloat16 [4096, 512], P('fsdp'), may hold values from -6 to 6
- dec_gains: bfloat16 [3, 512], P(None, 'fsdp'), may hold values from 0.5 to 1.5
- dec_self: bfloat16 [4, 512, 512], P(None, 'fsdp'), may hold values from -0.375 to 0.375
- dec_cross: bfloat16 [4, 512, 512], P(None, 'fsdp'), may hold values from -0.375 to 0.375
- dec_table: bfloat16 [256], P('fsdp'), may hold values from -4 to 4
- dec_up: bfloat16 [512, 2048], P('fsdp'), may hold values from -0.25 to 0.25
- dec_down: bfloat16 [2048, 512], P('fsdp'), may hold values from -0.125 to 0.125
Outputs:
- enc_out: bfloat16 [64, 512, 512], P(('fsdp', 'dp'))
- dec_out: bfloat16 [64, 64, 512], P(('fsdp', 'dp'))
- grad_input: float32 [64, 512, 512], P(('fsdp', 'dp'))
- grad_memory: float32 [64, 512, 512], P(('fsdp', 'dp'))
- grad_enc_gains: float32 [2, 512], P(None, 'fsdp')
- grad_enc_attn: float32 [4, 512, 512], P(None, 'fsdp')
- grad_enc_table: float32 [256], P('fsdp')
- grad_enc_up: float32 [512, 2048], P('fsdp')
- grad_enc_down: float32 [2048, 512], P('fsdp')
- grad_embed: float32 [4096, 512], P('fsdp')
- grad_dec_gains: float32 [3, 512], P(None, 'fsdp')
- grad_dec_self: float32 [4, 512, 512], P(None, 'fsdp')
- grad_dec_cross: float32 [4, 512, 512], P(None, 'fsdp')
- grad_dec_table: float32 [256], P('fsdp')
- grad_dec_up: float32 [512, 2048], P('fsdp')
- grad_dec_down: float32 [2048, 512], P('fsdp')
Inputs may be any that keep to these rules, and one draw needn't show every extreme that they name: `segments`: along each row the series numbers never fall; each series holds 1 to 256 positions, and some series holds exactly 256.
All inputs are finite; a program needn't handle non-finite values.
Results may differ from a plain program's by a relative error of at most 0.028.
The roundings to bfloat16 on the way count: a program that leaves them out, or rounds other values in their place, can miss the bound.
Values may be sent and summed in bfloat16 or wider, within the bound.
No kernel may reach another device: no remote copies, remote signals or barrier semaphores. Data moves between devices by JAX's collectives and lax.ppermute only.
A program may use at most 256 MiB of HBM per device.

v0:
```python
import jax
import jax.numpy as jnp
import numpy as np
from jax import lax
from jax.sharding import PartitionSpec as P

HEADS = 8
HEAD_DIM = 64
BUCKETS = 32
MICRO = 2


epsilon = 1e-06


def bucket_codes(length, both_ways):
    bucket_list = []
    for offset in range(-(length - 1), length):
        if both_ways:
            upper_half = 16 if offset > 0 else 0
            distance = abs(offset)
            if distance < 8:
                bucket = distance
            else:
                bucket = 8 + sum(
                    (1 for exponent in range(1, 8) if distance * distance >= 64 * 2**exponent)
                )
        else:
            upper_half = 0
            distance = max(-offset, 0)
            if distance < 16:
                bucket = distance
            else:
                bucket = 16 + sum(
                    (1 for exponent in range(1, 16) if distance**16 >= 16**16 * 2 ** (3 * exponent))
                )
        bucket_list.append(upper_half + bucket)
    return np.array(bucket_list, dtype=np.int32)


def spread_diagonals(by_offset, length):
    heads_now = by_offset.shape[0]
    padded = jnp.pad(by_offset, ((0, 0), (0, 1)))
    repeated = jnp.tile(padded, (1, length))[:, : length * (2 * length - 1)]
    return repeated.reshape(heads_now, length, 2 * length - 1)[:, :, length - 1 :]


def diagonal_sums(score_sum):
    heads_now, length, _ = score_sum.shape
    padded = jnp.pad(score_sum, ((0, 0), (0, 0), (length - 1, 0))).reshape(
        heads_now, length * (2 * length - 1)
    )
    padded = jnp.pad(padded, ((0, 0), (0, length))).reshape(heads_now, length, 2 * length)
    return jnp.sum(padded, axis=1, dtype=jnp.float32)[:, : 2 * length - 1]


def relative_bias(bias_table, buckets, length):
    table_grid = bias_table.astype(jnp.float32).reshape(HEADS, BUCKETS)
    picked = buckets[None, None, :] == jnp.arange(BUCKETS)[None, :, None]
    by_offset = jnp.sum(jnp.where(picked, table_grid[:, :, None], 0.0), axis=1)
    return spread_diagonals(by_offset.astype(jnp.bfloat16), length)


def bias_gradient(diag_totals, buckets):
    picked = buckets[None, None, :] == jnp.arange(BUCKETS)[None, :, None]
    return jnp.sum(jnp.where(picked, diag_totals[:, None, :], 0.0), axis=2).reshape(-1)


def forward_dot(left_side, right_side):
    return jnp.dot(left_side, right_side, preferred_element_type=jnp.float32)


def weight_grad(activation, gradient):
    return lax.dot_general(
        activation, gradient, (((0,), (0,)), ((), ())), preferred_element_type=jnp.float32
    )


def input_grad(gradient, matrix):
    return lax.dot_general(
        gradient, matrix, (((1,), (1,)), ((), ())), preferred_element_type=jnp.float32
    )


def normalize(tensor, scales):
    factor = lax.rsqrt(jnp.mean(tensor * tensor, axis=-1, keepdims=True) + epsilon)
    return tensor * factor * scales.astype(jnp.float32)


def normalize_back(tensor, scales, grad_norm):
    factor = lax.rsqrt(jnp.mean(tensor * tensor, axis=-1, keepdims=True) + epsilon)
    normed_unit = tensor * factor
    grad_unit = grad_norm * scales.astype(jnp.float32)
    grad_in = factor * (
        grad_unit - normed_unit * jnp.mean(grad_unit * normed_unit, axis=-1, keepdims=True)
    )
    return (grad_in, jnp.sum(grad_norm * normed_unit, axis=0))


def split_heads(tensor):
    return tensor.reshape(tensor.shape[0], tensor.shape[1], HEADS, HEAD_DIM)


def score_grid(queries, keyset, position, allowed):
    scores = jnp.einsum(
        "bqhd,bkhd->bhqk",
        split_heads(queries),
        split_heads(keyset),
        preferred_element_type=jnp.float32,
    )
    if position is not None:
        scores = scores + position[None].astype(jnp.float32)
    return jnp.where(allowed[:, None], scores, -1000000000.0)


def attend(queries, keyset, values, position, allowed):
    scores = score_grid(queries, keyset, position, allowed)
    highest = jnp.max(scores, axis=-1, keepdims=True)
    scaled = jnp.exp(scores - highest)
    totals = jnp.sum(scaled, axis=-1, keepdims=True)
    weights = (scaled / totals).astype(jnp.bfloat16)
    blended = jnp.einsum(
        "bhqk,bkhd->bqhd", weights, split_heads(values), preferred_element_type=jnp.float32
    )
    return (blended.reshape(queries.shape).astype(jnp.bfloat16), highest + jnp.log(totals))


def attend_back(queries, keyset, values, position, allowed, log_total, grad_out):
    weights = jnp.exp(score_grid(queries, keyset, position, allowed) - log_total)
    grad_weights = jnp.einsum(
        "bqhd,bkhd->bhqk",
        split_heads(grad_out),
        split_heads(values),
        preferred_element_type=jnp.float32,
    )
    grad_score = (
        weights * (grad_weights - jnp.sum(grad_weights * weights, axis=-1, keepdims=True))
    ).astype(jnp.bfloat16)
    grad_query = jnp.einsum(
        "bhqk,bkhd->bqhd", grad_score, split_heads(keyset), preferred_element_type=jnp.float32
    )
    grad_key = jnp.einsum(
        "bhqk,bqhd->bkhd", grad_score, split_heads(queries), preferred_element_type=jnp.float32
    )
    grad_value = jnp.einsum(
        "bhqk,bqhd->bkhd",
        weights.astype(jnp.bfloat16),
        split_heads(grad_out),
        preferred_element_type=jnp.float32,
    )
    return (
        grad_query.reshape(queries.shape).astype(jnp.bfloat16),
        grad_key.reshape(keyset.shape).astype(jnp.bfloat16),
        grad_value.reshape(values.shape).astype(jnp.bfloat16),
        grad_score,
    )


def feed_forward(hidden, scales, up_weights, down_weights):
    normalized_state = normalize(hidden, scales).astype(jnp.bfloat16)
    pre_act = forward_dot(normalized_state, up_weights)
    active = jax.nn.gelu(pre_act).astype(jnp.bfloat16)
    return (hidden + forward_dot(active, down_weights), (normalized_state, pre_act, active))


def feed_back(hidden, scales, up_weights, down_weights, stored, grad_y):
    normalized_state, pre_act, active = stored
    grad_branch = grad_y.astype(jnp.bfloat16)
    grad_down = weight_grad(active, grad_branch)
    _, gelu_pull = jax.vjp(jax.nn.gelu, pre_act)
    grad_pre = gelu_pull(input_grad(grad_branch, down_weights))[0].astype(jnp.bfloat16)
    grad_up = weight_grad(normalized_state, grad_pre)
    grad_hidden, grad_scale = normalize_back(hidden, scales, input_grad(grad_pre, up_weights))
    return (grad_y + grad_hidden, grad_scale, grad_up, grad_down)


def project_three(normalized_state, projection_weights):
    return jnp.einsum(
        "zc,hcg->hzg", normalized_state, projection_weights[:3], preferred_element_type=jnp.float32
    ).astype(jnp.bfloat16)


def encoder_forward(inputs, segment, weights, buckets):
    gain_rows, projection_weights, bias_table, up_weights, down_weights = weights
    row_count, length, width = inputs.shape
    inputs = inputs.reshape(-1, width).astype(jnp.float32)
    normalized_state = normalize(inputs, gain_rows[0]).astype(jnp.bfloat16)
    triple = project_three(normalized_state, projection_weights).reshape(
        3, row_count, length, width
    )
    position = relative_bias(bias_table, buckets, length)
    allowed = segment[:, :, None] == segment[:, None, :]

    def one_row(row_item):
        queries, keyset, values, mask_row = row_item
        blended, log_total = attend(
            queries[None], keyset[None], values[None], position, mask_row[None]
        )
        return (blended[0], log_total[0])

    blended, log_total = lax.map(one_row, (triple[0], triple[1], triple[2], allowed))
    blended = blended.reshape(-1, width)
    hidden = inputs + forward_dot(blended, projection_weights[3])
    output, dense_kept = feed_forward(hidden, gain_rows[1], up_weights, down_weights)
    return (
        output,
        (
            inputs,
            normalized_state,
            triple,
            allowed,
            log_total,
            blended,
            hidden,
            dense_kept,
            position,
        ),
    )


def encoder_backward(weights, buckets, stored, grad_y):
    gain_rows, projection_weights, bias_table, up_weights, down_weights = weights
    inputs, normalized_state, triple, allowed, log_total, blended, hidden, dense_kept, position = (
        stored
    )
    length = allowed.shape[1]
    width = inputs.shape[-1]
    grad_hidden, grad_gain_b, grad_up, grad_down = feed_back(
        hidden, gain_rows[1], up_weights, down_weights, dense_kept, grad_y
    )
    grad_branch = grad_hidden.astype(jnp.bfloat16)
    grad_out_proj = weight_grad(blended, grad_branch)
    grad_blended = (
        input_grad(grad_branch, projection_weights[3])
        .astype(jnp.bfloat16)
        .reshape(triple.shape[1:])
    )

    def one_row(diag_totals, row_item):
        queries, keyset, values, mask_row, total_row, grad_row = row_item
        grad_query, grad_key, grad_value, grad_score = attend_back(
            queries[None],
            keyset[None],
            values[None],
            position,
            mask_row[None],
            total_row[None],
            grad_row[None],
        )
        diag_totals = diag_totals + diagonal_sums(grad_score[0])
        return (diag_totals, (grad_query[0], grad_key[0], grad_value[0]))

    zero_sums = jnp.zeros((HEADS, 2 * length - 1), jnp.float32)
    diag_totals, grad_parts = lax.scan(
        one_row, zero_sums, (triple[0], triple[1], triple[2], allowed, log_total, grad_blended)
    )
    gradient_query_key_value = jnp.stack(grad_parts).reshape(3, -1, width)
    grad_proj_three = jnp.einsum(
        "cm,kcv->kmv",
        normalized_state,
        gradient_query_key_value,
        preferred_element_type=jnp.float32,
    )
    grad_normed = jnp.einsum(
        "gvt,gpt->vp",
        gradient_query_key_value,
        projection_weights[:3],
        preferred_element_type=jnp.float32,
    )
    grad_in, grad_gain_a = normalize_back(inputs, gain_rows[0], grad_normed)
    gradients = (
        jnp.stack([grad_gain_a, grad_gain_b]),
        jnp.concatenate([grad_proj_three, grad_out_proj[None]], axis=0),
        bias_gradient(diag_totals, buckets),
        grad_up,
        grad_down,
    )
    return (grad_hidden + grad_in, gradients)


def decoder_forward(encoder_memory, segment, embedded, weights, buckets):
    (
        gain_rows,
        self_projection_weight,
        cross_projection_weight,
        bias_table,
        up_weights,
        down_weights,
    ) = weights
    row_count, length = segment.shape
    width = encoder_memory.shape[-1]
    steps_now = embedded.shape[0] // row_count
    normalized_first = normalize(embedded, gain_rows[0]).astype(jnp.bfloat16)
    triple = project_three(normalized_first, self_projection_weight).reshape(
        3, row_count, steps_now, width
    )
    position = relative_bias(bias_table, buckets, steps_now)
    places = jnp.arange(steps_now)
    causal = places[None, :, None] >= places[None, None, :]
    blended_a, total_a = attend(triple[0], triple[1], triple[2], position, causal)
    blended_a = blended_a.reshape(-1, width)
    hidden_a = embedded + forward_dot(blended_a, self_projection_weight[3])
    normed_b = normalize(hidden_a, gain_rows[1]).astype(jnp.bfloat16)
    cross_query = (
        forward_dot(normed_b, cross_projection_weight[0])
        .astype(jnp.bfloat16)
        .reshape(row_count, steps_now, width)
    )
    cross_pair = (
        jnp.einsum(
            "zc,hcg->hzg",
            encoder_memory,
            cross_projection_weight[1:3],
            preferred_element_type=jnp.float32,
        )
        .astype(jnp.bfloat16)
        .reshape(2, row_count, -1, width)
    )
    allowed = jnp.broadcast_to(
        (segment == segment[:, -1:])[:, None, :], (row_count, steps_now, length)
    )
    blended_b, total_b = attend(cross_query, cross_pair[0], cross_pair[1], None, allowed)
    blended_b = blended_b.reshape(-1, width)
    hidden_b = hidden_a + forward_dot(blended_b, cross_projection_weight[3])
    output, dense_kept = feed_forward(hidden_b, gain_rows[2], up_weights, down_weights)
    stored = (
        embedded,
        normalized_first,
        triple,
        causal,
        total_a,
        blended_a,
        hidden_a,
        normed_b,
        cross_query,
        cross_pair,
        allowed,
        total_b,
        blended_b,
        hidden_b,
        dense_kept,
        position,
    )
    return (output, stored)


def decoder_backward(encoder_memory, weights, buckets, stored, grad_y):
    (
        gain_rows,
        self_projection_weight,
        cross_projection_weight,
        bias_table,
        up_weights,
        down_weights,
    ) = weights
    (
        embedded,
        normalized_first,
        triple,
        causal,
        total_a,
        blended_a,
        hidden_a,
        normed_b,
        cross_query,
        cross_pair,
        allowed,
        total_b,
        blended_b,
        hidden_b,
        dense_kept,
        position,
    ) = stored
    width = encoder_memory.shape[-1]
    grad_b, grad_gain_c, grad_up, grad_down = feed_back(
        hidden_b, gain_rows[2], up_weights, down_weights, dense_kept, grad_y
    )
    branch_b = grad_b.astype(jnp.bfloat16)
    grad_cross_out = weight_grad(blended_b, branch_b)
    grad_blended_b = (
        input_grad(branch_b, cross_projection_weight[3])
        .astype(jnp.bfloat16)
        .reshape(cross_query.shape)
    )
    grad_query_b, grad_key_b, grad_value_b, _ = attend_back(
        cross_query, cross_pair[0], cross_pair[1], None, allowed, total_b, grad_blended_b
    )
    grad_query_b = grad_query_b.reshape(-1, width)
    gradient_key_value_pair = jnp.stack([grad_key_b, grad_value_b]).reshape(2, -1, width)
    grad_cross_query = weight_grad(normed_b, grad_query_b)
    grad_cross_pair = jnp.einsum(
        "cm,kcv->kmv", encoder_memory, gradient_key_value_pair, preferred_element_type=jnp.float32
    )
    grad_memory = jnp.einsum(
        "gvt,gpt->vp",
        gradient_key_value_pair,
        cross_projection_weight[1:3],
        preferred_element_type=jnp.float32,
    )
    grad_hidden, grad_gain_b = normalize_back(
        hidden_a, gain_rows[1], input_grad(grad_query_b, cross_projection_weight[0])
    )
    grad_a = grad_b + grad_hidden
    branch_a = grad_a.astype(jnp.bfloat16)
    grad_self_out = weight_grad(blended_a, branch_a)
    grad_blended_a = (
        input_grad(branch_a, self_projection_weight[3])
        .astype(jnp.bfloat16)
        .reshape(triple.shape[1:])
    )
    grad_query, grad_key, grad_value, grad_score = attend_back(
        triple[0], triple[1], triple[2], position, causal, total_a, grad_blended_a
    )
    gradient_query_key_value = jnp.stack([grad_query, grad_key, grad_value]).reshape(3, -1, width)
    grad_self_three = jnp.einsum(
        "cm,kcv->kmv",
        normalized_first,
        gradient_query_key_value,
        preferred_element_type=jnp.float32,
    )
    grad_normed = jnp.einsum(
        "gvt,gpt->vp",
        gradient_query_key_value,
        self_projection_weight[:3],
        preferred_element_type=jnp.float32,
    )
    grad_embedded, grad_gain_a = normalize_back(embedded, gain_rows[0], grad_normed)
    grad_rows = (grad_a + grad_embedded).astype(jnp.bfloat16)
    table_grad = bias_gradient(
        diagonal_sums(jnp.sum(grad_score.astype(jnp.float32), axis=0)), buckets
    )
    gradients = (
        jnp.stack([grad_gain_a, grad_gain_b, grad_gain_c]),
        jnp.concatenate([grad_self_three, grad_self_out[None]], axis=0),
        jnp.concatenate([grad_cross_query[None], grad_cross_pair, grad_cross_out[None]], axis=0),
        table_grad,
        grad_up,
        grad_down,
    )
    return (grad_memory, grad_rows, gradients)


def on_device(
    enc_input,
    segments,
    targets,
    enc_cot,
    dec_cot,
    enc_gains,
    enc_attn,
    enc_table,
    enc_up,
    enc_down,
    embed,
    dec_gains,
    dec_self,
    dec_cross,
    dec_table,
    dec_up,
    dec_down,
):
    per_micro = enc_input.shape[0] // MICRO
    length = enc_input.shape[1]
    width = enc_input.shape[2]
    steps_now = targets.shape[1]
    enc_buckets = jnp.asarray(bucket_codes(length, True))
    dec_buckets = jnp.asarray(bucket_codes(steps_now, False))
    shard_rows = embed.shape[0]
    group_size = lax.axis_size("fsdp")
    row_offset = lax.axis_index("fsdp") * shard_rows
    kept_encoder = tuple(
        (
            lax.all_gather(enc_gains, "fsdp", axis=1, tiled=True),
            lax.all_gather(enc_attn, "fsdp", axis=1, tiled=True),
            lax.all_gather(enc_table, "fsdp", axis=0, tiled=True),
            lax.all_gather(enc_up, "fsdp", axis=0, tiled=True),
            lax.all_gather(enc_down, "fsdp", axis=0, tiled=True),
        )
    )
    kept_decoder = (embed,) + tuple(
        (
            lax.all_gather(dec_gains, "fsdp", axis=1, tiled=True),
            lax.all_gather(dec_self, "fsdp", axis=1, tiled=True),
            lax.all_gather(dec_cross, "fsdp", axis=1, tiled=True),
            lax.all_gather(dec_table, "fsdp", axis=0, tiled=True),
            lax.all_gather(dec_up, "fsdp", axis=0, tiled=True),
            lax.all_gather(dec_down, "fsdp", axis=0, tiled=True),
        )
    )
    totals = None
    enc_outs = []
    dec_outs = []
    input_grads = []
    memory_grads = []
    for micro_step in range(MICRO):
        row_start = micro_step * per_micro
        row_stop = row_start + per_micro
        segment_now = segments[row_start:row_stop]
        target_now = targets[row_start:row_stop]
        shifted = jnp.concatenate(
            [jnp.zeros((per_micro, 1), jnp.int32), target_now[:, :-1]], axis=1
        ).reshape(-1)
        encoder_memory, enc_stored = encoder_forward(
            enc_input[row_start:row_stop], segment_now, kept_encoder, enc_buckets
        )
        encoder_memory = encoder_memory.astype(jnp.bfloat16)
        all_ids = lax.all_gather(shifted, "fsdp", axis=0, tiled=True)
        local_hot = (all_ids[:, None] == row_offset + jnp.arange(shard_rows)[None, :]).astype(
            jnp.bfloat16
        )
        owned = forward_dot(local_hot, embed).astype(jnp.bfloat16).reshape(group_size, -1, width)
        returned = lax.all_to_all(owned, "fsdp", split_axis=0, concat_axis=0, tiled=True)
        embedded = jnp.sum(returned.astype(jnp.float32), axis=0)
        result, dec_stored = decoder_forward(
            encoder_memory, segment_now, embedded, kept_decoder[1:], dec_buckets
        )
        grad_dec_out = dec_cot[row_start:row_stop].reshape(-1, width).astype(jnp.float32)
        grad_memory, grad_rows, dec_gradients = decoder_backward(
            encoder_memory, kept_decoder[1:], dec_buckets, dec_stored, grad_dec_out
        )
        gathered_rows = lax.all_gather(grad_rows, "fsdp", axis=0, tiled=True)
        grad_embed = weight_grad(local_hot, gathered_rows)
        grad_memory = (
            enc_cot[row_start:row_stop].reshape(-1, width).astype(jnp.float32) + grad_memory
        )
        grad_input, enc_gradients = encoder_backward(
            kept_encoder, enc_buckets, enc_stored, grad_memory
        )
        gradients = enc_gradients + (grad_embed,) + dec_gradients
        totals = gradients if totals is None else jax.tree.map(jnp.add, totals, gradients)
        enc_outs.append(encoder_memory.reshape(per_micro, length, width))
        dec_outs.append(result.astype(jnp.bfloat16).reshape(per_micro, steps_now, width))
        input_grads.append(grad_input.reshape(per_micro, length, width))
        memory_grads.append(grad_memory.reshape(per_micro, length, width))
    others = tuple(
        (
            lax.psum_scatter(totals[0], "fsdp", scatter_dimension=1, tiled=True),
            lax.psum_scatter(totals[1], "fsdp", scatter_dimension=1, tiled=True),
            lax.psum_scatter(totals[2], "fsdp", scatter_dimension=0, tiled=True),
            lax.psum_scatter(totals[3], "fsdp", scatter_dimension=0, tiled=True),
            lax.psum_scatter(totals[4], "fsdp", scatter_dimension=0, tiled=True),
            lax.psum_scatter(totals[6], "fsdp", scatter_dimension=1, tiled=True),
            lax.psum_scatter(totals[7], "fsdp", scatter_dimension=1, tiled=True),
            lax.psum_scatter(totals[8], "fsdp", scatter_dimension=1, tiled=True),
            lax.psum_scatter(totals[9], "fsdp", scatter_dimension=0, tiled=True),
            lax.psum_scatter(totals[10], "fsdp", scatter_dimension=0, tiled=True),
            lax.psum_scatter(totals[11], "fsdp", scatter_dimension=0, tiled=True),
        )
    )
    totals = others[:5] + (totals[5],) + others[5:]
    totals = (
        lax.psum(totals[0].astype(jnp.bfloat16), "dp").astype(jnp.float32),
        lax.psum(totals[1].astype(jnp.bfloat16), "dp").astype(jnp.float32),
        lax.psum(totals[2].astype(jnp.bfloat16), "dp").astype(jnp.float32),
        lax.psum(totals[3].astype(jnp.bfloat16), "dp").astype(jnp.float32),
        lax.psum(totals[4].astype(jnp.bfloat16), "dp").astype(jnp.float32),
        lax.psum(totals[5].astype(jnp.bfloat16), "dp").astype(jnp.float32),
        lax.psum(totals[6].astype(jnp.bfloat16), "dp").astype(jnp.float32),
        lax.psum(totals[7].astype(jnp.bfloat16), "dp").astype(jnp.float32),
        lax.psum(totals[8].astype(jnp.bfloat16), "dp").astype(jnp.float32),
        lax.psum(totals[9].astype(jnp.bfloat16), "dp").astype(jnp.float32),
        lax.psum(totals[10].astype(jnp.bfloat16), "dp").astype(jnp.float32),
        lax.psum(totals[11].astype(jnp.bfloat16), "dp").astype(jnp.float32),
    )
    return (
        jnp.concatenate(enc_outs, axis=0),
        jnp.concatenate(dec_outs, axis=0),
        jnp.concatenate(input_grads, axis=0),
        jnp.concatenate(memory_grads, axis=0),
        totals[0],
        totals[1],
        totals[2],
        totals[3],
        totals[4],
        totals[5],
        totals[6],
        totals[7],
        totals[8],
        totals[9],
        totals[10],
        totals[11],
    )


def solution(mesh):
    placed = (
        P(("fsdp", "dp"), None, None),
        P(("fsdp", "dp"), None),
        P(("fsdp", "dp"), None),
        P(("fsdp", "dp"), None, None),
        P(("fsdp", "dp"), None, None),
        P(None, "fsdp"),
        P(None, "fsdp", None),
        P("fsdp"),
        P("fsdp", None),
        P("fsdp", None),
        P("fsdp", None),
        P(None, "fsdp"),
        P(None, "fsdp", None),
        P(None, "fsdp", None),
        P("fsdp"),
        P("fsdp", None),
        P("fsdp", None),
    )
    return jax.shard_map(
        on_device,
        mesh=mesh,
        in_specs=placed,
        out_specs=(
            P(("fsdp", "dp"), None, None),
            P(("fsdp", "dp"), None, None),
            P(("fsdp", "dp"), None, None),
            P(("fsdp", "dp"), None, None),
            P(None, "fsdp"),
            P(None, "fsdp", None),
            P("fsdp"),
            P("fsdp", None),
            P("fsdp", None),
            P("fsdp", None),
            P(None, "fsdp"),
            P(None, "fsdp", None),
            P(None, "fsdp", None),
            P("fsdp"),
            P("fsdp", None),
            P("fsdp", None),
        ),
        check_vma=False,
    )
```

profile of v0, /device:TPU:0, one launch (start us, length us, event | category | flops | bytes accessed | tf_op | source)
XLA Modules:
  0.0 1034.2 jit_solution(17011742973377527049)
XLA Ops:
  16.7 9.5 all-reduce.19
  27.5 3.5 all-to-all-start
  33.5 18.7 %all-reduce.21 = (bf16[256]{0:T(256)(128)(2,1)S(1)}, bf16[256]{0:T(256)(128)(2,1)S(1)}) all-reduce(bf16[256]{0:T(256)(128)(2,1)S(1)} %dynamic-update-slice, bf16[256]{0:T(256)(128)(2,1)S(1)} %dynamic-update-slice.2), channel_id=1, replica_groups=mesh['fsdp'=8,'dp'=4] {'fsdp'}, use_global_device_ids=true, to_apply=%add.10 | all-reduce | flops 512 | bytes 2048
  52.3 8.9 all-gather.2
  61.9 7.7 all-gather.3
  80.1 3.8 slice.277
  83.9 19.7 %reshape.1512 = bf16[4190208]{0:T(1024)(128)(2,1)} reshape(bf16[8,523776]{1,0:T(8,128)(2,1)} %slice.277) | data formatting | bytes 16760832
  103.6 17.3 %reshape.1389 = bf16[8,512,1023]{2,1,0:T(8,128)(2,1)} reshape(bf16[4190208]{0:T(1024)(128)(2,1)} %reshape.1512) | data formatting | bytes 16760832 | tf_op jit(solution)/shard_map/reshape | solution.py:45
  120.9 7.0 slice.278
  127.9 6.4 copy.615
  138.7 3.5 all-to-all-start.1
  142.4 12.0 %all-to-all-done.1 = bf16[8,64,512]{2,1,0:T(8,128)(2,1)S(1)} async-done(((bf16[8,64,512]{2,1,0:T(8,128)(2,1)}), bf16[8,64,512]{2,1,0:T(8,128)(2,1)S(1)}, u32[]{:S(2)}, u32[]{:S(2)}) %all-to-all-start.1) | async-done | bytes 524320 | tf_op jit(solution)/shard_map/all_to_all | solution.py:512
  160.0 2.8 slice.292
  172.6 2.8 slice.279
  175.5 4.5 copy.614
  201.4 5.6 fusion.237
  207.0 5.0 fusion.68
  224.5 3.1 fusion.234
  267.2 4.1 convolution_add_fusion.2
  280.3 5.8 fusion.12
  290.6 3.7 fusion.19
  295.6 3.3 convolution_add_fusion.3
  330.3 3.8 multiply_reduce_fusion.3
  346.4 5.4 fusion.55
  351.9 4.8 fusion.58
  357.6 3.4 convolution_bitcast_fusion.1
  361.0 3.3 convolution_bitcast_fusion
  364.3 3.7 maximum_add_fusion.2
  368.8 5.6 copy.549
  377.7 6.2 maximum_add_fusion.1
  383.9 5.6 copy.540
  389.4 6.0 multiply_reduce_fusion
  395.5 5.8 multiply_convert_fusion
  401.3 6.6 copy.624
  407.9 3.6 convolution_convert_fusion.6
  412.6 3.0 convolution_convert_fusion.7
  416.6 8.8 pad.50.clone
  425.4 14.2 %reshape.1516 = bf16[4190208]{0:T(1024)(128)(2,1)} reshape(bf16[8,512,1023]{2,1,0:T(8,128)(2,1)} %pad.50.clone) | data formatting | bytes 16760832
  439.6 15.7 %reshape.1429 = bf16[8,523776]{1,0:T(8,128)(2,1)} reshape(bf16[4190208]{0:T(1024)(128)(2,1)} %reshape.1516) | data formatting | bytes 16760832 | tf_op jit(solution)/shard_map/while/body/eval_jaxpr/reshape | solution.py:50
  455.3 5.3 multiply_reduce_fusion.1
  460.6 6.1 multiply_convert_fusion.1
  466.6 6.5 copy.623
  473.1 3.6 convolution_convert_fusion.10
  477.8 3.0 convolution_convert_fusion.11
  483.3 4.6 fusion.86
  489.3 2.7 convolution_add_fusion.1
  492.2 3.1 convolution_bitcast_fusion.14
  500.9 2.8 convolution_bitcast_fusion.2
  505.0 3.0 maximum_add_fusion
  508.1 5.8 copy.519
  513.9 9.4 pad.48.clone
  523.3 14.3 %reshape.1514 = bf16[4190208]{0:T(1024)(128)(2,1)} reshape(bf16[8,512,1023]{2,1,0:T(8,128)(2,1)} %pad.48.clone) | data formatting | bytes 16760832
  537.5 15.7 %reshape.1428 = bf16[8,523776]{1,0:T(8,128)(2,1)} reshape(bf16[4190208]{0:T(1024)(128)(2,1)} %reshape.1514) | data formatting | bytes 16760832 | tf_op jit(solution)/shard_map/while/body/eval_jaxpr/reshape | solution.py:50
  553.2 4.4 pad.51
  567.9 9.6 all_gather.58
  577.5 10.1 all_gather.59
  587.6 249.9 %all-reduce.28 = (bf16[4,512,512]{2,0,1:T(4,128)(2,1)}, bf16[4,512,512]{2,0,1:T(4,128)(2,1)}, bf16[4,512,512]{2,0,1:T(4,128)(2,1)}, bf16[256]{0:T(256)(128)(2,1)S(1)}, bf16[256]{0:T(256)(128)(2,1)S(1)}) all-reduce(f32[4,512,512]{2,0,1:T(4,128)} %copy.519, ...), channel_id=5, replica_groups=mesh['fsdp'=8,'dp'=4] {'fsdp'}, use_global_device_ids=true, to_apply=%region_42.43.clone | all-reduce | flops 3146240 | bytes 18877440
  859.3 2.7 pad_maximum_fusion.1
  862.0 3.0 copy.552
  867.7 2.9 copy.551
  872.5 3.0 reduce-scatter.19.cloned.1.call-done
  876.3 36.7 %reduce-scatter.21.cloned.1.call-done = f32[64,3]{1,0:T(8,128)} async-done(((f32[512,3]{1,0:T(8,128)}), f32[64,3]{1,0:T(8,128)}) %reduce-scatter.21.cloned.1.call-update) | async-done | bytes 784
  913.9 11.8 %all-reduce.22 = (bf16[2,64]{1,0:T(2,128)(2,1)S(1)}, bf16[32]{0:T(256)(128)(2,1)S(1)}, bf16[3,64]{1,0:T(4,128)(2,1)S(1)}, bf16[32]{0:T(256)(128)(2,1)S(1)}) all-reduce(bf16[2,64]{1,0:T(2,128)(2,1)S(1)} %copy.610, bf16[32]{0:T(256)(128)(2,1)S(1)} %dynamic-slice.22, ...), channel_id=1, replica_groups=mesh['fsdp'=8,'dp'=4] {'dp'}, use_global_device_ids=true, to_apply=%region_41.42 | all-reduce | flops 384 | bytes 1536 | tf_op jit(solution)/shard_map/psum | solution.py:552
  927.9 86.7 %all-reduce.27.cloned.1.call-done = (bf16[4,64,512]{2,0,1:T(4,128)(2,1)}, bf16[4,64,512]{2,0,1:T(4,128)(2,1)}, bf16[4,64,512]{2,0,1:T(4,128)(2,1)}, bf16[64,2048...) async-done(((bf16[4,64,512]{2,0,1:T(4,128)(2,1)}, ...) | async-done | bytes 2359312 | tf_op jit(solution)/shard_map/psum | solution.py:553
  (794 shorter events, 243.3 us)
Async XLA Ops:
  7.2 19.0 %copy-start = (bf16[512,512]{1,0:T(8,128)(2,1)S(1)}, bf16[512,512]{1,0:T(8,128)(2,1)}, u32[]{:S(2)}) copy-start(bf16[512,512]{1,0:T(8,128)(2,1)} %param.29) | copy-start | bytes 1572868
  7.2 45.0 %copy-start.244 = (s32[127]{0:T(128)S(1)}, s32[127]{0:T(128)}, u32[]{:S(2)}) copy-start(s32[127]{0:T(128)} %constant.148.clone) | copy-start | bytes 1528
  7.2 63.0 %copy-start.224 = (s32[1023]{0:T(1024)S(1)}, s32[1023]{0:T(1024)}, u32[]{:S(2)}) copy-start(s32[1023]{0:T(1024)} %constant.147.clone) | copy-start | bytes 12280
  7.2 24.5 %copy-start.192 = (s32[2,512]{1,0:T(2,128)S(1)}, s32[2,512]{1,0:T(2,128)}, u32[]{:S(2)}) copy-start(s32[2,512]{1,0:T(2,128)} %param.20) | copy-start | bytes 12292
  7.2 25.8 %copy-start.247 = (bf16[32]{0:T(256)(128)(2,1)S(1)}, bf16[32]{0:T(256)(128)(2,1)}, u32[]{:S(2)}) copy-start(bf16[32]{0:T(256)(128)(2,1)} %param.26) | copy-start | bytes 196
  7.2 26.0 %copy-start.248 = (bf16[32]{0:T(256)(128)(2,1)S(1)}, bf16[32]{0:T(256)(128)(2,1)}, u32[]{:S(2)}) copy-start(bf16[32]{0:T(256)(128)(2,1)} %param.33) | copy-start | bytes 196
  7.3 45.1 %copy-start.243 = (bf16[2,64]{1,0:T(2,128)(2,1)S(1)}, bf16[2,64]{1,0:T(2,128)(2,1)}, u32[]{:S(2)}) copy-start(bf16[2,64]{1,0:T(2,128)(2,1)} %param.24) | copy-start | bytes 772
  7.3 54.6 %copy-start.238 = (bf16[3,64]{1,0:T(4,128)(2,1)S(1)}, bf16[3,64]{1,0:T(4,128)(2,1)}, u32[]{:S(2)}) copy-start(bf16[3,64]{1,0:T(4,128)(2,1)} %param.30) | copy-start | bytes 1156
  7.3 147.4 %all-gather.18.cloned.1.call-start = ((), (), s32[]{:S(2)}) async-start(), calls=%async_computation.11 | async-start | bytes 2359296 | tf_op jit(solution)/shard_map/all_gather | solution.py:483
  8.0 152.0 %all-gather.20.cloned.1.call-start = ((), (), s32[]{:S(2)}) async-start(), calls=%async_computation.12 | async-start | bytes 2359296 | tf_op jit(solution)/shard_map/all_gather | solution.py:484
  9.9 162.7 %all-gather.12.cloned.1.call-start = ((), (), s32[]{:S(2)}) async-start(), calls=%async_computation.8 | async-start | bytes 2359296 | tf_op jit(solution)/shard_map/all_gather | solution.py:474
  11.9 189.5 %all-gather.14.cloned.1.call-start = ((), (), s32[]{:S(2)}) async-start(), calls=%async_computation.9 | async-start | bytes 2359296 | tf_op jit(solution)/shard_map/all_gather | solution.py:476
  12.4 194.5 %all-gather.16.cloned.1.call-start = ((), (), s32[]{:S(2)}) async-start(), calls=%async_computation.10 | async-start | bytes 2359296 | tf_op jit(solution)/shard_map/all_gather | solution.py:477
  13.0 211.5 %all-gather.22.cloned.1.call-start = ((), (), s32[]{:S(2)}) async-start(), calls=%async_computation.13 | async-start | bytes 2359296 | tf_op jit(solution)/shard_map/all_gather | solution.py:486
  26.1 111.2 %copy-start.236 = (s32[512]{0:T(512)}, s32[512]{0:T(512)S(1)}, u32[]{:S(2)}) copy-start(s32[512]{0:T(512)S(1)} %get-tuple-element.243) | copy-start | bytes 6148
  26.2 111.2 %copy-start.197 = (s32[512]{0:T(512)}, s32[512]{0:T(512)S(1)}, u32[]{:S(2)}) copy-start(s32[512]{0:T(512)S(1)} %iota_add_fusion) | copy-start | bytes 6148
  27.5 111.2 %all-to-all-start = ((bf16[8,64,512]{2,1,0:T(8,128)(2,1)}), bf16[8,64,512]{2,1,0:T(8,128)(2,1)S(1)}, u32[]{:S(2)}, u32[]{:S(2)}) async-start(bf16[8,64,512]{2,1,0:T(8,128)(2,1)} %bitcast.32), calls=%async_computation | async-start | bytes 1048576 | tf_op jit(solution)/shard_map/all_to_all | solution.py:512
  31.0 197.4 %all-gather.24.cloned.1.call-start = ((), (), s32[]{:S(2)}) async-start(), calls=%async_computation.14 | async-start | bytes 2359296 | tf_op jit(solution)/shard_map/all_gather | solution.py:487
  52.3 24.5 %copy-start.188 = (pred[32,127]{1,0:T(8,128)(4,1)}, pred[32,127]{1,0:T(8,128)(4,1)S(1)}, u32[]{:S(2)}) copy-start(pred[32,127]{1,0:T(8,128)(4,1)S(1)} %iota_compare_fusion.2) | copy-start | bytes 12196
  70.2 86.8 %copy-start.190 = (f32[1,512]{1,0:T(1,128)}, f32[1,512]{1,0:T(1,128)S(1)}, u32[]{:S(2)}) copy-start(f32[1,512]{1,0:T(1,128)S(1)} %get-tuple-element.289) | copy-start | bytes 6148
  74.2 108.5 %copy-start.34 = (bf16[1,512,512]{1,2,0:T(8,128)(2,1)}, bf16[1,512,512]{1,2,0:T(8,128)(2,1)S(1)}, u32[]{:S(2)}) copy-start(bf16[1,512,512]{1,2,0:T(8,128)(2,1)S(1)} %copy.613) | copy-start | bytes 1572868
  75.2 117.7 %copy-start.21 = (bf16[1,512,512]{1,2,0:T(8,128)(2,1)}, bf16[1,512,512]{1,2,0:T(8,128)(2,1)S(1)}, u32[]{:S(2)}) copy-start(bf16[1,512,512]{1,2,0:T(8,128)(2,1)S(1)} %copy.617) | copy-start | bytes 1572868
  138.7 15.8 %all-to-all-start.1 = ((bf16[8,64,512]{2,1,0:T(8,128)(2,1)}), bf16[8,64,512]{2,1,0:T(8,128)(2,1)S(1)}, u32[]{:S(2)}, u32[]{:S(2)}) async-start(bf16[8,64,512]{2,1,0:T(8,128)(2,1)} %bitcast.58), calls=%async_computation.1 | async-start | bytes 1048576 | tf_op jit(solution)/shard_map/all_to_all | solution.py:512
  142.2 704.8 %reduce-scatter.13.cloned.1.call-start = ((), (), s32[]{:S(2)}) async-start(), calls=%async_computation.16 | async-start | bytes 4718592 | tf_op jit(solution)/shard_map/reduce_scatter | solution.py:541
  142.3 26.2 %copy-start.77 = (f32[64,512]{1,0:T(8,128)}, f32[64,512]{1,0:T(8,128)S(1)}, u32[]{:S(2)}) copy-start(f32[64,512]{1,0:T(8,128)S(1)} %convert_reduce_fusion.3) | copy-start | bytes 393220
  142.4 20.4 %copy-start.230 = (f32[64]{0:T(128)}, f32[64]{0:T(128)S(1)}, u32[]{:S(2)}) copy-start(f32[64]{0:T(128)S(1)} %add_rsqrt_fusion.9) | copy-start | bytes 772
  154.6 14.4 %copy-start.79 = (f32[64,512]{1,0:T(8,128)}, f32[64,512]{1,0:T(8,128)S(1)}, u32[]{:S(2)}) copy-start(f32[64,512]{1,0:T(8,128)S(1)} %convert_reduce_fusion.2) | copy-start | bytes 393220
  171.6 41.3 %copy-start.116 = (bf16[64,512]{0,1:T(8,128)(2,1)}, bf16[64,512]{0,1:T(8,128)(2,1)S(1)}, u32[]{:S(2)}) copy-start(bf16[64,512]{0,1:T(8,128)(2,1)S(1)} %copy.630) | copy-start | bytes 196612
  175.5 17.4 %copy-start.23 = (bf16[1,512,512]{2,1,0:T(8,128)(2,1)}, bf16[1,512,512]{2,1,0:T(8,128)(2,1)S(1)}, u32[]{:S(2)}) copy-start(bf16[1,512,512]{2,1,0:T(8,128)(2,1)S(1)} %copy.650) | copy-start | bytes 1572868
  184.0 12.8 %copy-start.99 = (bf16[1,512,512]{1,2,0:T(8,128)(2,1)}, bf16[1,512,512]{1,2,0:T(8,128)(2,1)S(1)}, u32[]{:S(2)}) copy-start(bf16[1,512,512]{1,2,0:T(8,128)(2,1)S(1)} %get-tuple-element.267) | copy-start | bytes 1572868
  193.5 13.5 %copy-start.7 = (f32[512,512]{0,1:T(8,128)}, f32[512,512]{0,1:T(8,128)S(1)}, u32[]{:S(2)}) copy-start(f32[512,512]{0,1:T(8,128)S(1)} %get-tuple-element.309) | copy-start | bytes 3145732
  201.4 14.5 %copy-start.19 = (f32[512,512]{0,1:T(8,128)}, f32[512,512]{0,1:T(8,128)S(1)}, u32[]{:S(2)}) copy-start(f32[512,512]{0,1:T(8,128)S(1)} %get-tuple-element.313) | copy-start | bytes 3145732
  253.6 11.0 %copy-start.82 = (bf16[1,1,512,512]{3,2,0,1:T(8,128)(2,1)}, bf16[1,1,512,512]{3,2,0,1:T(8,128)(2,1)S(1)}, u32[]{:S(2)}) copy-start(bf16[1,1,512,512]{3,2,0,1:T(8,128)(2,1)S(1)} %copy.480) | copy-start | bytes 1572868
  271.5 577.3 %reduce-scatter.11.cloned.1.call-start = ((), (), s32[]{:S(2)}) async-start(), calls=%async_computation.15 | async-start | bytes 4718592 | tf_op jit(solution)/shard_map/reduce_scatter | solution.py:540
  273.3 12.8 %copy-start.132 = (f32[64,512]{1,0:T(8,128)}, f32[64,512]{1,0:T(8,128)S(1)}, u32[]{:S(2)}) copy-start(f32[64,512]{1,0:T(8,128)S(1)} %get-tuple-element.295) | copy-start | bytes 393220
  273.4 47.2 %copy-start.103 = (f32[64,512]{1,0:T(8,128)}, f32[64,512]{1,0:T(8,128)S(1)}, u32[]{:S(2)}) copy-start(f32[64,512]{1,0:T(8,128)S(1)} %multiply_add_fusion.3) | copy-start | bytes 393220
  298.9 15.9 %copy-start.123 = (bf16[1,64,512]{1,2,0:T(8,128)(2,1)S(1)}, bf16[1,64,512]{1,2,0:T(8,128)(2,1)}, u32[]{:S(2)}) copy-start(bf16[1,64,512]{1,2,0:T(8,128)(2,1)} %copy-done.122) | copy-start | bytes 196612
  298.9 23.9 %copy-start.107 = (f32[64,512]{1,0:T(8,128)S(1)}, f32[64,512]{1,0:T(8,128)}, u32[]{:S(2)}) copy-start(f32[64,512]{1,0:T(8,128)} %copy-done.105) | copy-start | bytes 393220
  299.0 26.1 %copy-start.110 = (f32[64,512]{1,0:T(8,128)S(1)}, f32[64,512]{1,0:T(8,128)}, u32[]{:S(2)}) copy-start(f32[64,512]{1,0:T(8,128)} %get-tuple-element.286) | copy-start | bytes 393220
  299.0 551.6 %reduce-scatter.17.cloned.1.call-start = ((), (), s32[]{:S(2)}) async-start(), calls=%async_computation.18 | async-start | bytes 4718592 | tf_op jit(solution)/shard_map/reduce_scatter | solution.py:547
  302.3 26.0 %copy-start.121 = (bf16[8,64,64]{2,1,0:T(8,128)(2,1)S(1)}, bf16[8,64,64]{2,1,0:T(8,128)(2,1)}, u32[]{:S(2)}) copy-start(bf16[8,64,64]{2,1,0:T(8,128)(2,1)} %copy-done.120) | copy-start | bytes 196612
  304.7 21.7 %copy-start.131 = (bf16[8,64,64]{2,1,0:T(8,128)(2,1)S(1)}, bf16[8,64,64]{2,1,0:T(8,128)(2,1)}, u32[]{:S(2)}) copy-start(bf16[8,64,64]{2,1,0:T(8,128)(2,1)} %convolution_convert_fusion.17) | copy-start | bytes 196612
  310.6 14.4 %copy-start.151 = (bf16[8,64,64]{2,1,0:T(8,128)(2,1)S(1)}, bf16[8,64,64]{2,1,0:T(8,128)(2,1)}, u32[]{:S(2)}) copy-start(bf16[8,64,64]{2,1,0:T(8,128)(2,1)} %copy-done.150) | copy-start | bytes 196612
  317.3 12.9 %copy-start.112 = (bf16[512,2048]{1,0:T(8,128)(2,1)S(1)}, bf16[512,2048]{1,0:T(8,128)(2,1)}, u32[]{:S(2)}) copy-start(bf16[512,2048]{1,0:T(8,128)(2,1)} %copy-done.111) | copy-start | bytes 6291460
  336.4 15.4 %copy-start.172 = (f32[8,512]{1,0:T(8,128)}, f32[8,512]{1,0:T(8,128)S(1)}, u32[]{:S(2)}) copy-start(f32[8,512]{1,0:T(8,128)S(1)} %log_add_fusion) | copy-start | bytes 49156
  356.7 495.7 %reduce-scatter.15.cloned.1.call-start = ((), (), s32[]{:S(2)}) async-start(), calls=%async_computation.17 | async-start | bytes 4718592 | tf_op jit(solution)/shard_map/reduce_scatter | solution.py:546
  439.6 15.7 %copy-start.100 = (bf16[1,512,512]{1,2,0:T(8,128)(2,1)S(1)}, bf16[1,512,512]{1,2,0:T(8,128)(2,1)}, u32[]{:S(2)}) copy-start(bf16[1,512,512]{1,2,0:T(8,128)(2,1)} %copy-done.99) | copy-start | bytes 1572868
  439.6 15.7 %copy-start.171 = (f32[8,512]{1,0:T(8,128)S(1)}, f32[8,512]{1,0:T(8,128)}, u32[]{:S(2)}) copy-start(f32[8,512]{1,0:T(8,128)} %copy-done.170) | copy-start | bytes 49156
  492.1 383.4 %reduce-scatter.19.cloned.1.call-start = ((), (), s32[]{:S(2)}) async-start(), calls=%async_computation.19 | async-start | bytes 294912
  562.6 25.0 %copy-start.225 = (f32[256]{0:T(256)S(1)}, f32[256]{0:T(256)}, u32[]{:S(2)}) copy-start(f32[256]{0:T(256)} %add.462) | copy-start | bytes 3076
  587.6 253.5 %copy-start.198 = (s32[512]{0:T(512)S(1)}, s32[512]{0:T(512)}, u32[]{:S(2)}) copy-start(s32[512]{0:T(512)} %copy-done.197) | copy-start | bytes 6148
  587.6 253.5 %copy-start.229 = (s32[512]{0:T(512)S(1)}, s32[512]{0:T(512)}, u32[]{:S(2)}) copy-start(s32[512]{0:T(512)} %copy-done.228) | copy-start | bytes 6148
  587.6 254.1 %copy-start.210 = (f32[512]{0:T(512)S(1)}, f32[512]{0:T(512)}, u32[]{:S(2)}) copy-start(f32[512]{0:T(512)} %get-tuple-element.226) | copy-start | bytes 6148
  587.6 254.1 %copy-start.211 = (f32[512]{0:T(512)S(1)}, f32[512]{0:T(512)}, u32[]{:S(2)}) copy-start(f32[512]{0:T(512)} %get-tuple-element.232) | copy-start | bytes 6148
  587.6 254.1 %copy-start.218 = (f32[512]{0:T(512)S(1)}, f32[512]{0:T(512)}, u32[]{:S(2)}) copy-start(f32[512]{0:T(512)} %get-tuple-element.234) | copy-start | bytes 6148
  587.6 254.1 %copy-start.219 = (f32[512]{0:T(512)S(1)}, f32[512]{0:T(512)}, u32[]{:S(2)}) copy-start(f32[512]{0:T(512)} %get-tuple-element.299) | copy-start | bytes 6148
  587.6 254.1 %copy-start.233 = (f32[512]{0:T(512)S(1)}, f32[512]{0:T(512)}, u32[]{:S(2)}) copy-start(f32[512]{0:T(512)} %get-tuple-element.230) | copy-start | bytes 6148
  587.6 255.1 %copy-start.237 = (s32[512]{0:T(512)S(1)}, s32[512]{0:T(512)}, u32[]{:S(2)}) copy-start(s32[512]{0:T(512)} %copy-done.236) | copy-start | bytes 6148
  841.7 71.4 %reduce-scatter.21.cloned.1.call-start = ((), (), s32[]{:S(2)}) async-start(), calls=%async_computation.20 | async-start | bytes 294912
  842.7 12.2 %copy-start.93 = (bf16[512,512]{0,1:T(8,128)(2,1)S(1)}, bf16[512,512]{0,1:T(8,128)(2,1)}, u32[]{:S(2)}) copy-start(bf16[512,512]{0,1:T(8,128)(2,1)} %copy-done.91) | copy-start | bytes 1572868
  842.7 171.9 %all-reduce.27.cloned.1.call-start = ((), (), s32[]{:S(2)}) async-start(), calls=%async_computation.21 | async-start | bytes 4718592 | tf_op jit(solution)/shard_map/psum | solution.py:553
  871.3 156.2 %copy-start.1 = (bf16[512,512]{1,0:T(8,128)(2,1)S(1)}, bf16[512,512]{1,0:T(8,128)(2,1)}, u32[]{:S(2)}) copy-start(bf16[512,512]{1,0:T(8,128)(2,1)} %param.29) | copy-start | bytes 1572868
  1014.6 10.9 %copy-start.163 = (bf16[256,512]{1,0:T(8,128)(2,1)S(1)}, bf16[256,512]{1,0:T(8,128)(2,1)}, u32[]{:S(2)}) copy-start(bf16[256,512]{1,0:T(8,128)(2,1)} %get-tuple-element.262) | copy-start | bytes 786436
  1014.6 11.7 %copy-start.147 = (bf16[512,512]{1,0:T(8,128)(2,1)S(1)}, bf16[512,512]{1,0:T(8,128)(2,1)}, u32[]{:S(2)}) copy-start(bf16[512,512]{1,0:T(8,128)(2,1)} %get-tuple-element.260) | copy-start | bytes 1572868
  (201 other events, 790.2 us)
Sparse Core Ops, SparseCore 0:
  10.0 36.0 all-gather.17
  48.6 28.1 all-gather.19
  79.2 27.8 all-gather.11
  108.9 27.8 all-gather.13
  138.5 30.3 all-gather.15
  170.6 27.9 all-gather.21
  200.5 27.8 all-gather.23
  271.6 51.3 reduce-scatter.12
  326.7 51.3 reduce-scatter.10
  381.3 51.2 reduce-scatter.16
  492.2 51.3 reduce-scatter.14
  841.8 33.6 reduce-scatter.18
  879.4 33.6 reduce-scatter.20
  916.4 98.1 all-reduce.26
where the time goes:
time: 1040 us; the launch traced here: 1030 us
  blocking collectives  326 us (31%)
  local copies, waits for them, and re-layouts  273 us (26%)
  matrix products  190 us (18%)
  waiting for transfers between devices  143 us (14%)
  other arithmetic  74.6 us (7%)
  between operations  20.1 us (2%)
    unnamed x3, blocking collectives  278 us
    unnamed x534, local copies, waits for them, and re-layouts  124 us
    psum x1, waiting for transfers between devices, on_device(): lax.psum(totals[1].astype(jnp.bfloat16), 'dp').astype(jnp.float32)  86.7 us
    unnamed x16, waiting for transfers between devices  42.9 us
    reshape x4, local copies, waits for them, and re-layouts, diagonal_sums(): jnp.pad(score_sum, ((0, 0), (0, 0), (length - 1, 0)))  35 us
    dot_general x18, matrix products, weight_grad(): lax.dot_general(activation, gradient, (((0,), (0,)), ((), ())), preferred...  34.5 us
    dot_general x16, matrix products, input_grad(): lax.dot_general(gradient, matrix, (((1,), (1,)), ((), ())), preferred_ele...  28 us
    dot_general x18, matrix products, forward_dot(): return jnp.dot(left_side, right_side, preferred_element_type=jnp.float32)  25.3 us
  transfers between devices with their start and end apart: 16, of which 5 were waited for; matrix products, arithmetic and copies ran while one was open for 45% of the time, Pallas kernels for 0%

commit v1 on v0

v1 whole, which is shorter than its diff:
```python
import functools

import jax
import jax.numpy as jnp
import numpy as np
from jax import lax
from jax.experimental import pallas as pl
from jax.experimental.pallas import tpu as pltpu
from jax.sharding import PartitionSpec as P

HEADS = 8
HEAD_DIM = 64
BUCKETS = 32
SERIES_MOST = 256
TILE = 128
MASKED = -1000000000.0

epsilon = 1e-06
f32 = jnp.float32
bf16 = jnp.bfloat16
PARAMS = pltpu.CompilerParams(vmem_limit_bytes=56 * 2**20)


def bucket_codes(length, both_ways):
    bucket_list = []
    for offset in range(-(length - 1), length):
        if both_ways:
            upper_half = 16 if offset > 0 else 0
            distance = abs(offset)
            if distance < 8:
                bucket = distance
            else:
                bucket = 8 + sum(
                    (1 for exponent in range(1, 8) if distance * distance >= 64 * 2**exponent)
                )
        else:
            upper_half = 0
            distance = max(-offset, 0)
            if distance < 16:
                bucket = distance
            else:
                bucket = 16 + sum(
                    (1 for exponent in range(1, 16) if distance**16 >= 16**16 * 2 ** (3 * exponent))
                )
        bucket_list.append(upper_half + bucket)
    return np.array(bucket_list, dtype=np.int32)


def offset_hot(length, both_ways, reverse):
    codes = np.concatenate([bucket_codes(length, both_ways), [-1]])
    if reverse:
        codes = codes[::-1]
    return jnp.asarray(codes[None, :] == np.arange(BUCKETS)[:, None], bf16)


def nn(a, b):
    return lax.dot_general(a, b, (((1,), (0,)), ((), ())), preferred_element_type=f32)


def nt(a, b):
    return lax.dot_general(a, b, (((1,), (1,)), ((), ())), preferred_element_type=f32)


def tn(a, b):
    return lax.dot_general(a, b, (((0,), (0,)), ((), ())), preferred_element_type=f32)


def rho_of(h):
    return lax.rsqrt(jnp.mean(h * h, axis=-1, keepdims=True) + epsilon)


def normed(h, gain):
    return (h * rho_of(h) * gain.astype(f32)).astype(bf16)


def norm_back(h, gain, dn):
    rho = rho_of(h)
    xh = h * rho
    gu = dn * gain.astype(f32)
    dh = rho * (gu - xh * jnp.mean(gu * xh, axis=-1, keepdims=True))
    return dh, jnp.sum(dn * xh, axis=0, keepdims=True)


def gelu(u):
    t = jnp.tanh(np.float32(np.sqrt(2 / np.pi)) * (u + 0.044715 * (u * u * u)))
    return 0.5 * u * (1.0 + t)


def gelu_both(u):
    c = np.float32(np.sqrt(2 / np.pi))
    u2 = u * u
    t = jnp.tanh(c * (u + 0.044715 * (u2 * u)))
    cdf = 0.5 * (1.0 + t)
    return u * cdf, cdf + 0.5 * u * (1.0 - t * t) * (c + (3 * 0.044715 * c) * u2)


def matrix(ref, w):
    part = ref[:, w]
    return part.reshape(part.shape[0] * part.shape[1], part.shape[2])


def packed(value, shards):
    return value.reshape(shards, value.shape[0] // shards, value.shape[1]).astype(bf16)


def half(lane, value, which):
    return jnp.where((lane // HEAD_DIM) == which, value, jnp.zeros_like(value))


def fill_strip(strip_ref, table, hot, shift):
    vec = nn(table, hot)
    width = hot.shape[1]
    rows = strip_ref.shape[1]
    for h in range(HEADS):
        row = jnp.broadcast_to(vec[h : h + 1], (rows, width))
        strip_ref[h] = pltpu.roll(row, (width + shift) % width, 1, stride=1, stride_axis=0)


def strip_sums(acc, hot):
    rows, width = acc.shape[1], acc.shape[2]
    total = jnp.zeros((HEADS, 8, width), f32)
    for g in range(rows // 8):
        part = acc[:, g * 8 : g * 8 + 8, :].reshape(HEADS * 8, width)
        if g:
            part = pltpu.roll(part, width - 8 * g, 1)
        total = total + part.reshape(HEADS, 8, width)
    flat = total.reshape(HEADS * 8, width)
    sub = lax.broadcasted_iota(jnp.int32, flat.shape, 0) % 8
    for b in range(3):
        flat = jnp.where((sub >> b) & 1 == 1, pltpu.roll(flat, width - (1 << b), 1), flat)
    diag = pltpu.roll(jnp.sum(flat.reshape(HEADS, 8, width), axis=1), rows, 1)
    return lax.dot_general(
        diag,
        hot.astype(f32),
        (((1,), (1,)), ((), ())),
        precision=lax.Precision.HIGHEST,
        preferred_element_type=f32,
    )


def soft_rows(s):
    e = jnp.exp(s - jnp.max(s, axis=-1, keepdims=True))
    return e * (1.0 / jnp.sum(e, axis=-1, keepdims=True))


def soft_columns(s):
    e = jnp.exp(s - jnp.max(s, axis=0, keepdims=True))
    return e * (1.0 / jnp.sum(e, axis=0, keepdims=True))


def enc_attn_fwd_kernel(
    x_ref, segc_ref, segr_ref, g_ref, w_ref, table_ref, hot_ref, hid_ref, q_ref, k_ref, v_ref, mix_ref, strip_ref
):
    length = x_ref.shape[1]
    blocks = length // TILE

    @pl.when(pl.program_id(0) == 0)
    def _():
        fill_strip(strip_ref, table_ref[...], hot_ref[...], 1 - TILE)

    x = x_ref[0].astype(f32)
    n = normed(x, g_ref[...])
    q_ref[0] = nn(n, matrix(w_ref, 0)).astype(bf16)
    k_ref[0] = nn(n, matrix(w_ref, 1)).astype(bf16)
    v_ref[0] = nn(n, matrix(w_ref, 2)).astype(bf16)
    lane = lax.broadcasted_iota(jnp.int32, (length, 2 * HEAD_DIM), 1)
    same = segc_ref[0] == segr_ref[0]
    for hp in range(HEADS // 2):
        ls = slice(hp * 2 * HEAD_DIM, (hp + 1) * 2 * HEAD_DIM)
        qp, kp, vp = q_ref[0, :, ls], k_ref[0, :, ls], v_ref[0, :, ls]
        outs = []
        for sub in range(2):
            s = nt(half(lane, qp, sub), kp)
            starts = [(blocks - 1 - b) * TILE for b in range(blocks)]
            bias = [strip_ref[hp * 2 + sub, :, c : c + length] for c in starts]
            s = jnp.where(same, s + jnp.concatenate(bias, axis=0), MASKED)
            outs.append(nn(soft_rows(s).astype(bf16), vp))
        mix_ref[0, :, ls] = jnp.where(lane < HEAD_DIM, outs[0], outs[1]).astype(bf16)
    hid_ref[0] = x + nn(mix_ref[0], matrix(w_ref, 3))


def enc_attn_fwd(x, segments, gain, weights, table):
    rows, length, width = x.shape
    hot = offset_hot(length, True, False)
    row = lambda r: (r, 0, 0)
    full = lambda r: (0, 0)
    sds = jax.ShapeDtypeStruct
    return pl.pallas_call(
        enc_attn_fwd_kernel,
        grid=(rows,),
        in_specs=[
            pl.BlockSpec((1, length, width), row),
            pl.BlockSpec((1, length, 1), row),
            pl.BlockSpec((1, 1, length), row),
            pl.BlockSpec((1, width), full),
            pl.BlockSpec(weights.shape, lambda r: (0, 0, 0, 0)),
            pl.BlockSpec(table.shape, full),
            pl.BlockSpec(hot.shape, full),
        ],
        out_specs=[pl.BlockSpec((1, length, width), row)] * 5,
        out_shape=[sds(x.shape, f32)] + [sds(x.shape, bf16)] * 4,
        scratch_shapes=[pltpu.VMEM((HEADS, TILE, 2 * length), f32)],
        compiler_params=PARAMS,
        name="enc_attn_fwd",
    )(x, segments[:, :, None], segments[:, None, :], gain, weights, table, hot)


def ffn_fwd_kernel(h_ref, g_ref, w_ref, o_ref, *, cols):
    h = h_ref[...]
    n = normed(h, g_ref[...])
    out = h
    per = w_ref.shape[0] // cols
    for b in range(cols):
        a = gelu(nn(n, matrix(w_ref, b))).astype(bf16)
        down = w_ref[b * per : (b + 1) * per, cols:]
        out = out + nn(a, down.reshape(-1, down.shape[-1]))
    o_ref[...] = out.astype(bf16)


def ffn_fwd(h, gain, weights, tokens=512):
    total, width = h.shape
    return pl.pallas_call(
        functools.partial(ffn_fwd_kernel, cols=weights.shape[1] // 2),
        grid=(total // tokens,),
        in_specs=[
            pl.BlockSpec((tokens, width), lambda t: (t, 0)),
            pl.BlockSpec((1, width), lambda t: (0, 0)),
            pl.BlockSpec(weights.shape, lambda t: (0, 0, 0, 0)),
        ],
        out_specs=pl.BlockSpec((tokens, width), lambda t: (t, 0)),
        out_shape=jax.ShapeDtypeStruct((total, width), bf16),
        compiler_params=PARAMS,
        name="enc_ffn_fwd",
    )(h, gain, weights)


def ffn_step(n, gb, wu_ref, wd_ref, dwu_ref, dwd_ref):
    wu = matrix(wu_ref, 0)
    wd = wd_ref[...].reshape(-1, wd_ref.shape[-1])
    a, slope = gelu_both(nn(n, wu))
    a = a.astype(bf16)
    dwd_ref[...] = tn(a, gb).astype(bf16).reshape(dwd_ref.shape)
    du = (slope * nt(gb, wd)).astype(bf16)
    dwu_ref[:, 0] = packed(tn(n, du), dwu_ref.shape[0])
    return a, wd, nt(du, wu)


def enc_ffn_bwd_kernel(
    h_ref, g_ref, wu_ref, wd_ref, cot_ref, gm_ref, gmem_ref, gh_ref, dwu_ref, dwd_ref, dg_ref, n_s, gb_s, dn_s
):
    i = pl.program_id(0)
    rows, length, width = cot_ref.shape
    late = gm_ref.shape[1]

    @pl.when(i == 0)
    def _():
        n_s[...] = normed(h_ref[...], g_ref[...])
        for r in range(rows):
            gmem_ref[r, : length - late] = cot_ref[r, : length - late].astype(f32)
            gmem_ref[r, length - late :] = cot_ref[r, length - late :].astype(f32) + gm_ref[r]
            gb_s[r * length : (r + 1) * length] = gmem_ref[r].astype(bf16)
        dn_s[...] = jnp.zeros_like(dn_s)

    _, _, dn = ffn_step(n_s[...], gb_s[...], wu_ref, wd_ref, dwu_ref, dwd_ref)
    dn_s[...] += dn

    @pl.when(i == pl.num_programs(0) - 1)
    def _():
        dh, dg = norm_back(h_ref[...], g_ref[...], dn_s[...])
        dg_ref[...] = dg
        gh_ref[...] = gmem_ref[...].reshape(rows * length, width) + dh


def ffn_specs(weights):
    shards, both, blk, width = weights.shape
    cols = both // 2
    up = pl.BlockSpec((shards, 1, blk, width), lambda i: (0, i, 0, 0))
    down_in = pl.BlockSpec((shards // cols, cols, blk, width), lambda i: (i, 1, 0, 0))
    down_out = pl.BlockSpec((shards // cols, cols, blk, width), lambda i: (i, 0, 0, 0))
    grads = jax.ShapeDtypeStruct((shards, cols, blk, width), bf16)
    return cols, up, down_in, down_out, grads


def enc_ffn_bwd(h, gain, weights, cot, late_grad):
    rows, length, width = cot.shape
    tokens = rows * length
    cols, up, down_in, down_out, grads = ffn_specs(weights)
    full = lambda i: (0, 0)
    full3 = lambda i: (0, 0, 0)
    sds = jax.ShapeDtypeStruct
    return pl.pallas_call(
        enc_ffn_bwd_kernel,
        grid=(cols,),
        in_specs=[
            pl.BlockSpec((tokens, width), full),
            pl.BlockSpec((1, width), full),
            up,
            down_in,
            pl.BlockSpec(cot.shape, full3),
            pl.BlockSpec(late_grad.shape, full3),
        ],
        out_specs=[
            pl.BlockSpec(cot.shape, full3),
            pl.BlockSpec((tokens, width), full),
            up,
            down_out,
            pl.BlockSpec((1, width), full),
        ],
        out_shape=[sds(cot.shape, f32), sds((tokens, width), f32), grads, grads, sds((1, width), f32)],
        scratch_shapes=[
            pltpu.VMEM((tokens, width), bf16),
            pltpu.VMEM((tokens, width), bf16),
            pltpu.VMEM((tokens, width), f32),
        ],
        compiler_params=PARAMS,
        name="enc_ffn_bwd",
    )(h, gain, weights, weights, cot, late_grad)


def enc_attn_bwd_kernel(
    gh_ref, q_ref, k_ref, v_ref, segc_ref, segr_ref, w_ref, table_ref, hot_ref,
    dq_ref, dk_ref, dv_ref, dt_ref, strip_ref, acc_ref, do_s,
):
    r = pl.program_id(0)
    length = q_ref.shape[1]
    blocks = length // TILE

    @pl.when(r == 0)
    def _():
        fill_strip(strip_ref, table_ref[...], hot_ref[...], -TILE)
        acc_ref[...] = jnp.zeros_like(acc_ref)

    do_s[...] = nt(gh_ref[0].astype(bf16), matrix(w_ref, 0)).astype(bf16)
    lane = lax.broadcasted_iota(jnp.int32, (length, 2 * HEAD_DIM), 1)
    same = segc_ref[0] == segr_ref[0]
    for hp in range(HEADS // 2):
        ls = slice(hp * 2 * HEAD_DIM, (hp + 1) * 2 * HEAD_DIM)
        qp, kp, vp, dop = q_ref[0, :, ls], k_ref[0, :, ls], v_ref[0, :, ls], do_s[:, ls]
        dq = dk = dv = None
        for sub in range(2):
            h = hp * 2 + sub
            qm, km, dom = half(lane, qp, sub), half(lane, kp, sub), half(lane, dop, sub)
            s = nt(kp, qm)
            starts = [(blocks - 1 - b) * TILE for b in range(blocks)]
            bias = [strip_ref[h, :, c : c + length] for c in starts]
            p = soft_columns(jnp.where(same, s + jnp.concatenate(bias, axis=0), MASKED))
            dp = nt(vp, dom)
            ds = (p * (dp - jnp.sum(dp * p, axis=0, keepdims=True))).astype(bf16)
            new = (tn(ds, km), nn(ds, qm), nn(p.astype(bf16), dom))
            dq, dk, dv = new if dq is None else (dq + new[0], dk + new[1], dv + new[2])
            wide = ds.astype(f32)
            for b, c in enumerate(starts):
                acc_ref[h, :, c : c + length] += wide[b * TILE : (b + 1) * TILE]
        dq_ref[0, :, ls] = dq.astype(bf16)
        dk_ref[0, :, ls] = dk.astype(bf16)
        dv_ref[0, :, ls] = dv.astype(bf16)

    @pl.when(r == pl.num_programs(0) - 1)
    def _():
        dt_ref[...] = strip_sums(acc_ref[...], hot_ref[...])


def enc_attn_bwd(grad_hidden, q, k, v, segments, weights, table):
    rows, length, width = q.shape
    shards, _, blk, _ = weights.shape
    hot = offset_hot(length, True, True)
    row = lambda r: (r, 0, 0)
    full = lambda r: (0, 0)
    sds = jax.ShapeDtypeStruct
    strip = pltpu.VMEM((HEADS, TILE, 2 * length), f32)
    return pl.pallas_call(
        enc_attn_bwd_kernel,
        grid=(rows,),
        in_specs=[pl.BlockSpec((1, length, width), row)] * 4
        + [
            pl.BlockSpec((1, length, 1), row),
            pl.BlockSpec((1, 1, length), row),
            pl.BlockSpec((shards, 1, blk, width), lambda r: (0, 3, 0, 0)),
            pl.BlockSpec(table.shape, full),
            pl.BlockSpec(hot.shape, full),
        ],
        out_specs=[pl.BlockSpec((1, length, width), row)] * 3 + [pl.BlockSpec(table.shape, full)],
        out_shape=[sds(q.shape, bf16)] * 3 + [sds(table.shape, f32)],
        scratch_shapes=[strip, strip, pltpu.VMEM((length, width), bf16)],
        compiler_params=PARAMS,
        name="enc_attn_bwd",
    )(grad_hidden, q, k, v, segments[:, :, None], segments[:, None, :], weights, table, hot)


def enc_weight_grads_kernel(x_ref, g_ref, dq_ref, dk_ref, dv_ref, mix_ref, gh_ref, dw_ref):
    shards = dw_ref.shape[0]
    n = normed(x_ref[...].astype(f32), g_ref[...])
    for w, d_ref in enumerate((dq_ref, dk_ref, dv_ref)):
        dw_ref[:, w] = packed(tn(n, d_ref[...]), shards)
    dw_ref[:, 3] = packed(tn(mix_ref[...], gh_ref[...].astype(bf16)), shards)


def enc_weight_grads(x, gain, dq, dk, dv, mix, grad_hidden, shape):
    return pl.pallas_call(
        enc_weight_grads_kernel,
        out_shape=jax.ShapeDtypeStruct(shape, bf16),
        compiler_params=PARAMS,
        name="enc_weight_grads",
    )(x, gain, dq, dk, dv, mix, grad_hidden)


def enc_input_grad_kernel(x_ref, g_ref, dq_ref, dk_ref, dv_ref, gh_ref, w_ref, gi_ref, dg_ref):
    dn = nt(dq_ref[...], matrix(w_ref, 0)) + nt(dk_ref[...], matrix(w_ref, 1)) + nt(dv_ref[...], matrix(w_ref, 2))
    dh, dg = norm_back(x_ref[...].astype(f32), g_ref[...], dn)
    gi_ref[...] = gh_ref[...] + dh

    @pl.when(pl.program_id(0) == 0)
    def _():
        dg_ref[...] = jnp.zeros_like(dg_ref)

    dg_ref[...] += dg


def enc_input_grad(x, gain, dq, dk, dv, grad_hidden, weights, tokens=512):
    total, width = x.shape
    tile = pl.BlockSpec((tokens, width), lambda t: (t, 0))
    full = pl.BlockSpec((1, width), lambda t: (0, 0))
    sds = jax.ShapeDtypeStruct
    return pl.pallas_call(
        enc_input_grad_kernel,
        grid=(total // tokens,),
        in_specs=[tile, full, tile, tile, tile, tile, pl.BlockSpec(weights.shape, lambda t: (0, 0, 0, 0))],
        out_specs=[tile, full],
        out_shape=[sds((total, width), f32), sds((1, width), f32)],
        compiler_params=PARAMS,
        name="enc_input_grad",
    )(x, gain, dq, dk, dv, grad_hidden, weights)


def dec_masks(rows, steps, late, last_ref, key_major):
    tokens, keys = rows * steps, rows * late
    shape = (tokens, tokens)
    i = lax.broadcasted_iota(jnp.int32, shape, 1 if key_major else 0)
    j = lax.broadcasted_iota(jnp.int32, shape, 0 if key_major else 1)
    causal = (i // steps == j // steps) & (j <= i)
    shape = (keys, tokens) if key_major else (tokens, keys)
    i = lax.broadcasted_iota(jnp.int32, shape, 1 if key_major else 0)
    j = lax.broadcasted_iota(jnp.int32, shape, 0 if key_major else 1)
    return causal, (i // steps == j // late) & (last_ref[...] == 1)


def dec_attn_fwd_kernel(
    emb_ref, enc_ref, last_ref, g_ref, w_ref, table_ref, hot_ref,
    na_ref, qkv_ref, mixa_ref, hida_ref, nb_ref, cq_ref, ckv_ref, mixb_ref, hidb_ref, strip_ref, *, rows,
):
    tokens = emb_ref.shape[0]
    keys = enc_ref.shape[0]
    causal, allowed = dec_masks(rows, tokens // rows, keys // rows, last_ref, False)
    fill_strip(strip_ref, table_ref[...], hot_ref[...], 1 - tokens)
    lane = lax.broadcasted_iota(jnp.int32, (tokens, 2 * HEAD_DIM), 1)

    def attend(q_at, k_at, v_at, bias_at, mask, mix_ref):
        for hp in range(HEADS // 2):
            ls = slice(hp * 2 * HEAD_DIM, (hp + 1) * 2 * HEAD_DIM)
            qp, kp, vp = q_at(ls), k_at(ls), v_at(ls)
            outs = []
            for sub in range(2):
                s = nt(half(lane, qp, sub), kp)
                if bias_at is not None:
                    s = s + bias_at(hp * 2 + sub)
                outs.append(nn(soft_rows(jnp.where(mask, s, MASKED)).astype(bf16), vp))
            mix_ref[:, ls] = jnp.where(lane < HEAD_DIM, outs[0], outs[1]).astype(bf16)

    emb = emb_ref[...].astype(f32)
    na_ref[...] = normed(emb, g_ref[0:1])
    for w in range(3):
        qkv_ref[w] = nn(na_ref[...], matrix(w_ref, w)).astype(bf16)
    attend(
        lambda ls: qkv_ref[0, :, ls],
        lambda ls: qkv_ref[1, :, ls],
        lambda ls: qkv_ref[2, :, ls],
        lambda h: strip_ref[h, :, :tokens],
        causal,
        mixa_ref,
    )
    hida_ref[...] = emb + nn(mixa_ref[...], matrix(w_ref, 3))
    nb_ref[...] = normed(hida_ref[...], g_ref[1:2])
    cq_ref[...] = nn(nb_ref[...], matrix(w_ref, 4)).astype(bf16)
    for w in range(2):
        ckv_ref[w] = nn(enc_ref[...], matrix(w_ref, 5 + w)).astype(bf16)
    attend(
        lambda ls: cq_ref[:, ls],
        lambda ls: ckv_ref[0, :, ls],
        lambda ls: ckv_ref[1, :, ls],
        None,
        allowed,
        mixb_ref,
    )
    hidb_ref[...] = hida_ref[...] + nn(mixb_ref[...], matrix(w_ref, 7))


def whole_spec(a):
    zeros = (0,) * len(a.shape)
    return pl.BlockSpec(a.shape, lambda i: zeros)


def dec_attn_fwd(emb, enc_late, last, gains, weights, table, rows):
    tokens, width = emb.shape
    keys = enc_late.shape[0]
    shards, _, blk, _ = weights.shape
    hot = dec_hot(tokens, tokens // rows, False)
    sds = jax.ShapeDtypeStruct
    one = sds((tokens, width), bf16)
    wide = sds((tokens, width), f32)
    outs = [one, sds((3, tokens, width), bf16), one, wide, one, one, sds((2, keys, width), bf16), one, wide]
    args = (emb, enc_late, last, gains, weights, table, hot)
    specs = [whole_spec(a) for a in args]
    specs[4] = pl.BlockSpec((shards, 8, blk, width), lambda i: (0, 0, 0, 0))
    return pl.pallas_call(
        functools.partial(dec_attn_fwd_kernel, rows=rows),
        grid=(1,),
        in_specs=specs,
        out_specs=[whole_spec(o) for o in outs],
        out_shape=outs,
        scratch_shapes=[pltpu.VMEM((HEADS, tokens, 2 * tokens), f32)],
        compiler_params=PARAMS,
        name="dec_attn_fwd",
    )(*args)


def dec_hot(tokens, steps, reverse):
    codes = np.full(2 * tokens, -1, np.int32)
    own = bucket_codes(steps, False)
    codes[tokens - steps : tokens - steps + len(own)] = own
    if reverse:
        codes = codes[::-1]
    return jnp.asarray(codes[None, :] == np.arange(BUCKETS)[:, None], bf16)


def dec_ffn_kernel(
    h_ref, g_ref, wu_ref, wd_ref, cot_ref, out_ref, gh_ref, dwu_ref, dwd_ref, dg_ref, n_s, gb_s, dn_s, o_s
):
    i = pl.program_id(0)

    @pl.when(i == 0)
    def _():
        n_s[...] = normed(h_ref[...], g_ref[...])
        gb_s[...] = cot_ref[...]
        dn_s[...] = jnp.zeros_like(dn_s)
        o_s[...] = h_ref[...]

    a, wd, dn = ffn_step(n_s[...], gb_s[...], wu_ref, wd_ref, dwu_ref, dwd_ref)
    o_s[...] += nn(a, wd)
    dn_s[...] += dn

    @pl.when(i == pl.num_programs(0) - 1)
    def _():
        out_ref[...] = o_s[...].astype(bf16)
        dh, dg = norm_back(h_ref[...], g_ref[...], dn_s[...])
        dg_ref[...] = dg
        gh_ref[...] = cot_ref[...].astype(f32) + dh


def dec_ffn(h, gain, weights, cot):
    tokens, width = h.shape
    cols, up, down_in, down_out, grads = ffn_specs(weights)
    sds = jax.ShapeDtypeStruct
    tile = pl.BlockSpec((tokens, width), lambda i: (0, 0))
    one = pl.BlockSpec((1, width), lambda i: (0, 0))
    return pl.pallas_call(
        dec_ffn_kernel,
        grid=(cols,),
        in_specs=[tile, one, up, down_in, tile],
        out_specs=[tile, tile, up, down_out, one],
        out_shape=[sds(h.shape, bf16), sds(h.shape, f32), grads, grads, sds((1, width), f32)],
        scratch_shapes=[
            pltpu.VMEM(h.shape, bf16),
            pltpu.VMEM(h.shape, bf16),
            pltpu.VMEM(h.shape, f32),
            pltpu.VMEM(h.shape, f32),
        ],
        compiler_params=PARAMS,
        name="dec_ffn",
    )(h, gain, weights, weights, cot)


def dec_attn_bwd_kernel(
    gb_ref, emb_ref, enc_ref, last_ref, g_ref, w_ref, table_ref, hot_ref,
    na_ref, qkv_ref, mixa_ref, hida_ref, nb_ref, cq_ref, ckv_ref, mixb_ref,
    gm_ref, gr_ref, dw_ref, dg_ref, dt_ref, strip_ref, acc_ref, dq_s, dk_s, dv_s, *, rows,
):
    tokens = emb_ref.shape[0]
    keys = enc_ref.shape[0]
    shards = dw_ref.shape[0]
    causal, allowed = dec_masks(rows, tokens // rows, keys // rows, last_ref, True)
    fill_strip(strip_ref, table_ref[...], hot_ref[...], -tokens)
    lane = lax.broadcasted_iota(jnp.int32, (tokens, 2 * HEAD_DIM), 1)

    def attend_back(q_at, k_at, v_at, do, bias_at, mask, take_score):
        for hp in range(HEADS // 2):
            ls = slice(hp * 2 * HEAD_DIM, (hp + 1) * 2 * HEAD_DIM)
            qp, kp, vp, dop = q_at(ls), k_at(ls), v_at(ls), do[:, ls]
            lanek = lax.broadcasted_iota(jnp.int32, kp.shape, 1)
            dq = dk = dv = None
            for sub in range(2):
                qm, km, dom = half(lane, qp, sub), half(lanek, kp, sub), half(lane, dop, sub)
                s = nt(kp, qm)
                if bias_at is not None:
                    s = s + bias_at(hp * 2 + sub)
                p = soft_columns(jnp.where(mask, s, MASKED))
                dp = nt(vp, dom)
                ds = (p * (dp - jnp.sum(dp * p, axis=0, keepdims=True))).astype(bf16)
                new = (tn(ds, km), nn(ds, qm), nn(p.astype(bf16), dom))
                dq, dk, dv = new if dq is None else (dq + new[0], dk + new[1], dv + new[2])
                if take_score is not None:
                    take_score(hp * 2 + sub, ds)
            dq_s[:, ls] = dq.astype(bf16)
            dk_s[: dk.shape[0], ls] = dk.astype(bf16)
            dv_s[: dv.shape[0], ls] = dv.astype(bf16)

    grad_b = gb_ref[...]
    branch = grad_b.astype(bf16)
    dw_ref[:, 7] = packed(tn(mixb_ref[...], branch), shards)
    do = nt(branch, matrix(w_ref, 7)).astype(bf16)
    attend_back(
        lambda ls: cq_ref[:, ls],
        lambda ls: ckv_ref[0, :, ls],
        lambda ls: ckv_ref[1, :, ls],
        do,
        None,
        allowed,
        None,
    )
    gm_ref[...] = nt(dk_s[...], matrix(w_ref, 5)) + nt(dv_s[...], matrix(w_ref, 6))
    dw_ref[:, 4] = packed(tn(nb_ref[...], dq_s[...]), shards)
    dw_ref[:, 5] = packed(tn(enc_ref[...], dk_s[...]), shards)
    dw_ref[:, 6] = packed(tn(enc_ref[...], dv_s[...]), shards)
    dh, dg = norm_back(hida_ref[...], g_ref[1:2], nt(dq_s[...], matrix(w_ref, 4)))
    dg_ref[1:2] = dg
    grad_a = grad_b + dh

    branch = grad_a.astype(bf16)
    dw_ref[:, 3] = packed(tn(mixa_ref[...], branch), shards)
    do = nt(branch, matrix(w_ref, 3)).astype(bf16)
    acc_ref[...] = jnp.zeros_like(acc_ref)

    def take_score(h, ds):
        acc_ref[h, :, :tokens] = ds.astype(f32)

    attend_back(
        lambda ls: qkv_ref[0, :, ls],
        lambda ls: qkv_ref[1, :, ls],
        lambda ls: qkv_ref[2, :, ls],
        do,
        lambda h: strip_ref[h, :, :tokens],
        causal,
        take_score,
    )
    parts = (dq_s[...], dk_s[:tokens], dv_s[:tokens])
    dn = nt(parts[0], matrix(w_ref, 0)) + nt(parts[1], matrix(w_ref, 1)) + nt(parts[2], matrix(w_ref, 2))
    for w in range(3):
        dw_ref[:, w] = packed(tn(na_ref[...], parts[w]), shards)
    dh, dg = norm_back(emb_ref[...].astype(f32), g_ref[0:1], dn)
    dg_ref[0:1] = dg
    gr_ref[...] = (grad_a + dh).astype(bf16)
    dt_ref[...] = strip_sums(acc_ref[...], hot_ref[...])


def dec_attn_bwd(grad_b, emb, enc_late, last, gains, weights, table, kept, rows):
    tokens, width = emb.shape
    keys = enc_late.shape[0]
    shards, _, blk, _ = weights.shape
    hot = dec_hot(tokens, tokens // rows, True)
    sds = jax.ShapeDtypeStruct
    outs = [
        sds((keys, width), f32),
        sds((tokens, width), bf16),
        sds((shards, 8, blk, width), bf16),
        sds((2, width), f32),
        sds(table.shape, f32),
    ]
    args = (grad_b, emb, enc_late, last, gains, weights, table, hot) + kept
    specs = [whole_spec(a) for a in args]
    specs[5] = pl.BlockSpec((shards, 8, blk, width), lambda i: (0, 0, 0, 0))
    strip = pltpu.VMEM((HEADS, tokens, 2 * tokens), f32)
    return pl.pallas_call(
        functools.partial(dec_attn_bwd_kernel, rows=rows),
        grid=(1,),
        in_specs=specs,
        out_specs=[whole_spec(o) for o in outs],
        out_shape=outs,
        scratch_shapes=[
            strip,
            strip,
            pltpu.VMEM((tokens, width), bf16),
            pltpu.VMEM((keys, width), bf16),
            pltpu.VMEM((keys, width), bf16),
        ],
        compiler_params=PARAMS,
        name="dec_attn_bwd",
    )(*args)


def pack_up(up, width):
    return up.reshape(up.shape[0], -1, width).transpose(1, 0, 2)


def unpack_up(blocks):
    return blocks.transpose(1, 0, 2).reshape(blocks.shape[1], -1)


def on_device(
    enc_input,
    segments,
    targets,
    enc_cot,
    dec_cot,
    enc_gains,
    enc_attn,
    enc_table,
    enc_up,
    enc_down,
    embed,
    dec_gains,
    dec_self,
    dec_cross,
    dec_table,
    dec_up,
    dec_down,
):
    rows, length, width = enc_input.shape
    steps = targets.shape[1]
    shards = lax.axis_size("fsdp")
    blk = enc_attn.shape[1]
    own = embed.shape[0]
    me = lax.axis_index("fsdp")
    late = min(length, SERIES_MOST)

    shifted = jnp.concatenate([jnp.zeros((rows, 1), jnp.int32), targets[:, :-1]], axis=1).reshape(-1)
    small = jnp.concatenate(
        [
            enc_gains.reshape(-1),
            dec_gains.reshape(-1),
            enc_table,
            dec_table,
            (shifted // 64).astype(bf16),
            (shifted % 64).astype(bf16),
        ]
    )
    small = lax.all_gather(small, "fsdp", axis=0, tiled=False)
    n_e, n_d, tab, ids = enc_gains.shape[0], dec_gains.shape[0], enc_table.shape[0], shifted.shape[0]
    at = (n_e + n_d) * blk
    gains = small[:, :at].reshape(shards, n_e + n_d, blk).transpose(1, 0, 2).reshape(n_e + n_d, width)
    enc_tab = small[:, at : at + tab].reshape(HEADS, BUCKETS)
    dec_tab = small[:, at + tab : at + 2 * tab].reshape(HEADS, BUCKETS)
    at += 2 * tab
    all_ids = small[:, at : at + ids].astype(jnp.int32) * 64 + small[:, at + ids :].astype(jnp.int32)

    w_attn = lax.all_gather(enc_attn, "fsdp", axis=0, tiled=False)
    ffn_blocks = jnp.concatenate([pack_up(enc_up, width), enc_down.reshape(-1, blk, width)], axis=0)
    w_ffn = lax.all_gather(ffn_blocks, "fsdp", axis=0, tiled=False)
    dec_blocks = jnp.concatenate([dec_self, dec_cross], axis=0)
    w_dec = lax.all_gather(dec_blocks, "fsdp", axis=0, tiled=False)
    dffn_blocks = jnp.concatenate([pack_up(dec_up, width), dec_down.reshape(-1, blk, width)], axis=0)
    w_dffn = lax.all_gather(dffn_blocks, "fsdp", axis=0, tiled=False)

    hot = (all_ids.reshape(-1)[:, None] == me * own + jnp.arange(own)[None, :]).astype(bf16)
    found = jnp.dot(hot, embed, preferred_element_type=f32).astype(bf16)
    emb = lax.psum_scatter(found, "fsdp", scatter_dimension=0, tiled=True)

    hidden, q, k, v, mix = enc_attn_fwd(enc_input, segments, gains[0:1], w_attn, enc_tab)
    hidden = hidden.reshape(-1, width)
    enc_out = ffn_fwd(hidden, gains[1:2], w_ffn).reshape(rows, length, width)
    enc_late = enc_out[:, length - late :].reshape(-1, width)
    last = (segments == segments[:, -1:])[:, length - late :].astype(jnp.int32).reshape(1, -1)
    dec_gain = gains[n_e:]
    kept = dec_attn_fwd(emb, enc_late, last, dec_gain, w_dec, dec_tab, rows)
    cot = dec_cot.reshape(-1, width)
    dec_out, grad_b, d_dup, d_ddown, dg_c = dec_ffn(kept[-1], dec_gain[2:3], w_dffn, cot)

    grad_late, grad_rows, d_dec, dg_ab, d_dtab = dec_attn_bwd(
        grad_b, emb, enc_late, last.reshape(-1, 1), dec_gain, w_dec, dec_tab, tuple(kept[:-1]), rows
    )
    grad_memory, grad_hidden, d_up, d_down, dg_1 = enc_ffn_bwd(
        hidden, gains[1:2], w_ffn, enc_cot, grad_late.reshape(rows, late, width)
    )
    dq, dk, dv, d_etab = enc_attn_bwd(
        grad_hidden.reshape(rows, length, width), q, k, v, segments, w_attn, enc_tab
    )
    flat = lambda a: a.reshape(-1, width)
    d_attn = enc_weight_grads(
        flat(enc_input), gains[0:1], flat(dq), flat(dk), flat(dv), flat(mix), grad_hidden, w_attn.shape
    )
    grad_input, dg_0 = enc_input_grad(
        flat(enc_input), gains[0:1], flat(dq), flat(dk), flat(dv), grad_hidden, w_attn
    )

    def owned(a):
        return lax.psum_scatter(a, "fsdp", scatter_dimension=0, tiled=False)

    s_dec = owned(jnp.concatenate([d_dec, d_dup, d_ddown], axis=1))
    all_rows = lax.all_gather(grad_rows, "fsdp", axis=0, tiled=True)
    g_embed = lax.dot_general(hot, all_rows, (((0,), (0,)), ((), ())), preferred_element_type=f32)
    s_enc = owned(jnp.concatenate([d_up, d_down, d_attn], axis=1))

    g_small = jnp.concatenate([dg_0, dg_1, dg_ab, dg_c], axis=0)
    g_small = jnp.concatenate(
        [
            g_small.reshape(n_e + n_d, shards, blk).transpose(1, 0, 2).reshape(shards, -1),
            d_etab.reshape(shards, tab),
            d_dtab.reshape(shards, tab),
        ],
        axis=1,
    )
    g_small = lax.psum(g_small, ("fsdp", "dp"))
    g_small = lax.dynamic_index_in_dim(g_small, me, 0, keepdims=False)
    at = (n_e + n_d) * blk
    g_gains = g_small[:at].reshape(n_e + n_d, blk)

    summed = jnp.concatenate(
        [s_dec.reshape(-1, width), s_enc.reshape(-1, width), g_embed.astype(bf16)], axis=0
    )
    summed = lax.psum(summed, "dp").astype(f32)
    counts = np.cumsum([0, 4, 4, dffn_blocks.shape[0] // 2, dffn_blocks.shape[0] // 2, ffn_blocks.shape[0] // 2, ffn_blocks.shape[0] // 2, 4])
    pieces = [summed[a * blk : b * blk].reshape(-1, blk, width) for a, b in zip(counts[:-1], counts[1:])]
    return (
        enc_out,
        dec_out.reshape(rows, steps, width),
        grad_input.reshape(rows, length, width),
        grad_memory,
        g_gains[:n_e],
        pieces[6],
        g_small[at : at + tab],
        unpack_up(pieces[4]),
        pieces[5].reshape(-1, width),
        summed[counts[-1] * blk :],
        g_gains[n_e:],
        pieces[0],
        pieces[1],
        g_small[at + tab :],
        unpack_up(pieces[2]),
        pieces[3].reshape(-1, width),
    )


def solution(mesh):
    placed = (
        P(("fsdp", "dp"), None, None),
        P(("fsdp", "dp"), None),
        P(("fsdp", "dp"), None),
        P(("fsdp", "dp"), None, None),
        P(("fsdp", "dp"), None, None),
        P(None, "fsdp"),
        P(None, "fsdp", None),
        P("fsdp"),
        P("fsdp", None),
        P("fsdp", None),
        P("fsdp", None),
        P(None, "fsdp"),
        P(None, "fsdp", None),
        P(None, "fsdp", None),
        P("fsdp"),
        P("fsdp", None),
        P("fsdp", None),
    )
    return jax.shard_map(
        on_device,
        mesh=mesh,
        in_specs=placed,
        out_specs=(
            P(("fsdp", "dp"), None, None),
            P(("fsdp", "dp"), None, None),
            P(("fsdp", "dp"), None, None),
            P(("fsdp", "dp"), None, None),
            P(None, "fsdp"),
            P(None, "fsdp", None),
            P("fsdp"),
            P("fsdp", None),
            P("fsdp", None),
            P("fsdp", None),
            P(None, "fsdp"),
            P(None, "fsdp", None),
            P(None, "fsdp", None),
            P("fsdp"),
            P("fsdp", None),
            P("fsdp", None),
        ),
        check_vma=False,
    )
```

time: 1040 us -> 534 us (0.51)
  blocking collectives: 326 us -> 54.5 us
  local copies, waits for them, and re-layouts: 273 us -> 23.5 us
  matrix products: 190 us -> 4.12 us
  waiting for transfers between devices: 143 us -> 299 us
  Pallas kernels: 0 us -> 115 us
  other arithmetic: 74.6 us -> 18.6 us
    unnamed x3 -> x0, blocking collectives: 278 us -> none
    dot_general x106 -> x2, matrix products: 190 us -> 4.12 us  [the longest x1 2.39 us: on_device(): lax.dot_general(hot, all_rows, (((0,), (0,)), ((), ())), preferred_elemen...]
    reduce_scatter x4 -> x3, waiting for transfers between devices: 0.01 us -> 155 us  [the longest x2 126 us: owned(): return lax.psum_scatter(a, 'fsdp', scatter_dimension=0, tiled=False)]
    unnamed x534 -> x46, local copies, waits for them, and re-layouts: 124 us -> 2.49 us
    pallas_call x0 -> x9, Pallas kernels: none -> 115 us  [the longest x1 25.8 us: enc_attn_bwd(): pl.pallas_call(enc_attn_bwd_kernel, grid=(rows,), in_specs=[pl.BlockSpec(...]
    all_gather x7 -> x5, waiting for transfers between devices: 0.87 us -> 100 us  [the longest x1 39.1 us: on_device(): w_dec = lax.all_gather(dec_blocks, 'fsdp', axis=0, tiled=False)]
    reshape x6 -> x13, local copies, waits for them, and re-layouts: 52.8 us -> 4.84 us  [the longest x2 1.66 us: unpack_up(): return blocks.transpose(1, 0, 2).reshape(blocks.shape[1], -1)]
    psum x1, waiting for transfers between devices: 86.7 us -> 43.2 us  [on_device(): summed = lax.psum(summed, 'dp').astype(f32)]
  transfers between devices with their start and end apart: 16 -> 9, of which waited for: 5 -> 8; matrix products, arithmetic and copies ran while one was open for 45% -> 7% of each run, Pallas kernels for 0% -> 18%
where the time goes in v1:
time: 534 us; the launch traced here: 530 us
  waiting for transfers between devices  299 us (56%)
  Pallas kernels  115 us (22%)
  blocking collectives  54.5 us (10%)
  local copies, waits for them, and re-layouts  23.5 us (4%)
  other arithmetic  18.6 us (3%)
  between operations  14.3 us (3%)
    reduce_scatter x2, waiting for transfers between devices, owned(): return lax.psum_scatter(a, 'fsdp', scatter_dimension=0, tiled=False)  126 us
    psum x1, blocking collectives, on_device(): g_small = lax.psum(g_small, ('fsdp', 'dp'))  44 us
    psum x1, waiting for transfers between devices, on_device(): summed = lax.psum(summed, 'dp').astype(f32)  43.2 us
    all_gather x1, waiting for transfers between devices, on_device(): w_dec = lax.all_gather(dec_blocks, 'fsdp', axis=0, tiled=False)  39.1 us
    all_gather x1, waiting for transfers between devices, on_device(): w_dffn = lax.all_gather(dffn_blocks, 'fsdp', axis=0, tiled=False)  29.3 us
    reduce_scatter x1, waiting for transfers between devices, on_device(): emb = lax.psum_scatter(found, 'fsdp', scatter_dimension=0, tiled=True)  29.2 us
    pallas_call x1, Pallas kernels, enc_attn_bwd(): pl.pallas_call(enc_attn_bwd_kernel, grid=(rows,), in_specs=[pl.BlockSpec(...  25.8 us
    all_gather x1, waiting for transfers between devices, on_device(): w_ffn = lax.all_gather(ffn_blocks, 'fsdp', axis=0, tiled=False)  24.2 us
  transfers between devices with their start and end apart: 9, of which 8 were waited for; matrix products, arithmetic and copies ran while one was open for 7% of the time, Pallas kernels for 18%

profile of v1, /device:TPU:0, one launch (start us, length us, event | category | flops | bytes accessed | tf_op | source)
XLA Modules:
  0.0 529.8 jit_solution(17800440313741231275)
XLA Ops:
  7.3 0.7 all-gather.14.cloned.1.call-update
  8.0 1.1 reshape.152
  9.2 1.2 copy.78
  10.3 0.3 pad_maximum_fusion.3
  10.6 0.9 copy.79
  11.6 0.1 concatenate.30
  11.7 0.1 reshape.149
  11.8 0.1 reshape.147
  11.9 0.1 reshape.148
  12.0 0.1 concatenate.31
  12.1 10.5 %all-gather.5 = bf16[8,1,640]{2,1,0:T(2,128)(2,1)S(1)} all-gather(bf16[1,1,640]{2,1,0:T(2,128)(2,1)S(1)} %reshape.183), channel_id=2, replica_groups=mesh['fsdp'=8,'dp'=4] {'fsdp'}, dimensions={0}, use_global_device_ids=true | all-gather | bytes 11520 | tf_op jit(solution)/shard_map/all_gather | solution.py:745
  22.6 1.7 fusion.4
  24.4 0.8 pad_maximum_fusion.4
  25.4 0.2 reshape.157
  25.6 0.2 copy.81
  25.8 0.3 pad_maximum_fusion.5
  26.0 0.9 copy.82
  27.1 0.1 reshape.150
  27.2 0.7 slice.110.g_ref
  27.9 0.6 broadcast_in_dim.10.segr_ref
  28.5 1.0 copy.77.segc_ref
  29.5 0.6 slice.113.g_ref
  30.1 0.7 slice.120.g_ref
  30.8 0.2 slice_reduce_fusion.3
  31.0 0.1 fusion.14
  31.1 0.6 slice.123.g_ref
  31.7 0.9 copy.93
  32.5 0.6 fusion.18
  33.1 7.5 %all-gather.14.cloned.1.call-done = bf16[32,64,512]{2,1,0:T(8,128)(2,1)} async-done(((bf16[4,64,512]{2,1,0:T(8,128)(2,1)}), bf16[32,64,512]{2,1,0:T(8,128)(2,1)}) %all-gather.14.cloned.1.call-update) | async-done | bytes 2097168 | tf_op jit(solution)/shard_map/all_gather | solution.py:754
  40.6 15.0 %enc_attn_fwd.1 = (f32[2,512,512]{2,1,0:T(8,128)}, bf16[2,512,512]{2,1,0:T(8,128)(2,1)}, bf16[2,512,512]{2,1,0:T(8,128)(2,1)}, bf16[2,512,512]{2,1,0:T(8,128)(2,1)}, bf16[2,512,512]{2,1,0:T(8,128)(2,1)}) custom-call(bf16[2,512,512]{2,1,0:T(8,128)(2,1)} %x_ref.1, s32[2,512,1]{2,1,0:T(8,128)} %copy.77.segc_ref, s32[2,1,512]{2,1,0:T(1,128)} %broadcast_in_dim.10.segr_ref, ...), custom_call_target="tpu_custom_call" | custom-call | tf_op jit(solution)/shard_map/enc_attn_fwd/pallas_call | solution.py:188
  55.7 24.2 %all-gather.16.cloned.1.call-done = bf16[64,64,512]{2,1,0:T(8,128)(2,1)} async-done(((bf16[8,64,512]{2,1,0:T(8,128)(2,1)}), bf16[64,64,512]{2,1,0:T(8,128)(2,1)}) %all-gather.16.cloned.1.call-update) | async-done | bytes 4194320 | tf_op jit(solution)/shard_map/all_gather | solution.py:756
  79.8 8.7 %enc_ffn_fwd.1 = bf16[1024,512]{1,0:T(8,128)(2,1)} custom-call(f32[1024,512]{1,0:T(8,128)} %bitcast.74, bf16[1,512]{1,0:T(2,128)(2,1)} %slice.113.g_ref, bf16[8,8,64,512]{3,2,1,0:T(8,128)(2,1)} %bitcast.61), custom_call_target="tpu_custom_call" | custom-call | tf_op jit(solution)/shard_map/enc_ffn_fwd/pallas_call | solution.py:222
  88.6 1.9 slice.146
  90.4 29.2 %reduce-scatter.4.cloned.1.call-done.emb_ref = bf16[128,512]{1,0:T(8,128)(2,1)} async-done(((bf16[1024,512]{1,0:T(8,128)(2,1)}), bf16[128,512]{1,0:T(8,128)(2,1)}) %reduce-scatter.4.cloned.1.call-update) | async-done | bytes 131088 | tf_op jit(solution)/shard_map/reduce_scatter | solution.py:764
  119.7 39.1 %all-gather.18.cloned.1.call-done = bf16[64,64,512]{2,1,0:T(8,128)(2,1)} async-done(((bf16[8,64,512]{2,1,0:T(8,128)(2,1)}), bf16[64,64,512]{2,1,0:T(8,128)(2,1)}) %all-gather.18.cloned.1.call-update) | async-done | bytes 4194320 | tf_op jit(solution)/shard_map/all_gather | solution.py:758
  158.7 9.8 %dec_attn_fwd.1 = (bf16[128,512]{1,0:T(8,128)(2,1)}, bf16[3,128,512]{2,1,0:T(8,128)(2,1)}, bf16[128,512]{1,0:T(8,128)(2,1)}, f32[128,512]{1,0:T(8,128)}, bf16[12...) custom-call(bf16[128,512]{1,0:T(8,128)(2,1)} %reduce-scatter.4.clone, ...), custom_call_target="tpu_custom_call" | custom-call | tf_op jit(solution)/shard_map/dec_attn_fwd/pallas_call | solution.py:514
  168.5 29.3 %all-gather.20.cloned.1.call-done = bf16[64,64,512]{2,1,0:T(8,128)(2,1)} async-done(((bf16[8,64,512]{2,1,0:T(8,128)(2,1)}), bf16[64,64,512]{2,1,0:T(8,128)(2,1)}) %all-gather.20.cloned.1.call-update) | async-done | bytes 4194320 | tf_op jit(solution)/shard_map/all_gather | solution.py:760
  197.8 8.2 %dec_ffn.1 = (bf16[128,512]{1,0:T(8,128)(2,1)}, f32[128,512]{1,0:T(8,128)}, bf16[8,4,64,512]{3,2,1,0:T(8,128)(2,1)}, bf16[8,4,64,512]{3,2,1,0:T(8,128)(2,1)}, f32[1,512]{1,0:T(1,128)}) custom-call(f32[128,512]{1,0:T(8,128)} %get-tuple-element.52.h_ref, bf16[1,512]{1,0:T(2,128)(2,1)} %slice.123.g_ref, bf16[8,8,64,512]{3,2,1,0:T(8,128)(2,1)} %bitcast.68, ...), custom_call_target="tpu_custom_call" | custom-call | tf_op jit(solution)/shard_map/dec_ffn/pallas_call | solution.py:565
  206.0 12.8 %dec_attn_bwd.1 = (f32[512,512]{1,0:T(8,128)}, bf16[128,512]{1,0:T(8,128)(2,1)}, bf16[8,8,64,512]{3,2,1,0:T(8,128)(2,1)}, f32[2,512]{1,0:T(2,128)}, f32[8,32]{1,0:T(8,128)}) custom-call(f32[128,512]{1,0:T(8,128)} %get-tuple-element.54.gb_ref, bf16[128,512]{1,0:T(8,128)(2,1)} %reduce-scatter.4.cloned.1.call-done.emb_ref, bf16[512,512]{1,0:T(8,128)(2,1)} %bitcast.77, ...), custom_call_target="tpu_custom_call" | custom-call | tf_op jit(solution)/shard_map/dec_attn_bwd/pallas_call | solution.py:681
  218.9 20.8 %enc_ffn_bwd.1 = (f32[2,512,512]{2,1,0:T(8,128)}, f32[1024,512]{1,0:T(8,128)}, bf16[8,4,64,512]{3,2,1,0:T(8,128)(2,1)}, bf16[8,4,64,512]{3,2,1,0:T(8,128)(2,1)}, f32[1,512]{1,0:T(1,128)}) custom-call(f32[1024,512]{1,0:T(8,128)} %bitcast.75, bf16[1,512]{1,0:T(2,128)(2,1)} %slice.113.g_ref, bf16[8,8,64,512]{3,2,1,0:T(8,128)(2,1)} %bitcast.62, ...), custom_call_target="tpu_custom_call" | custom-call | tf_op jit(solution)/shard_map/enc_ffn_bwd/pallas_call | solution.py:291
  239.6 25.8 %enc_attn_bwd.1 = (bf16[2,512,512]{2,1,0:T(8,128)(2,1)}, bf16[2,512,512]{2,1,0:T(8,128)(2,1)}, bf16[2,512,512]{2,1,0:T(8,128)(2,1)}, f32[8,32]{1,0:T(8,128)}) custom-call(f32[2,512,512]{2,1,0:T(8,128)} %bitcast.67, bf16[2,512,512]{2,1,0:T(8,128)(2,1)} %get-tuple-element.65.q_ref, bf16[2,512,512]{2,1,0:T(8,128)(2,1)} %get-tuple-element.66.k_ref, ...), custom_call_target="tpu_custom_call" | custom-call | tf_op jit(solution)/shard_map/enc_attn_bwd/pallas_call | solution.py:371
  265.5 7.3 %enc_weight_grads.1 = bf16[8,4,64,512]{3,2,1,0:T(8,128)(2,1)} custom-call(bf16[1024,512]{1,0:T(8,128)(2,1)} %bitcast.72, bf16[1,512]{1,0:T(2,128)(2,1)} %slice.110.g_ref, bf16[1024,512]{1,0:T(8,128)(2,1)} %bitcast.78, bf16[1024,512]{1,0:T(8,128)(2,1)} %bitcast.80, bf16[1024,512]{1,0:T(8,128)(2,1)} %bitcast.82, bf16[1024,512]{1,0:T(8,128)(2,1)} %bitcast.88, ...), custom_call_target="tpu_custom_call" | custom-call | tf_op jit(solution)/shard_map/enc_weight_grads/pallas_call | solution.py:399
  272.8 6.4 %pad_maximum_fusion.1 = bf16[8,12,64,512]{3,2,1,0:T(8,128)(2,1)} fusion(bf16[8,4,64,512]{3,2,1,0:T(8,128)(2,1)} %enc_weight_grads.1, bf16[8,4,64,512]{3,2,1,0:T(8,128)(2,1)S(1)} %copy-done.3, bf16[8,4,64,512]{3,2,1,0:T(8,128)(2,1)S(1)} %copy-done.2), kind=kLoop, calls=%fused_computation.1 | loop fusion | flops 6291456 | bytes 12582912 | tf_op jit(solution)/shard_map/concatenate | solution.py:799
  279.4 1.5 copy-done.4
  280.9 6.8 %pad_maximum_fusion = bf16[8,16,64,512]{3,2,1,0:T(8,128)(2,1)} fusion(bf16[8,4,64,512]{3,2,1,0:T(8,128)(2,1)} %get-tuple-element.81, bf16[8,4,64,512]{3,2,1,0:T(8,128)(2,1)S(1)} %copy-done.4, bf16[8,8,64,512]{3,2,1,0:T(8,128)(2,1)} %get-tuple-element.79), kind=kLoop, calls=%fused_computation | loop fusion | flops 8388608 | bytes 16777216 | tf_op jit(solution)/shard_map/concatenate | solution.py:796
  287.8 2.4 fusion.7
  290.2 51.0 %reduce-scatter.8.cloned.1.call-done = bf16[1,12,64,512]{3,2,1,0:T(8,128)(2,1)} async-done(((bf16[8,12,64,512]{3,2,1,0:T(8,128)(2,1)}), bf16[1,12,64,512]{3,2,1,0:T(8,128)(2,1)}) %reduce-scatter.8.cloned.1.call-update) | async-done | bytes 786448 | tf_op jit(solution)/shard_map/reduce_scatter | solution.py:794
  341.2 75.2 %reduce-scatter.6.cloned.1.call-done = bf16[1,16,64,512]{3,2,1,0:T(8,128)(2,1)} async-done(((bf16[8,16,64,512]{3,2,1,0:T(8,128)(2,1)}), bf16[1,16,64,512]{3,2,1,0:T(8,128)(2,1)}) %reduce-scatter.6.cloned.1.call-update) | async-done | bytes 1048592 | tf_op jit(solution)/shard_map/reduce_scatter | solution.py:794
  416.4 3.1 pad_maximum_fusion.2
  419.5 6.5 %enc_input_grad.1 = (f32[1024,512]{1,0:T(8,128)}, f32[1,512]{1,0:T(1,128)}) custom-call(bf16[1024,512]{1,0:T(8,128)(2,1)} %bitcast.73, bf16[1,512]{1,0:T(2,128)(2,1)} %slice.110.g_ref, bf16[1024,512]{1,0:T(8,128)(2,1)} %bitcast.79, bf16[1024,512]{1,0:T(8,128)(2,1)} %bitcast.81, bf16[1024,512]{1,0:T(8,128)(2,1)} %bitcast.83, ...), custom_call_target="tpu_custom_call" | custom-call | tf_op jit(solution)/shard_map/enc_input_grad/pallas_call | solution.py:424
  426.0 0.7 pad_maximum_fusion.6
  426.7 0.1 reshape.168
  426.8 0.1 reshape.169
  426.9 0.1 pad_maximum_fusion.7
  427.0 44.0 %psum.14 = f32[8,384]{1,0:T(8,128)S(1)} all-reduce(f32[8,384]{1,0:T(8,128)S(1)} %pad_maximum_fusion.7), channel_id=1, replica_groups=mesh['fsdp'=8,'dp'=4] {'fsdp','dp'}, use_global_device_ids=true, to_apply=%region_1.2 | all-reduce | flops 3072 | bytes 24576 | tf_op jit(solution)/shard_map/psum | solution.py:810
  471.0 0.1 dynamic-slice_reduce_fusion
  471.1 0.7 slice.133
  471.7 0.6 slice.125
  472.4 0.6 dynamic-slice_bitcast_fusion
  473.0 43.2 %all-reduce.3.cloned.1.call-done = bf16[2304,512]{1,0:T(8,128)(2,1)} async-done(((bf16[2304,512]{1,0:T(8,128)(2,1)}), bf16[2304,512]{1,0:T(8,128)(2,1)}) %all-reduce.3.cloned.1.call-update) | async-done | bytes 2359312 | tf_op jit(solution)/shard_map/psum | solution.py:818
  516.2 3.0 fusion.17
  519.2 0.8 copy.89
  520.1 0.8 copy.90
  520.9 2.1 slice.154
  (71 shorter events, 0.8 us)
Async XLA Ops:
  7.2 15.4 %copy-start = (bf16[512,512]{1,0:T(8,128)(2,1)S(1)}, bf16[512,512]{1,0:T(8,128)(2,1)}, u32[]{:S(2)}) copy-start(bf16[512,512]{1,0:T(8,128)(2,1)} %param.31) | copy-start | bytes 1572868
  7.2 4.4 copy-start.16
  7.2 4.6 copy-start.20
  7.2 4.7 copy-start.19
  7.2 4.8 copy-start.17
  7.2 4.8 copy-start.18
  7.2 33.4 %all-gather.14.cloned.1.call-start = ((), (), s32[]{:S(2)}) async-start(), calls=%async_computation.8 | async-start | bytes 2359296 | tf_op jit(solution)/shard_map/all_gather | solution.py:754
  8.0 71.8 %all-gather.16.cloned.1.call-start = ((), (), s32[]{:S(2)}) async-start(), calls=%async_computation.9 | async-start | bytes 4718592 | tf_op jit(solution)/shard_map/all_gather | solution.py:756
  11.5 12.9 %copy-start.7 = (bf16[4,64,512]{2,1,0:T(8,128)(2,1)S(1)}, bf16[4,64,512]{2,1,0:T(8,128)(2,1)}, u32[]{:S(2)}) copy-start(bf16[4,64,512]{2,1,0:T(8,128)(2,1)} %param.34) | copy-start | bytes 786436
  11.6 12.9 %copy-start.8 = (bf16[4,64,512]{2,1,0:T(8,128)(2,1)S(1)}, bf16[4,64,512]{2,1,0:T(8,128)(2,1)}, u32[]{:S(2)}) copy-start(bf16[4,64,512]{2,1,0:T(8,128)(2,1)} %param.33) | copy-start | bytes 786436
  11.6 108.1 %reduce-scatter.4.cloned.1.call-start = ((), (), s32[]{:S(2)}) async-start(), calls=%async_computation.3 | async-start | bytes 1179648 | tf_op jit(solution)/shard_map/reduce_scatter | solution.py:764
  22.6 2.8 copy-start.5
  22.6 3.0 copy-start.6
  24.4 134.3 %all-gather.18.cloned.1.call-start = ((), (), s32[]{:S(2)}) async-start(), calls=%async_computation.10 | async-start | bytes 4718592 | tf_op jit(solution)/shard_map/all_gather | solution.py:758
  25.3 2.6 copy-start.9
  25.3 172.5 %all-gather.20.cloned.1.call-start = ((), (), s32[]{:S(2)}) async-start(), calls=%async_computation.11 | async-start | bytes 4718592 | tf_op jit(solution)/shard_map/all_gather | solution.py:760
  27.0 260.8 %all-gather.12.cloned.1.call-start = ((), (), s32[]{:S(2)}) async-start(), calls=%async_computation.6 | async-start | bytes 1179648 | tf_op jit(solution)/shard_map/all_gather | solution.py:797
  31.1 57.5 %copy-start.10 = (s32[1,1,2,256]{3,1,2,0:T(1,128)}, s32[1,1,2,256]{3,1,2,0:T(1,128)S(1)}, u32[]{:S(2)}) copy-start(s32[1,1,2,256]{3,1,2,0:T(1,128)S(1)} %copy.91) | copy-start | bytes 6148
  218.8 122.4 %reduce-scatter.8.cloned.1.call-start = ((), (), s32[]{:S(2)}) async-start(), calls=%async_computation.5 | async-start | bytes 7077888 | tf_op jit(solution)/shard_map/reduce_scatter | solution.py:794
  265.5 7.3 %copy-start.2 = (bf16[8,4,64,512]{3,2,1,0:T(8,128)(2,1)S(1)}, bf16[8,4,64,512]{3,2,1,0:T(8,128)(2,1)}, u32[]{:S(2)}) copy-start(bf16[8,4,64,512]{3,2,1,0:T(8,128)(2,1)} %get-tuple-element.82) | copy-start | bytes 6291460
  265.5 7.3 %copy-start.3 = (bf16[8,4,64,512]{3,2,1,0:T(8,128)(2,1)S(1)}, bf16[8,4,64,512]{3,2,1,0:T(8,128)(2,1)}, u32[]{:S(2)}) copy-start(bf16[8,4,64,512]{3,2,1,0:T(8,128)(2,1)} %get-tuple-element.83) | copy-start | bytes 6291460
  279.3 1.6 copy-start.4
  279.3 137.1 %reduce-scatter.6.cloned.1.call-start = ((), (), s32[]{:S(2)}) async-start(), calls=%async_computation.4 | async-start | bytes 9437184 | tf_op jit(solution)/shard_map/reduce_scatter | solution.py:794
  287.7 228.5 %all-reduce.3.cloned.1.call-start = ((), (), s32[]{:S(2)}) async-start(), calls=%async_computation.7 | async-start | bytes 4718592 | tf_op jit(solution)/shard_map/psum | solution.py:818
  419.5 6.5 %copy-start.11 = (f32[2,512]{1,0:T(2,128)S(1)}, f32[2,512]{1,0:T(2,128)}, u32[]{:S(2)}) copy-start(f32[2,512]{1,0:T(2,128)} %get-tuple-element.75) | copy-start | bytes 12292
  419.5 6.5 %copy-start.14 = (f32[1,512]{1,0:T(1,128)S(1)}, f32[1,512]{1,0:T(1,128)}, u32[]{:S(2)}) copy-start(f32[1,512]{1,0:T(1,128)} %get-tuple-element.76) | copy-start | bytes 6148
  419.5 6.5 %copy-start.15 = (f32[1,512]{1,0:T(1,128)S(1)}, f32[1,512]{1,0:T(1,128)}, u32[]{:S(2)}) copy-start(f32[1,512]{1,0:T(1,128)} %get-tuple-element.74) | copy-start | bytes 6148
  419.5 7.4 %copy-start.12 = (f32[8,32]{1,0:T(8,128)S(1)}, f32[8,32]{1,0:T(8,128)}, u32[]{:S(2)}) copy-start(f32[8,32]{1,0:T(8,128)} %get-tuple-element.78) | copy-start | bytes 3076
  419.5 7.4 %copy-start.13 = (f32[8,32]{1,0:T(8,128)S(1)}, f32[8,32]{1,0:T(8,128)}, u32[]{:S(2)}) copy-start(f32[8,32]{1,0:T(8,128)} %get-tuple-element.77) | copy-start | bytes 3076
  516.2 6.8 %copy-start.1 = (bf16[512,512]{1,0:T(8,128)(2,1)S(1)}, bf16[512,512]{1,0:T(8,128)(2,1)}, u32[]{:S(2)}) copy-start(bf16[512,512]{1,0:T(8,128)(2,1)} %param.31) | copy-start | bytes 1572868
Sparse Core Ops, SparseCore 0:
  10.0 30.5 all-gather.13
  43.1 36.7 all-gather.15
  83.6 36.0 reduce-scatter.3
  122.0 36.6 all-gather.17
  161.0 36.7 all-gather.19
  219.0 23.5 all-gather.11
  279.4 61.7 reduce-scatter.7
  345.1 71.2 reduce-scatter.5
  419.6 96.5 all-reduce.2

commit v2 on v1

v2 whole, which is shorter than its diff:
```python
import functools

import jax
import jax.numpy as jnp
import numpy as np
from jax import lax
from jax.experimental import pallas as pl
from jax.experimental.pallas import tpu as pltpu
from jax.sharding import PartitionSpec as P

HEADS = 8
HEAD_DIM = 64
BUCKETS = 32
SERIES_MOST = 256
TILE = 128
MASKED = -1000000000.0

epsilon = 1e-06
f32 = jnp.float32
bf16 = jnp.bfloat16
PEAK = 1.15e9

TABLE_ROW = 0
GAIN_ROW = 8
ID_ROW = 13
SMALL_ROWS = 16
DEC_LANE = 128


def bucket_codes(length, both_ways):
    bucket_list = []
    for offset in range(-(length - 1), length):
        if both_ways:
            upper_half = 16 if offset > 0 else 0
            distance = abs(offset)
            if distance < 8:
                bucket = distance
            else:
                bucket = 8 + sum(
                    (1 for exponent in range(1, 8) if distance * distance >= 64 * 2**exponent)
                )
        else:
            upper_half = 0
            distance = max(-offset, 0)
            if distance < 16:
                bucket = distance
            else:
                bucket = 16 + sum(
                    (1 for exponent in range(1, 16) if distance**16 >= 16**16 * 2 ** (3 * exponent))
                )
        bucket_list.append(upper_half + bucket)
    return np.array(bucket_list, dtype=np.int32)


def offset_hot(length, both_ways, reverse):
    codes = np.concatenate([bucket_codes(length, both_ways), [-1]])
    if reverse:
        codes = codes[::-1]
    return jnp.asarray(codes[None, :] == np.arange(BUCKETS)[:, None], bf16)


def nn(a, b):
    return lax.dot_general(a, b, (((1,), (0,)), ((), ())), preferred_element_type=f32)


def nt(a, b):
    return lax.dot_general(a, b, (((1,), (1,)), ((), ())), preferred_element_type=f32)


def tn(a, b):
    return lax.dot_general(a, b, (((0,), (0,)), ((), ())), preferred_element_type=f32)


def rho_of(h):
    return lax.rsqrt(jnp.mean(h * h, axis=-1, keepdims=True) + epsilon)


def normed(h, gain):
    return (h * rho_of(h) * gain.astype(f32)).astype(bf16)


def norm_back(h, gain, dn):
    rho = rho_of(h)
    xh = h * rho
    gu = dn * gain.astype(f32)
    return rho * (gu - xh * jnp.mean(gu * xh, axis=-1, keepdims=True))


def gelu(u):
    t = jnp.tanh(np.float32(np.sqrt(2 / np.pi)) * (u + 0.044715 * (u * u * u)))
    return 0.5 * u * (1.0 + t)


def gelu_both(u):
    c = np.float32(np.sqrt(2 / np.pi))
    u2 = u * u
    t = jnp.tanh(c * (u + 0.044715 * (u2 * u)))
    cdf = 0.5 * (1.0 + t)
    return u * cdf, cdf + 0.5 * u * (1.0 - t * t) * (c + (3 * 0.044715 * c) * u2)


def matrix(ref, w):
    part = ref[:, w]
    return part.reshape(part.shape[0] * part.shape[1], part.shape[2])


def packed(value, shards):
    return value.reshape(shards, value.shape[0] // shards, value.shape[1]).astype(bf16)


def place(shard, me, shards):
    upper = shards.bit_length() - 2
    diff = shard ^ me
    spot = 0
    for j in range(upper):
        even = (diff >> (1 + j)) & 1
        odd = (diff >> (upper - j)) & 1
        spot = spot | (jnp.where((shard & 1) == 0, even, odd) << (upper - 1 - j))
    return spot


def shard_at(spot, me, shards):
    upper = shards.bit_length() - 2
    diff_even = diff_odd = 0
    for j in range(upper):
        bit = (spot >> (upper - 1 - j)) & 1
        diff_even = diff_even | (bit << (1 + j))
        diff_odd = diff_odd | (bit << (upper - j))
    return me ^ jnp.where((me & 1) == 0, diff_even, diff_odd)


def spread(refs):
    return [(ref, i) for ref in refs for i in range(ref.shape[0])]


def collect(out_ref, refs, me, rows=None):
    shards = out_ref.shape[0]
    count = len(refs) // 2
    for core, part in ((me, refs[:count]), (me ^ 1, refs[count:])):
        for p, (ref, i) in enumerate(spread(part)):
            piece = ref[i] if rows is None else ref[i, :rows]
            out_ref[shard_at(p, core, shards)] = piece.reshape(out_ref.shape[1:])


SCALAR = pl.BlockSpec(memory_space=pltpu.SMEM)
ANYWHERE = pl.BlockSpec(memory_space=pl.ANY)
sds = jax.ShapeDtypeStruct


def whole_spec(a):
    zeros = (0,) * len(a.shape)
    return pl.BlockSpec(a.shape, lambda i: zeros)


def call(kernel, name, us, args, in_specs, outs, out_specs, scratch=(), grid=1, after=(), vmem=24):
    waits = len(after)

    def body(*refs):
        kernel(*refs[waits:])

    return pl.pallas_call(
        body,
        grid=(grid,),
        in_specs=[ANYWHERE] * waits + list(in_specs),
        out_specs=list(out_specs),
        out_shape=[sds(o.shape, o.dtype) for o in outs],
        scratch_shapes=list(scratch),
        compiler_params=pltpu.CompilerParams(vmem_limit_bytes=int(vmem * 2**20)),
        cost_estimate=pl.CostEstimate(flops=int(us * PEAK), bytes_accessed=1024, transcendentals=0),
        name=name,
    )(*after, *args)


def simple(kernel, name, us, args, outs, after=(), scratch=(), vmem=None):
    if vmem is None:
        vmem = 1 + sum(2 * np.prod(a.shape) * a.dtype.itemsize for a in (*args, *outs)) / 2**20
    return call(
        kernel, name, us, args, [whole_spec(a) for a in args], outs, [whole_spec(o) for o in outs], scratch,
        after=after, vmem=vmem,
    )


def half(lane, value, which):
    return jnp.where((lane // HEAD_DIM) == which, value, jnp.zeros_like(value))


def fill_strip(strip_ref, table, hot, shift):
    vec = nn(table, hot)
    width = hot.shape[1]
    rows = strip_ref.shape[1]
    for h in range(HEADS):
        row = jnp.broadcast_to(vec[h : h + 1], (rows, width))
        strip_ref[h] = pltpu.roll(row, (width + shift) % width, 1, stride=1, stride_axis=0)


def strip_sums(acc, hot):
    rows, width = acc.shape[1], acc.shape[2]
    total = jnp.zeros((HEADS, 8, width), f32)
    for g in range(rows // 8):
        part = acc[:, g * 8 : g * 8 + 8, :].reshape(HEADS * 8, width)
        if g:
            part = pltpu.roll(part, width - 8 * g, 1)
        total = total + part.reshape(HEADS, 8, width)
    flat = total.reshape(HEADS * 8, width)
    sub = lax.broadcasted_iota(jnp.int32, flat.shape, 0) % 8
    for b in range(3):
        flat = jnp.where((sub >> b) & 1 == 1, pltpu.roll(flat, width - (1 << b), 1), flat)
    diag = pltpu.roll(jnp.sum(flat.reshape(HEADS, 8, width), axis=1), rows, 1)
    return lax.dot_general(
        diag,
        hot.astype(f32),
        (((1,), (1,)), ((), ())),
        precision=lax.Precision.HIGHEST,
        preferred_element_type=f32,
    )


def soft_rows(s):
    e = jnp.exp(s - jnp.max(s, axis=-1, keepdims=True))
    return e * (1.0 / jnp.sum(e, axis=-1, keepdims=True))


def soft_columns(s):
    e = jnp.exp(s - jnp.max(s, axis=0, keepdims=True))
    return e * (1.0 / jnp.sum(e, axis=0, keepdims=True))


def pack_first_kernel(me_ref, attn_ref, eg_ref, dg_ref, et_ref, dt_ref, tok_ref, out_ref, *, shards):
    count, blk, width = attn_ref.shape
    me = me_ref[0]
    out_ref[: count * blk] = attn_ref[...].reshape(count * blk, width)
    base = count * blk
    lane = lax.broadcasted_iota(jnp.int32, (1, width), 1)
    here = (lane // blk) == me
    per = et_ref.shape[1]
    row8 = lax.broadcasted_iota(jnp.int32, (HEADS, BUCKETS), 0)
    lane8 = lax.broadcasted_iota(jnp.int32, (HEADS, BUCKETS), 1)
    held = (row8 * BUCKETS + lane8) // per == me
    small = jnp.zeros((SMALL_ROWS, width), f32)
    rows = lax.broadcasted_iota(jnp.int32, (SMALL_ROWS, width), 0)
    gains = [eg_ref[i : i + 1] for i in range(eg_ref.shape[0])] + [dg_ref[i : i + 1] for i in range(dg_ref.shape[0])]
    for i, g in enumerate(gains):
        wide = jnp.where(here, jnp.concatenate([g.astype(f32)] * shards, axis=1), 0.0)
        small = jnp.where(rows == GAIN_ROW + i, jnp.broadcast_to(wide, small.shape), small)
    tok = tok_ref[...]
    steps = tok.shape[1]
    first = lax.broadcasted_iota(jnp.int32, tok.shape, 1) == 0
    shifted = jnp.where(first, 0, pltpu.roll(tok, 1, 1) if steps % 128 == 0 else jnp.concatenate([tok[:, -1:], tok[:, :-1]], axis=1))
    parts = [(shifted[r : r + 1] >> 6).astype(f32) for r in range(tok.shape[0])]
    parts += [(shifted[r : r + 1] & 63).astype(f32) for r in range(tok.shape[0])]
    ids = jnp.concatenate(parts, axis=1)
    ids = jnp.concatenate([ids, jnp.zeros((1, width - ids.shape[1]), f32)], axis=1)
    small = jnp.where(rows == ID_ROW, jnp.broadcast_to(ids, small.shape), small)
    out_ref[base:] = small.astype(bf16)
    for t_ref, at in ((et_ref, 0), (dt_ref, DEC_LANE)):
        table = jnp.concatenate([t_ref[...].astype(f32)] * (BUCKETS // per), axis=1)
        table = jnp.where(held, jnp.broadcast_to(table, held.shape), 0.0)
        out_ref[base : base + HEADS, at : at + BUCKETS] = table.astype(bf16)


def pack_first(me, attn, enc_gains, dec_gains, enc_table, dec_table, targets, shards):
    count, blk, width = attn.shape
    out = sds((1, count * blk + SMALL_ROWS, width), bf16)
    args = (attn, enc_gains, dec_gains, enc_table.reshape(1, -1), dec_table.reshape(1, -1), targets)

    def body(me_ref, *refs):
        pack_first_kernel(me_ref, *refs[:-1], refs[-1].at[0], shards=shards)

    return call(
        body, "pack_first", 2, (me,) + args, [SCALAR] + [whole_spec(a) for a in args], [out], [whole_spec(out)], vmem=4
    )[0]


def pack_ffn_kernel(up_ref, down_ref, out_ref, *, shards):
    blocks = out_ref.shape[0] // 2
    blk = up_ref.shape[0]
    for b in range(blocks):
        parts = [up_ref[:, (c * blocks + b) * blk : (c * blocks + b + 1) * blk] for c in range(shards)]
        out_ref[2 * b] = jnp.concatenate(parts, axis=1)
        out_ref[2 * b + 1] = down_ref[b * blk : (b + 1) * blk]


def pack_ffn(up, down, shards, after):
    blk, width = up.shape[0], down.shape[1]
    out = sds((1, 2 * up.shape[1] // width, blk, width), bf16)

    def body(up_ref, down_ref, out_ref):
        pack_ffn_kernel(up_ref, down_ref, out_ref.at[0], shards=shards)

    return simple(body, "pack_ffn", 1, (up, down), [out], after)[0]


def pack_attn_kernel(a_ref, b_ref, out_ref):
    count = a_ref.shape[0]
    out_ref[0, :count] = a_ref[...]
    out_ref[0, count:] = b_ref[...]


def pack_attn(a, b, after):
    out = sds((1, 2 * a.shape[0]) + a.shape[1:], bf16)
    return simple(pack_attn_kernel, "pack_attn", 1, (a, b), [out], after)[0]


def gate_kernel(a_ref, o_ref):
    o_ref[...] = a_ref[...]


def gate(a, after):
    return simple(gate_kernel, "gate", 0.5, (a,), [a], after)[0]


def join_kernel(a_ref, b_ref, o_ref):
    size = a_ref.shape[0]
    o_ref[:size] = a_ref[...]
    o_ref[size:] = b_ref[...]


def join(a, b, after):
    return simple(join_kernel, "join", 1, (a, b), [sds((2 * a.shape[0],) + a.shape[1:], a.dtype)], after)[0]


def add_first_kernel(me_ref, *refs):
    parts = len(refs[:-2]) // 4
    keep_ref, send_ref = refs[-2:]
    for out_ref, far in ((keep_ref, 0), (send_ref, 1)):
        at = 0
        for i in range(parts):
            a_ref, b_ref = refs[4 * i + 2 * far], refs[4 * i + 2 * far + 1]
            size = a_ref.shape[1]
            out_ref[0, at : at + size] = (a_ref[0].astype(f32) + b_ref[0].astype(f32)).astype(bf16)
            at += size


def add_first(me, pairs, after):
    shards = pairs[0][0].shape[0]
    quarter = shards // 4
    rest = (0,) * (len(pairs[0][0].shape) - 1)
    waits = len(after)

    def body(*refs):
        add_first_kernel(refs[0], *refs[1 + waits :])

    args, specs, size, total = [], [], 0, 0
    for grads, other in pairs:
        block = (1,) + grads.shape[1:]
        near = pl.BlockSpec(block, lambda p, me_ref: (shard_at(p, me_ref[0], shards),) + rest)
        far = pl.BlockSpec(block, lambda p, me_ref: (shard_at(p + quarter, me_ref[0], shards),) + rest)
        args += [grads, other, grads, other]
        specs += [near, near, far, far]
        size += grads.shape[1]
        total += np.prod(block) * 2
    out = (quarter, size) + pairs[0][0].shape[2:]
    out_spec = pl.BlockSpec((1,) + out[1:], lambda p, me_ref: (p,) + rest)
    return pl.pallas_call(
        body,
        grid_spec=pltpu.PrefetchScalarGridSpec(
            num_scalar_prefetch=1,
            grid=(quarter,),
            in_specs=[ANYWHERE] * waits + specs,
            out_specs=[out_spec, out_spec],
        ),
        out_shape=[sds(out, bf16)] * 2,
        compiler_params=pltpu.CompilerParams(vmem_limit_bytes=int(2 * 6 * total + 2**20)),
        cost_estimate=pl.CostEstimate(flops=int(2 * PEAK), bytes_accessed=1024, transcendentals=0),
        name="add_first",
    )(me, *after, *args)


def add_halves_kernel(a_ref, b_ref, keep_ref, send_ref):
    mid = keep_ref.shape[0]
    keep_ref[...] = (a_ref[:mid].astype(f32) + b_ref[:mid].astype(f32)).astype(bf16)
    send_ref[...] = (a_ref[mid:].astype(f32) + b_ref[mid:].astype(f32)).astype(bf16)


def add_halves(a, b, after):
    out = sds((a.shape[0] // 2,) + a.shape[1:], bf16)
    return simple(add_halves_kernel, "add_halves", 1, (a, b), [out] * 2, after)


def add_kernel(a_ref, b_ref, o_ref):
    o_ref[...] = (a_ref[...].astype(f32) + b_ref[...].astype(f32)).astype(o_ref.dtype)


def add(a, b, after, dtype=bf16):
    return simple(add_kernel, "add", 0.7, (a, b), [sds(a.shape, dtype)], after)[0]


def enc_attn_fwd_body(x_ref, segc_ref, segr_ref, small, w_ref, hot_ref, hid_ref, q_ref, k_ref, v_ref, mix_ref, strip_ref):
    length = x_ref.shape[1]
    blocks = length // TILE
    table = small[TABLE_ROW : TABLE_ROW + HEADS, :BUCKETS].astype(bf16)
    fill_strip(strip_ref, table, hot_ref[...], 1 - TILE)
    x = x_ref[0].astype(f32)
    n = normed(x, small[GAIN_ROW : GAIN_ROW + 1])
    q_ref[0] = nn(n, matrix(w_ref, 0)).astype(bf16)
    k_ref[0] = nn(n, matrix(w_ref, 1)).astype(bf16)
    v_ref[0] = nn(n, matrix(w_ref, 2)).astype(bf16)
    lane = lax.broadcasted_iota(jnp.int32, (length, 2 * HEAD_DIM), 1)
    same = segc_ref[0] == segr_ref[0]
    for hp in range(HEADS // 2):
        ls = slice(hp * 2 * HEAD_DIM, (hp + 1) * 2 * HEAD_DIM)
        qp, kp, vp = q_ref[0, :, ls], k_ref[0, :, ls], v_ref[0, :, ls]
        outs = []
        for sub in range(2):
            s = nt(half(lane, qp, sub), kp)
            starts = [(blocks - 1 - b) * TILE for b in range(blocks)]
            bias = [strip_ref[hp * 2 + sub, :, c : c + length] for c in starts]
            s = jnp.where(same, s + jnp.concatenate(bias, axis=0), MASKED)
            outs.append(nn(soft_rows(s).astype(bf16), vp))
        mix_ref[0, :, ls] = jnp.where(lane < HEAD_DIM, outs[0], outs[1]).astype(bf16)
    hid_ref[0] = x + nn(mix_ref[0], matrix(w_ref, 3))


def enc_attn_fwd_kernel(me_ref, x_ref, segc_ref, segr_ref, hot_ref, *refs):
    pieces, outs, (w_ref, small_ref, strip_ref) = refs[:-8], refs[-8:-3], refs[-3:]

    @pl.when(pl.program_id(0) == 0)
    def _():
        rows = pieces[0].shape[1] - SMALL_ROWS
        collect(w_ref, pieces, me_ref[0], rows)
        small = jnp.zeros(small_ref.shape, f32)
        for ref, i in spread(pieces):
            small = small + ref[i, rows:].astype(f32)
        small_ref[...] = small

    enc_attn_fwd_body(x_ref, segc_ref, segr_ref, small_ref, w_ref, hot_ref, *outs, strip_ref)


def enc_attn_fwd(me, x, segc, segr, pieces, after):
    rows, length, width = x.shape
    shards = sum(p.shape[0] for p in pieces)
    hot = offset_hot(length, True, False)
    row = lambda a: pl.BlockSpec((1,) + tuple(a.shape[1:]), lambda r: (r, 0, 0))
    outs = [sds(x.shape, f32)] + [sds(x.shape, bf16)] * 4
    full = sds((shards, 4, width // shards, width), bf16)
    small = sds((SMALL_ROWS, width), f32)
    args = [me, x, segc, segr, hot] + list(pieces)
    return call(
        enc_attn_fwd_kernel, "enc_attn_fwd", 14, args,
        [SCALAR, row(x), row(segc), row(segr)] + [whole_spec(a) for a in args[4:]],
        outs + [full, small], [row(o) for o in outs] + [whole_spec(full), whole_spec(small)],
        [pltpu.VMEM((HEADS, TILE, 2 * length), f32)], grid=rows, after=after, vmem=24,
    )


def enc_ffn_fwd_kernel(me_ref, h_ref, small_ref, *refs):
    pieces, (o_ref, w_ref, n_s, acc_s) = refs[:-4], refs[-4:]
    i = pl.program_id(0)

    @pl.when(i == 0)
    def _():
        n_s[...] = normed(h_ref[...], small_ref[GAIN_ROW + 1 : GAIN_ROW + 2])
        acc_s[...] = h_ref[...]

    collect(w_ref, pieces, me_ref[0])
    a = gelu(nn(n_s[...], matrix(w_ref, 0))).astype(bf16)
    acc_s[...] += nn(a, matrix(w_ref, 1))

    @pl.when(i == pl.num_programs(0) - 1)
    def _():
        o_ref[...] = acc_s[...].astype(bf16)


def pair_spec(a, start=0):
    return pl.BlockSpec((a.shape[0], 2) + tuple(a.shape[2:]), lambda i: (0, start + i, 0, 0))


def enc_ffn_fwd(me, h, small, pieces, after):
    tokens, width = h.shape
    full = sds((sum(p.shape[0] for p in pieces),) + pieces[0].shape[1:], bf16)
    out = sds(h.shape, bf16)
    return call(
        enc_ffn_fwd_kernel, "enc_ffn_fwd", 9, (me, h, small, *pieces),
        [SCALAR, whole_spec(h), whole_spec(small)] + [pair_spec(p) for p in pieces],
        [out, full], [whole_spec(out), pair_spec(full)],
        [pltpu.VMEM(h.shape, bf16), pltpu.VMEM(h.shape, f32)],
        grid=full.shape[1] // 2, after=after, vmem=24,
    )


def ffn_step(n, gb, w_ref, dw_ref):
    shards = w_ref.shape[0]
    wu, wd = matrix(w_ref, 0), matrix(w_ref, 1)
    a, slope = gelu_both(nn(n, wu))
    a = a.astype(bf16)
    dw_ref[:, 1] = packed(tn(a, gb), shards)
    du = (slope * nt(gb, wd)).astype(bf16)
    dw_ref[:, 0] = packed(tn(n, du), shards)
    return a, wd, nt(du, wu)


def enc_ffn_bwd_first_kernel(h_ref, small_ref, w_ref, cot_ref, gm_ref, gmem_ref, dn_ref, dw_ref, n_s, gb_s):
    rows, length, width = cot_ref.shape
    late = gm_ref.shape[1]

    @pl.when(pl.program_id(0) == 0)
    def _():
        n_s[...] = normed(h_ref[...], small_ref[GAIN_ROW + 1 : GAIN_ROW + 2])
        for r in range(rows):
            gmem_ref[r, : length - late] = cot_ref[r, : length - late].astype(f32)
            gmem_ref[r, length - late :] = cot_ref[r, length - late :].astype(f32) + gm_ref[r]
            gb_s[r * length : (r + 1) * length] = gmem_ref[r].astype(bf16)
        dn_ref[...] = jnp.zeros_like(dn_ref)

    dn_ref[...] += ffn_step(n_s[...], gb_s[...], w_ref, dw_ref)[2]


def enc_ffn_bwd_next_kernel(h_ref, small_ref, w_ref, gmem_ref, dn_ref, gh_ref, dw_ref, n_s, gb_s, dn_s):
    rows, length, width = gmem_ref.shape
    gain = small_ref[GAIN_ROW + 1 : GAIN_ROW + 2]

    @pl.when(pl.program_id(0) == 0)
    def _():
        n_s[...] = normed(h_ref[...], gain)
        gb_s[...] = gmem_ref[...].reshape(rows * length, width).astype(bf16)
        dn_s[...] = dn_ref[...]

    dn_s[...] += ffn_step(n_s[...], gb_s[...], w_ref, dw_ref)[2]

    @pl.when(pl.program_id(0) == pl.num_programs(0) - 1)
    def _():
        gh_ref[...] = gmem_ref[...].reshape(rows * length, width) + norm_back(h_ref[...], gain, dn_s[...])


def enc_ffn_bwd_first(h, small, weights, cot, late_grad, after):
    blocks = weights.shape[1] // 4
    grads = sds((weights.shape[0], 2 * blocks) + weights.shape[2:], bf16)
    gmem, dn = sds(cot.shape, f32), sds(h.shape, f32)
    args = (h, small, weights, cot, late_grad)
    specs = [whole_spec(h), whole_spec(small), pair_spec(weights), whole_spec(cot), whole_spec(late_grad)]
    return call(
        enc_ffn_bwd_first_kernel, "enc_ffn_bwd", 10, args, specs, [gmem, dn, grads],
        [whole_spec(gmem), whole_spec(dn), pair_spec(grads)],
        [pltpu.VMEM(h.shape, bf16)] * 2, grid=blocks, after=after, vmem=24,
    )


def enc_ffn_bwd_next(h, small, weights, gmem, dn, after):
    blocks = weights.shape[1] // 4
    grads = sds((weights.shape[0], 2 * blocks) + weights.shape[2:], bf16)
    gh = sds(h.shape, f32)
    args = (h, small, weights, gmem, dn)
    specs = [whole_spec(h), whole_spec(small), pair_spec(weights, blocks), whole_spec(gmem), whole_spec(dn)]
    return call(
        enc_ffn_bwd_next_kernel, "enc_ffn_bwd", 10, args, specs, [gh, grads],
        [whole_spec(gh), pair_spec(grads)],
        [pltpu.VMEM(h.shape, bf16)] * 2 + [pltpu.VMEM(h.shape, f32)], grid=blocks, after=after, vmem=24,
    )


def enc_attn_bwd_kernel(
    gh_ref, q_ref, k_ref, v_ref, segc_ref, segr_ref, w_ref, small_ref, hot_ref,
    dq_ref, dk_ref, dv_ref, dt_ref, strip_ref, acc_ref, do_s,
):
    length = q_ref.shape[1]
    blocks = length // TILE
    table = small_ref[TABLE_ROW : TABLE_ROW + HEADS, :BUCKETS].astype(bf16)
    fill_strip(strip_ref, table, hot_ref[...], -TILE)
    acc_ref[...] = jnp.zeros_like(acc_ref)
    do_s[...] = nt(gh_ref[0].astype(bf16), matrix(w_ref, 0)).astype(bf16)
    lane = lax.broadcasted_iota(jnp.int32, (length, 2 * HEAD_DIM), 1)
    same = segc_ref[0] == segr_ref[0]
    for hp in range(HEADS // 2):
        ls = slice(hp * 2 * HEAD_DIM, (hp + 1) * 2 * HEAD_DIM)
        qp, kp, vp, dop = q_ref[0, :, ls], k_ref[0, :, ls], v_ref[0, :, ls], do_s[:, ls]
        dq = dk = dv = None
        for sub in range(2):
            h = hp * 2 + sub
            qm, km, dom = half(lane, qp, sub), half(lane, kp, sub), half(lane, dop, sub)
            s = nt(kp, qm)
            starts = [(blocks - 1 - b) * TILE for b in range(blocks)]
            bias = [strip_ref[h, :, c : c + length] for c in starts]
            p = soft_columns(jnp.where(same, s + jnp.concatenate(bias, axis=0), MASKED))
            dp = nt(vp, dom)
            ds = (p * (dp - jnp.sum(dp * p, axis=0, keepdims=True))).astype(bf16)
            new = (tn(ds, km), nn(ds, qm), nn(p.astype(bf16), dom))
            dq, dk, dv = new if dq is None else (dq + new[0], dk + new[1], dv + new[2])
            wide = ds.astype(f32)
            for b, c in enumerate(starts):
                acc_ref[h, :, c : c + length] += wide[b * TILE : (b + 1) * TILE]
        dq_ref[0, :, ls] = dq.astype(bf16)
        dk_ref[0, :, ls] = dk.astype(bf16)
        dv_ref[0, :, ls] = dv.astype(bf16)
    dt_ref[...] = strip_sums(acc_ref[...], hot_ref[...])


def enc_attn_bwd(r, grad_hidden, q, k, v, segc, segr, weights, small, after):
    rows, length, width = q.shape
    shards, _, blk, _ = weights.shape
    hot = offset_hot(length, True, True)
    strip = pltpu.VMEM((HEADS, TILE, 2 * length), f32)
    args = [grad_hidden, q, k, v, segc, segr]
    specs = [pl.BlockSpec((1,) + tuple(a.shape[1:]), lambda i: (r, 0, 0)) for a in args]
    specs += [pl.BlockSpec((shards, 1, blk, width), lambda i: (0, 3, 0, 0)), whole_spec(small), whole_spec(hot)]
    args += [weights, small, hot]
    outs = [sds((1, length, width), bf16)] * 3 + [sds((HEADS, BUCKETS), f32)]
    return call(
        enc_attn_bwd_kernel, "enc_attn_bwd", 10, args, specs, outs, [whole_spec(o) for o in outs],
        [strip, strip, pltpu.VMEM((length, width), bf16)], after=after, vmem=24,
    )


def enc_weight_grads_kernel(x_ref, small_ref, mix_ref, gh_ref, td_ref, *refs):
    *parts, dw_ref = refs
    rows, length, width = x_ref.shape
    shards = dw_ref.shape[0]
    blk = width // shards
    gain = small_ref[GAIN_ROW : GAIN_ROW + 1]
    n = normed(x_ref[...].astype(f32).reshape(rows * length, width), gain)
    for w in range(3):
        total = None
        for r in range(rows):
            new = tn(n[r * length : (r + 1) * length], parts[4 * r + w][0])
            total = new if total is None else total + new
        dw_ref[:, w * blk : (w + 1) * blk] = packed(total, shards)
    dw_ref[:, 3 * blk : 4 * blk] = packed(tn(mix_ref[...], gh_ref[...].astype(bf16)), shards)
    table = sum(parts[4 * r + 3][...] for r in range(rows))
    for s in range(shards):
        dw_ref[s, 4 * blk :] = jnp.zeros((SMALL_ROWS, width), bf16)
        dw_ref[s, 4 * blk : 4 * blk + HEADS, :BUCKETS] = table.astype(bf16)
        dw_ref[s, 4 * blk : 4 * blk + HEADS, DEC_LANE : DEC_LANE + BUCKETS] = td_ref[...].astype(bf16)


def enc_weight_grads(x, small, mix, grad_hidden, dec_grad, parts, shards, after):
    width = x.shape[-1]
    grads = sds((shards, 4 * width // shards + SMALL_ROWS, width), bf16)
    args = (x, small, mix, grad_hidden, dec_grad) + tuple(a for row in parts for a in row)
    return simple(enc_weight_grads_kernel, "enc_weight_grads", 3, args, [grads], after, vmem=24)[0]


def enc_input_grad_kernel(x_ref, small_ref, gh_ref, w_ref, *refs):
    *parts, gi_ref = refs
    rows, length, width = x_ref.shape
    gain = small_ref[GAIN_ROW : GAIN_ROW + 1]
    for r in range(rows):
        dn = sum(nt(parts[4 * r + w][0], matrix(w_ref, w)) for w in range(3))
        gi_ref[r] = gh_ref[r * length : (r + 1) * length] + norm_back(x_ref[r].astype(f32), gain, dn)


def enc_input_grad(x, small, grad_hidden, weights, parts, after):
    args = (x, small, grad_hidden, weights) + tuple(a for row in parts for a in row)
    return simple(enc_input_grad_kernel, "enc_input_grad", 4, args, [sds(x.shape, f32)], after, vmem=24)[0]


def embed_rows_kernel(me_ref, embed_ref, *refs):
    pieces, (found_ref, ids_ref) = refs[:-2], refs[-2:]
    shards, tokens, _ = found_ref.shape
    own = embed_ref.shape[0]
    me = me_ref[0]
    count = len(pieces) // 2
    row = pieces[0].shape[1] - SMALL_ROWS + ID_ROW
    for core, part in ((me, pieces[:count]), (me ^ 1, pieces[count:])):
        for p, (ref, i) in enumerate(spread(part)):
            code = ref[i, row : row + 1, :].astype(f32).astype(jnp.int32)
            ids = code[:, :tokens] * 64 + code[:, tokens : 2 * tokens]
            s = shard_at(p, core, shards)
            ids_ref[s] = ids
            found_ref[s] = tn(one_hot(ids, own, me), embed_ref[...]).astype(bf16)


def one_hot(ids, own, me):
    return (lax.broadcasted_iota(jnp.int32, (own, ids.shape[1]), 0) + me * own == ids).astype(f32).astype(bf16)


def embed_rows(me, embed, pieces, tokens, after):
    shards = sum(p.shape[0] for p in pieces)
    outs = [sds((shards, tokens, embed.shape[1]), bf16), sds((shards, 1, tokens), jnp.int32)]
    args = (embed, *pieces)
    return call(
        embed_rows_kernel, "embed_rows", 2, (me,) + args, [SCALAR] + [whole_spec(a) for a in args], outs,
        [whole_spec(o) for o in outs], after=after, vmem=10,
    )


def embed_grads_kernel(me_ref, ids_ref, *refs):
    pieces, out_ref = refs[:-1], refs[-1]
    shards = ids_ref.shape[0]
    me = me_ref[0]
    count = len(pieces) // 2
    total = jnp.zeros(out_ref.shape, f32)
    for core, part in ((me, pieces[:count]), (me ^ 1, pieces[count:])):
        for p, (ref, i) in enumerate(spread(part)):
            ids = ids_ref[shard_at(p, core, shards)]
            total = total + nn(one_hot(ids, out_ref.shape[0], me), ref[i])
    out_ref[...] = total.astype(bf16)


def embed_grads(me, ids, pieces, own, after):
    out = sds((own, pieces[0].shape[-1]), bf16)
    args = (ids, *pieces)
    return call(
        embed_grads_kernel, "embed_grads", 2, (me,) + args, [SCALAR] + [whole_spec(a) for a in args], [out],
        [whole_spec(out)], after=after, vmem=10,
    )[0]


def dec_masks(rows, steps, late, last_ref, key_major):
    tokens, keys = rows * steps, rows * late
    shape = (tokens, tokens)
    i = lax.broadcasted_iota(jnp.int32, shape, 1 if key_major else 0)
    j = lax.broadcasted_iota(jnp.int32, shape, 0 if key_major else 1)
    causal = (i // steps == j // steps) & (j <= i)
    shape = (keys, tokens) if key_major else (tokens, keys)
    i = lax.broadcasted_iota(jnp.int32, shape, 1 if key_major else 0)
    j = lax.broadcasted_iota(jnp.int32, shape, 0 if key_major else 1)
    return causal, (i // steps == j // late) & (last_ref[...] == 1)


def dec_table(small_ref):
    return small_ref[TABLE_ROW : TABLE_ROW + HEADS, DEC_LANE : DEC_LANE + BUCKETS].astype(bf16)


def dec_attn_fwd_kernel(
    emb_ref, enc_ref, last_ref, small_ref, w_ref, hot_ref,
    na_ref, qkv_ref, mixa_ref, hida_ref, nb_ref, cq_ref, ckv_ref, mixb_ref, hidb_ref, strip_ref, *, rows,
):
    tokens = emb_ref.shape[0]
    keys = enc_ref.shape[0]
    causal, allowed = dec_masks(rows, tokens // rows, keys // rows, last_ref, False)
    fill_strip(strip_ref, dec_table(small_ref), hot_ref[...], 1 - tokens)
    lane = lax.broadcasted_iota(jnp.int32, (tokens, 2 * HEAD_DIM), 1)

    def attend(q_at, k_at, v_at, bias_at, mask, mix_ref):
        for hp in range(HEADS // 2):
            ls = slice(hp * 2 * HEAD_DIM, (hp + 1) * 2 * HEAD_DIM)
            qp, kp, vp = q_at(ls), k_at(ls), v_at(ls)
            outs = []
            for sub in range(2):
                s = nt(half(lane, qp, sub), kp)
                if bias_at is not None:
                    s = s + bias_at(hp * 2 + sub)
                outs.append(nn(soft_rows(jnp.where(mask, s, MASKED)).astype(bf16), vp))
            mix_ref[:, ls] = jnp.where(lane < HEAD_DIM, outs[0], outs[1]).astype(bf16)

    emb = emb_ref[...].astype(f32)
    na_ref[...] = normed(emb, small_ref[GAIN_ROW + 2 : GAIN_ROW + 3])
    for w in range(3):
        qkv_ref[w] = nn(na_ref[...], matrix(w_ref, w)).astype(bf16)
    attend(
        lambda ls: qkv_ref[0, :, ls],
        lambda ls: qkv_ref[1, :, ls],
        lambda ls: qkv_ref[2, :, ls],
        lambda h: strip_ref[h, :, :tokens],
        causal,
        mixa_ref,
    )
    hida_ref[...] = emb + nn(mixa_ref[...], matrix(w_ref, 3))
    nb_ref[...] = normed(hida_ref[...], small_ref[GAIN_ROW + 3 : GAIN_ROW + 4])
    cq_ref[...] = nn(nb_ref[...], matrix(w_ref, 4)).astype(bf16)
    for w in range(2):
        ckv_ref[w] = nn(enc_ref[...], matrix(w_ref, 5 + w)).astype(bf16)
    attend(
        lambda ls: cq_ref[:, ls],
        lambda ls: ckv_ref[0, :, ls],
        lambda ls: ckv_ref[1, :, ls],
        None,
        allowed,
        mixb_ref,
    )
    hidb_ref[...] = hida_ref[...] + nn(mixb_ref[...], matrix(w_ref, 7))


def dec_attn_fwd(emb, enc_late, last, small, pieces, me, rows, after):
    tokens, width = emb.shape
    keys = enc_late.shape[0]
    hot = dec_hot(tokens, tokens // rows, False)
    one = sds((tokens, width), bf16)
    wide = sds((tokens, width), f32)
    full = sds((sum(p.shape[0] for p in pieces),) + pieces[0].shape[1:], bf16)
    outs = [one, sds((3, tokens, width), bf16), one, wide, one, one, sds((2, keys, width), bf16), one, wide, full]
    args = (emb, enc_late, last, small, hot, *pieces)

    def body(me_ref, emb_ref, enc_ref, last_ref, small_ref, hot_ref, *refs):
        parts, kept, w_ref, strip_ref = refs[: len(pieces)], refs[len(pieces) : -2], refs[-2], refs[-1]
        collect(w_ref, parts, me_ref[0])
        dec_attn_fwd_kernel(
            emb_ref, enc_ref, last_ref, small_ref, w_ref, hot_ref, *kept, strip_ref, rows=rows
        )

    return call(
        body, "dec_attn_fwd", 7, (me,) + args, [SCALAR] + [whole_spec(a) for a in args], outs,
        [whole_spec(o) for o in outs], [pltpu.VMEM((HEADS, tokens, 2 * tokens), f32)], after=after, vmem=24,
    )


def dec_hot(tokens, steps, reverse):
    codes = np.full(2 * tokens, -1, np.int32)
    own = bucket_codes(steps, False)
    codes[tokens - steps : tokens - steps + len(own)] = own
    if reverse:
        codes = codes[::-1]
    return jnp.asarray(codes[None, :] == np.arange(BUCKETS)[:, None], bf16)


def dec_ffn_kernel(me_ref, h_ref, small_ref, cot_ref, *refs):
    pieces, (out_ref, gh_ref, dw_ref, w_s, n_s, dn_s, o_s) = refs[:-7], refs[-7:]
    i = pl.program_id(0)
    gain = small_ref[GAIN_ROW + 4 : GAIN_ROW + 5]

    @pl.when(i == 0)
    def _():
        n_s[...] = normed(h_ref[...], gain)
        dn_s[...] = jnp.zeros_like(dn_s)
        o_s[...] = h_ref[...]

    collect(w_s, pieces, me_ref[0])
    a, wd, dn = ffn_step(n_s[...], cot_ref[...], w_s, dw_ref)
    o_s[...] += nn(a, wd)
    dn_s[...] += dn

    @pl.when(i == pl.num_programs(0) - 1)
    def _():
        out_ref[...] = o_s[...].astype(bf16)
        gh_ref[...] = cot_ref[...].astype(f32) + norm_back(h_ref[...], gain, dn_s[...])


def dec_ffn(me, h, small, cot, pieces, after):
    grads = sds((sum(p.shape[0] for p in pieces),) + pieces[0].shape[1:], bf16)
    outs = [sds(h.shape, bf16), sds(h.shape, f32), grads]
    return call(
        dec_ffn_kernel, "dec_ffn", 8, (me, h, small, cot, *pieces),
        [SCALAR, whole_spec(h), whole_spec(small), whole_spec(cot)] + [pair_spec(p) for p in pieces],
        outs, [whole_spec(outs[0]), whole_spec(outs[1]), pair_spec(grads)],
        [
            pltpu.VMEM((grads.shape[0], 2) + grads.shape[2:], bf16),
            pltpu.VMEM(h.shape, bf16),
            pltpu.VMEM(h.shape, f32),
            pltpu.VMEM(h.shape, f32),
        ],
        grid=grads.shape[1] // 2, after=after, vmem=16,
    )


def attend_back(q_at, k_at, v_at, do, bias_at, mask, take_score, dq_s, dk_s, dv_s):
    for hp in range(HEADS // 2):
        ls = slice(hp * 2 * HEAD_DIM, (hp + 1) * 2 * HEAD_DIM)
        qp, kp, vp, dop = q_at(ls), k_at(ls), v_at(ls), do[:, ls]
        lane = lax.broadcasted_iota(jnp.int32, qp.shape, 1)
        lanek = lax.broadcasted_iota(jnp.int32, kp.shape, 1)
        dq = dk = dv = None
        for sub in range(2):
            qm, km, dom = half(lane, qp, sub), half(lanek, kp, sub), half(lane, dop, sub)
            s = nt(kp, qm)
            if bias_at is not None:
                s = s + bias_at(hp * 2 + sub)
            p = soft_columns(jnp.where(mask, s, MASKED))
            dp = nt(vp, dom)
            ds = (p * (dp - jnp.sum(dp * p, axis=0, keepdims=True))).astype(bf16)
            new = (tn(ds, km), nn(ds, qm), nn(p.astype(bf16), dom))
            dq, dk, dv = new if dq is None else (dq + new[0], dk + new[1], dv + new[2])
            if take_score is not None:
                take_score(hp * 2 + sub, ds)
        dq_s[:, ls] = dq.astype(bf16)
        dk_s[:, ls] = dk.astype(bf16)
        dv_s[:, ls] = dv.astype(bf16)


def dec_cross_bwd_kernel(
    gb_ref, enc_ref, last_ref, small_ref, w_ref, hida_ref, nb_ref, cq_ref, ckv_ref, mixb_ref,
    gm_ref, ga_ref, dw_ref, dq_s, dk_s, dv_s, *, rows,
):
    tokens = gb_ref.shape[0]
    keys = enc_ref.shape[0]
    shards = dw_ref.shape[0]
    _, allowed = dec_masks(rows, tokens // rows, keys // rows, last_ref, True)
    grad_b = gb_ref[...]
    branch = grad_b.astype(bf16)
    dw_ref[:, 3] = packed(tn(mixb_ref[...], branch), shards)
    do = nt(branch, matrix(w_ref, 7)).astype(bf16)
    attend_back(
        lambda ls: cq_ref[:, ls],
        lambda ls: ckv_ref[0, :, ls],
        lambda ls: ckv_ref[1, :, ls],
        do,
        None,
        allowed,
        None,
        dq_s,
        dk_s,
        dv_s,
    )
    gm_ref[...] = nt(dk_s[...], matrix(w_ref, 5)) + nt(dv_s[...], matrix(w_ref, 6))
    dw_ref[:, 0] = packed(tn(nb_ref[...], dq_s[...]), shards)
    dw_ref[:, 1] = packed(tn(enc_ref[...], dk_s[...]), shards)
    dw_ref[:, 2] = packed(tn(enc_ref[...], dv_s[...]), shards)
    gain = small_ref[GAIN_ROW + 3 : GAIN_ROW + 4]
    ga_ref[...] = grad_b + norm_back(hida_ref[...], gain, nt(dq_s[...], matrix(w_ref, 4)))


def dec_cross_bwd(grad_b, enc_late, last, small, weights, kept, rows, after):
    tokens, width = grad_b.shape
    keys = enc_late.shape[0]
    _, _, _, hida, nb, cq, ckv, mixb, _ = kept
    shards, _, blk, _ = weights.shape
    outs = [sds((keys, width), f32), sds((tokens, width), f32), sds((shards, 4, blk, width), bf16)]
    args = (grad_b, enc_late, last, small, weights, hida, nb, cq, ckv, mixb)
    return simple(
        functools.partial(dec_cross_bwd_kernel, rows=rows), "dec_cross_bwd", 6, args, outs, after,
        [pltpu.VMEM((tokens, width), bf16), pltpu.VMEM((keys, width), bf16), pltpu.VMEM((keys, width), bf16)], vmem=24,
    )


def dec_self_bwd_kernel(
    ga_ref, emb_ref, small_ref, w_ref, hot_ref, na_ref, qkv_ref, mixa_ref,
    gr_ref, dt_ref, dw_ref, strip_ref, acc_ref, dq_s, dk_s, dv_s, *, rows,
):
    tokens = emb_ref.shape[0]
    shards = dw_ref.shape[0]
    steps = tokens // rows
    i = lax.broadcasted_iota(jnp.int32, (tokens, tokens), 1)
    j = lax.broadcasted_iota(jnp.int32, (tokens, tokens), 0)
    causal = (i // steps == j // steps) & (j <= i)
    fill_strip(strip_ref, dec_table(small_ref), hot_ref[...], -tokens)
    grad_a = ga_ref[...]
    branch = grad_a.astype(bf16)
    dw_ref[:, 3] = packed(tn(mixa_ref[...], branch), shards)
    do = nt(branch, matrix(w_ref, 3)).astype(bf16)
    acc_ref[...] = jnp.zeros_like(acc_ref)

    def take_score(h, ds):
        acc_ref[h, :, :tokens] = ds.astype(f32)

    attend_back(
        lambda ls: qkv_ref[0, :, ls],
        lambda ls: qkv_ref[1, :, ls],
        lambda ls: qkv_ref[2, :, ls],
        do,
        lambda h: strip_ref[h, :, :tokens],
        causal,
        take_score,
        dq_s,
        dk_s,
        dv_s,
    )
    parts = (dq_s[...], dk_s[...], dv_s[...])
    dn = nt(parts[0], matrix(w_ref, 0)) + nt(parts[1], matrix(w_ref, 1)) + nt(parts[2], matrix(w_ref, 2))
    for w in range(3):
        dw_ref[:, w] = packed(tn(na_ref[...], parts[w]), shards)
    gain = small_ref[GAIN_ROW + 2 : GAIN_ROW + 3]
    gr_ref[0] = (grad_a + norm_back(emb_ref[...].astype(f32), gain, dn)).astype(bf16)
    dt_ref[...] = strip_sums(acc_ref[...], hot_ref[...])


def dec_self_bwd(grad_a, emb, small, weights, kept, rows, after):
    tokens, width = emb.shape
    shards, _, blk, _ = weights.shape
    na, qkv, mixa = kept[:3]
    hot = dec_hot(tokens, tokens // rows, True)
    outs = [sds((1, tokens, width), bf16), sds((HEADS, BUCKETS), f32), sds((shards, 4, blk, width), bf16)]
    args = (grad_a, emb, small, weights, hot, na, qkv, mixa)
    strip = pltpu.VMEM((HEADS, tokens, 2 * tokens), f32)
    return simple(
        functools.partial(dec_self_bwd_kernel, rows=rows), "dec_self_bwd", 4, args, outs, after,
        [strip, strip] + [pltpu.VMEM((tokens, width), bf16)] * 3, vmem=24,
    )


def exchange(value, shards, even_bit, odd_bit):
    pairs = [(i, i ^ (1 << (odd_bit if i & 1 else even_bit))) for i in range(shards)]
    return lax.ppermute(value, "fsdp", pairs)


def swap_cores(value, shards):
    return exchange(value, shards, 0, 0)


def round_of(value, j, shards):
    upper = shards.bit_length() - 2
    return exchange(value, shards, 1 + j, upper - j)


class Gather:
    def __init__(self, block, shards):
        self.shards = shards
        self.upper = shards.bit_length() - 2
        self.block = block
        if self.upper == 2:
            self.one, self.two = round_of(block, 0, shards), round_of(block, 1, shards)
            self.swapped = [swap_cores(block, shards)]
        else:
            self.one = round_of(block, self.upper - 1, shards)

    def forward(self, after):
        if self.upper == 2:
            passed = gate(self.one, after)
            self.far = round_of(passed, 1, self.shards)
            self.pieces = [self.block, self.two, passed, self.far]
            self.swapped += [swap_cores(p, self.shards) for p in self.pieces[1:3]]
            return passed
        held = join(self.block, self.one, after)
        for j in reversed(range(self.upper - 1)):
            held = join(held, round_of(held, j, self.shards), ())
        self.pieces = [held]
        self.swapped = []
        return held

    def finish(self):
        return self.pieces + self.swapped + [swap_cores(self.pieces[-1], self.shards)]


class Sum:
    def __init__(self, me, groups, short=False):
        self.me, self.shards, self.short, self.line = me, groups[0].shape[0], short, None
        self.groups = [(g, swap_cores(g, self.shards)) for g in groups]
        self.upper = self.shards.bit_length() - 2
        self.size = lax.axis_size("dp")
        self.step = -1

    def include(self, group):
        self.groups.append((group, swap_cores(group, self.shards)))

    def done(self):
        return self.line is not None and self.line.done()

    def advance(self, after):
        if self.done():
            return after[0]
        if self.step < 0:
            self.keep, send = add_first(self.me, self.groups, after)
        elif self.step < self.upper - 1:
            self.keep, send = add_halves(self.keep, self.flight, after)
        else:
            if self.step == self.upper - 1:
                self.keep = add(self.keep, self.flight, after)[0]
                self.line = Line(self.keep, self.size, self.short)
            else:
                self.keep = self.line.advance(after)
            self.step += 1
            return self.keep
        self.step += 1
        self.flight = round_of(send, self.step, self.shards)
        return self.keep


class Line:
    def __init__(self, value, size, short=False):
        self.value, self.size = value, size
        self.short = short or size != 4
        self.step = 0
        self.start()

    def start(self):
        if self.short:
            pairs = [(i, i ^ (1 << self.step)) for i in range(self.size)]
        else:
            pairs = ([(0, 1), (3, 2)], [(1, 2), (2, 1)], [(1, 0), (2, 3)])[self.step]
        self.flight = lax.ppermute(self.value, "dp", pairs)

    def rounds(self):
        return self.size.bit_length() - 1 if self.short else 3

    def done(self):
        return self.step >= self.rounds()

    def advance(self, after):
        if self.done():
            return after[0]
        if self.short or self.step < 2:
            self.value = add(self.value, self.flight, after)
        else:
            inner = ((lax.axis_index("dp") + 1) // 2 % 2).astype(jnp.int32).reshape(1)
            self.value = pick(inner, self.value, self.flight, after)
        self.step += 1
        if not self.done():
            self.start()
        return self.value


def pick_kernel(inner_ref, a_ref, b_ref, o_ref):
    @pl.when(inner_ref[0] == 1)
    def _():
        o_ref[...] = a_ref[...]

    @pl.when(inner_ref[0] == 0)
    def _():
        o_ref[...] = b_ref[...]


def pick(inner, a, b, after):
    size = 1 + 6 * np.prod(a.shape) * a.dtype.itemsize / 2**20
    return call(
        pick_kernel, "pick", 0.7, (inner, a, b), [SCALAR, whole_spec(a), whole_spec(b)], [a], [whole_spec(a)],
        after=after, vmem=size,
    )[0]


def unpack_ffn_kernel(sum_ref, up_ref, down_ref, *, shards):
    blocks = sum_ref.shape[0] // 2
    blk = up_ref.shape[0]
    for b in range(blocks):
        up = sum_ref[2 * b].astype(f32)
        for c in range(shards):
            up_ref[:, (c * blocks + b) * blk : (c * blocks + b + 1) * blk] = up[:, c * blk : (c + 1) * blk]
        down_ref[b * blk : (b + 1) * blk] = sum_ref[2 * b + 1].astype(f32)


def unpack_ffn(a, shards, after=()):
    count, blk, width = a.shape
    outs = [sds((blk, count // 2 * width), f32), sds((count // 2 * blk, width), f32)]
    return simple(functools.partial(unpack_ffn_kernel, shards=shards), "unpack_ffn", 1.5, (a,), outs, after)


def on_device(
    enc_input,
    segments,
    targets,
    enc_cot,
    dec_cot,
    enc_gains,
    enc_attn,
    enc_table,
    enc_up,
    enc_down,
    embed,
    dec_gains,
    dec_self,
    dec_cross,
    dec_table,
    dec_up,
    dec_down,
):
    rows, length, width = enc_input.shape
    steps = targets.shape[1]
    tokens = rows * steps
    shards = lax.axis_size("fsdp")
    blk = enc_attn.shape[1]
    own = embed.shape[0]
    index = lax.axis_index("fsdp").astype(jnp.int32)
    me = index.reshape(1)
    late = min(length, SERIES_MOST)
    flat = lambda a: a.reshape(-1, width)
    segc, segr = segments[:, :, None], segments[:, None, :]

    first = pack_first(me, enc_attn, enc_gains, dec_gains, enc_table, dec_table, targets, shards)
    a = Gather(first, shards)
    b = Gather(pack_ffn(enc_up, enc_down, shards, (a.forward((a.two,)) if a.upper == 2 else a.forward(()),)), shards)
    a_pieces = a.finish()
    found, ids = embed_rows(me, embed, a_pieces, tokens, (b.block,))
    e = Sum(me, [found])
    mark = b.forward((found,))
    c = Gather(pack_attn(dec_self, dec_cross, (mark,)), shards)
    hidden, q, k, v, mix, w_attn, small = enc_attn_fwd(me, enc_input, segc, segr, a_pieces, (c.block,))
    hidden = flat(hidden)

    b_pieces = b.finish()
    mark = e.advance((hidden,))
    d = Gather(pack_ffn(dec_up, dec_down, shards, (mark,)), shards)
    enc_out, w_ffn = enc_ffn_fwd(me, hidden, small, b_pieces, (d.block,))
    mark = c.forward((e.advance((enc_out,)),))
    mark = d.forward((mark,))
    enc_out = enc_out.reshape(rows, length, width)
    enc_late = flat(enc_out[:, length - late :])
    last = (segments == segments[:, -1:])[:, length - late :].astype(jnp.int32).reshape(1, -1)
    while e.step < e.upper - 1:
        mark = e.advance((mark,))
    emb = add(e.keep, e.flight, (mark,))[0]
    kept = dec_attn_fwd(emb, enc_late, last, small, c.finish(), me, rows, ())
    kept, w_dec = kept[:-1], kept[-1]
    dec_out, grad_b, g_dffn = dec_ffn(me, kept[-1], small, flat(dec_cot), d.finish(), ())

    r1 = Sum(me, [g_dffn])
    grad_late, grad_a, g_cross = dec_cross_bwd(grad_b, enc_late, last.reshape(-1, 1), small, w_dec, kept, rows, ())
    r2 = Sum(me, [g_cross])
    grad_rows, d_dtab, g_self = dec_self_bwd(grad_a, emb, small, w_dec, kept, rows, ())
    mark = r1.advance((grad_rows,))
    r2.include(g_self)
    f = Gather(grad_rows, shards)
    grad_memory, dn, g_ffn = enc_ffn_bwd_first(
        hidden, small, w_ffn, enc_cot, grad_late.reshape(rows, late, width), (mark,)
    )
    mark = r2.advance((r1.advance((dn,)),))
    mark = f.forward((mark,))
    r3 = Sum(me, [g_ffn])
    grad_hidden, g_ffn = enc_ffn_bwd_next(hidden, small, w_ffn, grad_memory, dn, (mark,))
    mark = r2.advance((r1.advance((grad_hidden,)),))
    mark = r3.advance((mark,))
    r4 = Sum(me, [g_ffn])
    three = grad_hidden.reshape(rows, length, width)
    parts = [enc_attn_bwd(0, three, q, k, v, segc, segr, w_attn, small, (mark,))]
    mark = parts[0][3]
    for r in (r1, r2, r3, r4):
        mark = r.advance((mark,))
    g_embed = embed_grads(me, ids, f.finish(), own, (mark,))
    r5 = Line(g_embed, lax.axis_size("dp"))
    mark = g_embed
    for row in range(1, rows):
        parts.append(enc_attn_bwd(row, three, q, k, v, segc, segr, w_attn, small, (mark,)))
        mark = parts[-1][3]
    for r in (r1, r2, r3, r4, r5):
        mark = r.advance((mark,))
    g_attn = enc_weight_grads(enc_input, small, flat(mix), grad_hidden, d_dtab, parts, shards, (mark,))
    r6 = Sum(me, [g_attn], short=True)
    grad_input = enc_input_grad(enc_input, small, grad_hidden, w_attn, parts, (g_attn,))
    mark = r6.advance((grad_input,))
    while not r6.done():
        for r in (r4, r3, r2, r1, r5, r6):
            mark = r.advance((mark,))
    for r in (r1, r2, r3, r4, r5):
        while not r.done():
            mark = r.advance((mark,))
    s_dup, s_ddown = unpack_ffn(r1.keep, shards)
    s_up, s_down = unpack_ffn(jnp.concatenate([r3.keep, r4.keep], axis=0), shards)
    s_attn = r6.keep.astype(f32)
    tabs = s_attn[4 * blk :]
    per = enc_table.shape[0]
    entries = lambda lane: lax.dynamic_slice(
        tabs[:HEADS, lane : lane + BUCKETS].reshape(-1), (index * per,), (per,)
    )
    s_attn = s_attn[: 4 * blk].reshape(4, blk, width)
    s_dec = r2.keep.astype(f32)

    def gain_grad(weights, sums, gain):
        axes = (0, 2) if weights.ndim == 3 else 1
        return jnp.sum(weights.astype(f32) * sums, axis=axes) / gain.astype(f32)

    return (
        enc_out,
        dec_out.reshape(rows, steps, width),
        grad_input,
        grad_memory,
        jnp.stack([gain_grad(enc_attn[:3], s_attn[:3], enc_gains[0]), gain_grad(enc_up, s_up, enc_gains[1])]),
        s_attn,
        entries(0),
        s_up,
        s_down,
        r5.value.astype(f32),
        jnp.stack(
            [
                gain_grad(dec_self[:3], s_dec[4:7], dec_gains[0]),
                gain_grad(dec_cross[0], s_dec[0], dec_gains[1]),
                gain_grad(dec_up, s_dup, dec_gains[2]),
            ]
        ),
        s_dec[4:],
        s_dec[:4],
        entries(DEC_LANE),
        s_dup,
        s_ddown,
    )


def solution(mesh):
    placed = (
        P(("fsdp", "dp"), None, None),
        P(("fsdp", "dp"), None),
        P(("fsdp", "dp"), None),
        P(("fsdp", "dp"), None, None),
        P(("fsdp", "dp"), None, None),
        P(None, "fsdp"),
        P(None, "fsdp", None),
        P("fsdp"),
        P("fsdp", None),
        P("fsdp", None),
        P("fsdp", None),
        P(None, "fsdp"),
        P(None, "fsdp", None),
        P(None, "fsdp", None),
        P("fsdp"),
        P("fsdp", None),
        P("fsdp", None),
    )
    return jax.shard_map(
        on_device,
        mesh=mesh,
        in_specs=placed,
        out_specs=(
            P(("fsdp", "dp"), None, None),
            P(("fsdp", "dp"), None, None),
            P(("fsdp", "dp"), None, None),
            P(("fsdp", "dp"), None, None),
            P(None, "fsdp"),
            P(None, "fsdp", None),
            P("fsdp"),
            P("fsdp", None),
            P("fsdp", None),
            P("fsdp", None),
            P(None, "fsdp"),
            P(None, "fsdp", None),
            P(None, "fsdp", None),
            P("fsdp"),
            P("fsdp", None),
            P("fsdp", None),
        ),
        check_vma=False,
    )
```

time: 534 us -> 312 us (0.58)
  waiting for transfers between devices: 299 us -> 85.2 us
  starting transfers between devices: 0.37 us -> 71.9 us
  blocking collectives: 54.5 us -> 0 us
  local copies, waits for them, and re-layouts: 23.5 us -> 37.5 us
  other arithmetic: 18.6 us -> 5.13 us
  between operations: 14.3 us -> 2.64 us
  Pallas kernels: 115 us -> 105 us
    reduce_scatter x3 -> x0, waiting for transfers between devices: 155 us -> none  [the longest x2 126 us: owned(): return lax.psum_scatter(a, 'fsdp', scatter_dimension=0, tiled=False)]
    all_gather x5 -> x0, waiting for transfers between devices: 100 us -> none  [the longest x1 39.1 us: on_device(): w_dec = lax.all_gather(dec_blocks, 'fsdp', axis=0, tiled=False)]
    ppermute x0 -> x71, waiting for transfers between devices: none -> 85.2 us  [the longest x54 44.4 us: exchange(): return lax.ppermute(value, 'fsdp', pairs)]
    ppermute x0 -> x71, starting transfers between devices: none -> 71.9 us  [the longest x54 38.9 us: exchange(): return lax.ppermute(value, 'fsdp', pairs)]
    psum x1 -> x0, blocking collectives: 44 us -> none  [on_device(): g_small = lax.psum(g_small, ('fsdp', 'dp'))]
    psum x1 -> x0, waiting for transfers between devices: 43.2 us -> none  [on_device(): summed = lax.psum(summed, 'dp').astype(f32)]
    unnamed x46 -> x206, local copies, waits for them, and re-layouts: 2.49 us -> 33.7 us
    concatenate x8 -> x1, other arithmetic: 18.5 us -> 0.05 us  [on_device(): jnp.concatenate([r3.keep, r4.keep], axis=0)]
  transfers between devices with their start and end apart: 9 -> 71, of which waited for: 8 -> 19; matrix products, arithmetic and copies ran while one was open for 7% -> 2% of each run, Pallas kernels for 18% -> 31%
where the time goes in v2:
time: 312 us; the launch traced here: 308 us
  Pallas kernels  105 us (34%)
  waiting for transfers between devices  85.2 us (27%)
  starting transfers between devices  71.9 us (23%)
  local copies, waits for them, and re-layouts  37.5 us (12%)
  other arithmetic  5.13 us (2%)
    pallas_call x54, Pallas kernels, call(): pl.pallas_call(body, grid=(grid,), in_specs=[ANYWHERE] * waits + list(in_...  100 us
    ppermute x54, waiting for transfers between devices, exchange(): return lax.ppermute(value, 'fsdp', pairs)  44.4 us
    ppermute x17, waiting for transfers between devices, start(): self.flight = lax.ppermute(self.value, 'dp', pairs)  40.8 us
    ppermute x54, starting transfers between devices, exchange(): return lax.ppermute(value, 'fsdp', pairs)  38.9 us
    unnamed x206, local copies, waits for them, and re-layouts  33.7 us
    ppermute x17, starting transfers between devices, start(): self.flight = lax.ppermute(self.value, 'dp', pairs)  33 us
  transfers between devices with their start and end apart: 71, of which 19 were waited for; matrix products, arithmetic and copies ran while one was open for 2% of the time, Pallas kernels for 31%

profile of v2, /device:TPU:0, one launch (start us, length us, event | category | flops | bytes accessed | tf_op | source)
XLA Modules:
  0.0 307.7 jit_solution(11364916593773482027)
XLA Ops:
  5.1 3.0 collective-permute-start
  8.1 1.5 collective-permute-start.1
  9.6 5.5 %collective-permute-done.refs_0_.refs_4_.refs_7_ = bf16[1,272,512]{2,1,0:T(8,128)(2,1)S(1)} collective-permute-done((bf16[1,272,512]{2,1,0:T(8,128)(2,1)S(1)}, bf16[1,272,512]{2,1,0:T(8,128)(2,1)S(1)}, u32[]{:S(2)}, u32[]{:S(2)}) %collective-permute-start) | collective-permute-done | bytes 278560 | tf_op jit(solution)/shard_map/ppermute | solution.py:960
  15.1 2.5 collective-permute-start.2
  19.1 6.1 %collective-permute-done.2.refs_6_.refs_9_ = bf16[1,272,512]{2,1,0:T(8,128)(2,1)S(1)} collective-permute-done((bf16[1,272,512]{2,1,0:T(8,128)(2,1)S(1)}, bf16[1,272,512]{2,1,0:T(8,128)(2,1)S(1)}, u32[]{:S(2)}, u32[]{:S(2)}) %collective-permute-start.2) | collective-permute-done | bytes 278560 | tf_op jit(solution)/shard_map/ppermute | solution.py:960
  25.2 2.0 collective-permute-start.9
  29.0 1.4 collective-permute-start.10
  30.8 3.6 %collective-permute-done.9.refs_5_ = bf16[1,8,64,512]{3,2,1,0:T(8,128)(2,1)S(1)} collective-permute-done((bf16[1,8,64,512]{3,2,1,0:T(8,128)(2,1)S(1)}, bf16[1,8,64,512]{3,2,1,0:T(8,128)(2,1)S(1)}, u32[]{:S(2)}, u32[]{:S(2)}) %collective-permute-start.9) | collective-permute-done | bytes 524320 | tf_op jit(solution)/shard_map/ppermute | solution.py:960
  35.0 5.2 %collective-permute-done.10.refs_7_ = bf16[1,8,64,512]{3,2,1,0:T(8,128)(2,1)} collective-permute-done((bf16[1,8,64,512]{3,2,1,0:T(8,128)(2,1)}, bf16[1,8,64,512]{3,2,1,0:T(8,128)(2,1)}, u32[]{:S(2)}, u32[]{:S(2)}) %collective-permute-start.10) | collective-permute-done | bytes 524320 | tf_op jit(solution)/shard_map/ppermute | solution.py:960
  40.2 17.8 %enc_attn_fwd.1 = (f32[2,512,512]{2,1,0:T(8,128)S(1)}, bf16[2,512,512]{2,1,0:T(8,128)(2,1)S(1)}, bf16[2,512,512]{2,1,0:T(8,128)(2,1)S(1)}, bf16[2,512,512]{2,1,0...) custom-call(bf16[1,8,64,512]{3,2,1,0:T(8,128)(2,1)S(1)} %pack_attn.1, ...), custom_call_target="tpu_custom_call" | custom-call | flops 16099999744 | bytes 1024 | tf_op jit(solution)/shard_map/enc_attn_fwd/pallas_call | solution.py:161
  60.9 2.0 collective-permute-start.19
  63.9 1.1 collective-permute-start.17
  65.0 9.2 %enc_ffn_fwd.1 = (bf16[1024,512]{1,0:T(8,128)(2,1)}, bf16[8,8,64,512]{3,2,1,0:T(8,128)(2,1)S(1)}) custom-call(bf16[1,8,64,512]{3,2,1,0:T(8,128)(2,1)S(1)} %pack_ffn.3.refs_0_.refs_4_, s32[1]{0:T(128)} %bitcast.refs_0_.refs_1_, f32[1024,512]{1,0:T(8,128)S(1)} %bitcast.67, f32[16,512]{1,0:T(8,128)S(1)} %get-tuple-element.90.refs_3_.refs_4_.refs_2_.refs_8_, ...), custom_call_target="tpu_custom_call" | custom-call | flops 10350000128 | bytes 1024 | tf_op jit(solution)/shard_map/enc_ffn_fwd/pallas_call | solution.py:161
  74.3 2.1 copy-done.82
  76.3 1.2 copy-done.3
  77.7 1.5 collective-permute-start.20
  79.8 2.8 collective-permute-done.17.refs_1_
  82.6 3.2 %collective-permute-start.25 = (bf16[1,8,64,512]{3,2,1,0:T(8,128)(2,1)S(1)}, bf16[1,8,64,512]{3,2,1,0:T(8,128)(2,1)S(1)}, u32[]{:S(2)}, u32[]{:S(2)}) collective-permute-start(bf16[1,8,64,512]{3,2,1,0:T(8,128)(2,1)S(1)} %pack_ffn.3.refs_0_.refs_4_), channel_id=1, source_target_pairs={{0,16},{4,12},{8,24},{12,4},{16,0},{20,28},{24,8},{28,20},{1,17},{... | collective-permute-start | bytes 1572872 | tf_op jit(solution)/shard_map/ppermute | solution.py:960
  85.9 2.4 collective-permute-done.18.refs_2_
  88.3 1.6 collective-permute-start.26
  90.9 3.1 collective-permute-done.25.refs_5_
  94.5 5.1 %collective-permute-done.26.refs_7_ = bf16[1,8,64,512]{3,2,1,0:T(8,128)(2,1)S(1)} collective-permute-done((bf16[1,8,64,512]{3,2,1,0:T(8,128)(2,1)S(1)}, bf16[1,8,64,512]{3,2,1,0:T(8,128)(2,1)S(1)}, u32[]{:S(2)}, u32[]{:S(2)}) %collective-permute-start.26) | collective-permute-done | bytes 524320 | tf_op jit(solution)/shard_map/ppermute | solution.py:960
  99.7 6.9 %dec_attn_fwd.1 = (bf16[128,512]{1,0:T(8,128)(2,1)S(1)}, bf16[3,128,512]{2,1,0:T(8,128)(2,1)S(1)}, bf16[128,512]{1,0:T(8,128)(2,1)S(1)}, f32[128,512]{1,0:T(8,12...) custom-call(s32[1]{0:T(128)} %bitcast.refs_0_.refs_1_, ...), custom_call_target="tpu_custom_call" | custom-call | flops 8049999872 | bytes 1024 | tf_op jit(solution)/shard_map/dec_attn_fwd/pallas_call | solution.py:161
  106.7 6.5 %dec_ffn.1 = (bf16[128,512]{1,0:T(8,128)(2,1)}, f32[128,512]{1,0:T(8,128)S(1)}, bf16[8,8,64,512]{3,2,1,0:T(8,128)(2,1)}) custom-call(s32[1]{0:T(128)} %bitcast.refs_0_.refs_1_, f32[128,512]{1,0:T(8,128)S(1)} %get-tuple-element.95.refs_1_, f32[16,512]{1,0:T(8,128)S(1)} %get-tuple-element.90.refs_3_.refs_4_.refs_2_.refs_8_, bf16[128,512]{1,0:T(8,128)(2,1)S(1)} %bitcast.63, ...), custom_call_target="tpu_custom_call" | custom-call | flops 9200000000 | bytes 1024 | tf_op jit(solution)/shard_map/dec_ffn/pallas_call | solution.py:161
  114.5 2.2 copy-done.77
  121.3 4.9 %dec_cross_bwd.1 = (f32[512,512]{1,0:T(8,128)S(1)}, f32[128,512]{1,0:T(8,128)S(1)}, bf16[8,4,64,512]{3,2,1,0:T(8,128)(2,1)S(1)}) custom-call(f32[128,512]{1,0:T(8,128)S(1)} %copy-done.93, bf16[512,512]{1,0:T(8,128)(2,1)S(1)} %bitcast.45, s32[512,1]{1,0:T(8,128)S(1)} %bitcast.48, f32[16,512]{1,0:T(8,128)S(1)} %get-tuple-element.90.refs_3_.refs_4_.refs_2_.refs_8_, ...), custom_call_target="tpu_custom_call" | custom-call | flops 6899999744 | bytes 1024 | tf_op jit(solution)/shard_map/dec_cross_bwd/pallas_call | solution.py:161
  126.4 2.8 dec_self_bwd.1
  129.7 2.6 add_first.7
  134.1 8.7 %enc_ffn_bwd.2 = (f32[2,512,512]{2,1,0:T(8,128)}, f32[1024,512]{1,0:T(8,128)S(1)}, bf16[8,4,64,512]{3,2,1,0:T(8,128)(2,1)S(1)}) custom-call(bf16[2,8,64,512]{3,2,1,0:T(8,128)(2,1)S(1)} %get-tuple-element.110.refs_0_.refs_1_, f32[1024,512]{1,0:T(8,128)S(1)} %bitcast.68, f32[16,512]{1,0:T(8,128)S(1)} %get-tuple-element.90.refs_3_.refs_4_.refs_2_.refs_8_, ...), custom_call_target="tpu_custom_call" | custom-call | flops 11500000256 | bytes 1024 | tf_op jit(solution)/shard_map/enc_ffn_bwd/pallas_call | solution.py:161
  143.7 3.4 %collective-permute-done.32.refs_2_ = bf16[2,8,64,512]{3,2,1,0:T(8,128)(2,1)S(1)} collective-permute-done((bf16[2,8,64,512]{3,2,1,0:T(8,128)(2,1)S(1)}, bf16[2,8,64,512]{3,2,1,0:T(8,128)(2,1)S(1)}, u32[]{:S(2)}, u32[]{:S(2)}) %collective-permute-start.32) | collective-permute-done | bytes 1048608 | tf_op jit(solution)/shard_map/ppermute | solution.py:960
  147.4 1.7 collective-permute-start.36
  151.2 8.8 %enc_ffn_bwd.3 = (f32[1024,512]{1,0:T(8,128)S(1)}, bf16[8,4,64,512]{3,2,1,0:T(8,128)(2,1)S(1)}) custom-call(bf16[1,128,512]{2,1,0:T(8,128)(2,1)S(1)} %gate.9.refs_0_.refs_5_, f32[1024,512]{1,0:T(8,128)S(1)} %bitcast.69, f32[16,512]{1,0:T(8,128)S(1)} %get-tuple-element.90.refs_3_.refs_4_.refs_2_.refs_8_, bf16[8,8,64,512]{3,2,1,0:T(8,128)(2,1)S(1)} %copy-done.83, ...), custom_call_target="tpu_custom_call" | custom-call | flops 11500000256 | bytes 1024 | tf_op jit(solution)/shard_map/enc_ffn_bwd/pallas_call | solution.py:161
  160.6 1.6 collective-permute-done.36.refs_2_
  162.3 3.6 %collective-permute-start.39 = (bf16[8,64,512]{2,1,0:T(8,128)(2,1)S(1)}, bf16[8,64,512]{2,1,0:T(8,128)(2,1)S(1)}, u32[]{:S(2)}, u32[]{:S(2)}) collective-permute-start(bf16[8,64,512]{2,1,0:T(8,128)(2,1)S(1)} %bitcast.41), channel_id=1, source_target_pairs={{0,1},{3,2},{4,5},{7,6},{8,9},{11,10},{12,13},{15,14},{16,17},{19,... | collective-permute-start | bytes 1572872 | tf_op jit(solution)/shard_map/ppermute | solution.py:1047
  165.9 1.7 collective-permute-done.37.refs_2_
  167.8 1.8 collective-permute-start.40
  172.2 9.9 %enc_attn_bwd.2 = (bf16[1,512,512]{2,1,0:T(8,128)(2,1)S(1)}, bf16[1,512,512]{2,1,0:T(8,128)(2,1)S(1)}, bf16[1,512,512]{2,1,0:T(8,128)(2,1)S(1)}, f32[8,32]{1,0:T(8,128)S(1)}) custom-call(bf16[2,4,64,512]{3,2,1,0:T(8,128)(2,1)S(1)} %get-tuple-element.125.refs_0_.refs_1_, f32[2,512,512]{2,1,0:T(8,128)S(1)} %bitcast.39, bf16[2,512,512]{2,1,0:T(8,128)(2,1)S(1)} %copy-done.85, ...), custom_call_target="tpu_custom_call" | custom-call | flops 11500000256 | bytes 1024 | tf_op jit(solution)/shard_map/enc_attn_bwd/pallas_call | solution.py:161
  183.4 3.8 %collective-permute-done.44.refs_6_ = bf16[1,128,512]{2,1,0:T(8,128)(2,1)S(1)} collective-permute-done((bf16[1,128,512]{2,1,0:T(8,128)(2,1)S(1)}, bf16[1,128,512]{2,1,0:T(8,128)(2,1)S(1)}, u32[]{:S(2)}, u32[]{:S(2)}) %collective-permute-start.44) | collective-permute-done | bytes 131104 | tf_op jit(solution)/shard_map/ppermute | solution.py:960
  188.9 6.3 %collective-permute-start.50 = (bf16[8,64,512]{2,1,0:T(8,128)(2,1)S(1)}, bf16[8,64,512]{2,1,0:T(8,128)(2,1)S(1)}, u32[]{:S(2)}, u32[]{:S(2)}) collective-permute-start(bf16[8,64,512]{2,1,0:T(8,128)(2,1)S(1)} %bitcast.52), channel_id=1, source_target_pairs={{0,1},{3,2},{4,5},{7,6},{8,9},{11,10},{12,13},{15,14},{16,17},{19,... | collective-permute-start | bytes 1572872 | tf_op jit(solution)/shard_map/ppermute | solution.py:1047
  196.4 1.2 embed_grads.1.refs_0_.refs_1_
  197.6 1.5 collective-permute-start.53
  199.2 9.9 %enc_attn_bwd.3 = (bf16[1,512,512]{2,1,0:T(8,128)(2,1)S(1)}, bf16[1,512,512]{2,1,0:T(8,128)(2,1)S(1)}, bf16[1,512,512]{2,1,0:T(8,128)(2,1)S(1)}, f32[8,32]{1,0:T(8,128)S(1)}) custom-call(bf16[512,512]{1,0:T(8,128)(2,1)S(1)} %embed_grads.1.refs_0_.refs_1_, f32[2,512,512]{2,1,0:T(8,128)S(1)} %bitcast.40, bf16[2,512,512]{2,1,0:T(8,128)(2,1)S(1)} %copy-done.85, ...), custom_call_target="tpu_custom_call" | custom-call | flops 11500000256 | bytes 1024 | tf_op jit(solution)/shard_map/enc_attn_bwd/pallas_call | solution.py:161
  211.0 6.4 %collective-permute-done.53.refs_2_ = bf16[512,512]{1,0:T(8,128)(2,1)S(1)} collective-permute-done((bf16[512,512]{1,0:T(8,128)(2,1)S(1)}, bf16[512,512]{1,0:T(8,128)(2,1)S(1)}, u32[]{:S(2)}, u32[]{:S(2)}) %collective-permute-start.53) | collective-permute-done | bytes 524320 | tf_op jit(solution)/shard_map/ppermute | solution.py:1047
  217.7 2.9 enc_weight_grads.1.refs_0_.refs_2_.refs_4_
  220.7 4.4 %collective-permute-start.56 = (bf16[4,64,512]{2,1,0:T(8,128)(2,1)}, bf16[4,64,512]{2,1,0:T(8,128)(2,1)S(1)}, u32[]{:S(2)}, u32[]{:S(2)}) collective-permute-start(bf16[4,64,512]{2,1,0:T(8,128)(2,1)} %bitcast.58), channel_id=1, source_target_pairs={{0,1},{3,2},{4,5},{7,6},{8,9},{11,10},{12,13},{15,14},{16,17},{19,... | collective-permute-start | bytes 786440 | tf_op jit(solution)/shard_map/ppermute | solution.py:1047
  225.8 1.3 collective-permute-start.58
  228.0 1.6 copy-done.1
  229.6 1.6 copy-done.63
  238.2 3.4 %enc_input_grad.1.refs_1_ = f32[2,512,512]{2,1,0:T(8,128)} custom-call(bf16[8,272,512]{2,1,0:T(8,128)(2,1)S(1)} %enc_weight_grads.1.refs_0_.refs_2_.refs_4_, bf16[2,512,512]{2,1,0:T(8,128)(2,1)S(1)} %copy-done.19, f32[16,512]{1,0:T(8,128)S(1)} %copy-done.81, f32[1024,512]{1,0:T(8,128)S(1)} %copy-done.1, bf16[8,4,64,512]{3,2,1,0:T(8,128)(2,1)S(1)} %copy-done.63, ...), custom_call_target="tpu_custom_call" | custom-call | flops 4600000000 | bytes 1024 | tf_op jit(solution)/shard_map/enc_input_grad/pallas_call | solution.py:161
  242.3 1.6 copy-done.2
  243.9 1.4 add_first.11
  246.2 6.4 %collective-permute-start.61 = (bf16[4,64,512]{2,1,0:T(8,128)(2,1)S(1)}, bf16[4,64,512]{2,1,0:T(8,128)(2,1)S(1)}, u32[]{:S(2)}, u32[]{:S(2)}) collective-permute-start(bf16[4,64,512]{2,1,0:T(8,128)(2,1)S(1)} %bitcast.60), channel_id=1, source_target_pairs={{0,1},{3,2},{4,5},{7,6},{8,9},{11,10},{12,13},{15,14},{16,17},{19,... | collective-permute-start | bytes 786440 | tf_op jit(solution)/shard_map/ppermute | solution.py:1047
  253.6 1.3 collective-permute-start.63
  255.0 1.1 unpack_ffn.3
  256.2 1.4 collective-permute-start.64
  259.9 1.4 collective-permute-start.67
  261.3 9.0 %collective-permute-done.63.refs_3_ = bf16[8,64,512]{2,1,0:T(8,128)(2,1)S(1)} collective-permute-done((bf16[8,64,512]{2,1,0:T(8,128)(2,1)S(1)}, bf16[8,64,512]{2,1,0:T(8,128)(2,1)S(1)}, u32[]{:S(2)}, u32[]{:S(2)}) %collective-permute-start.63) | collective-permute-done | bytes 524320 | tf_op jit(solution)/shard_map/ppermute | solution.py:1047
  271.6 9.9 %collective-permute-done.64.refs_3_ = bf16[512,512]{1,0:T(8,128)(2,1)S(1)} collective-permute-done((bf16[512,512]{1,0:T(8,128)(2,1)S(1)}, bf16[512,512]{1,0:T(8,128)(2,1)S(1)}, u32[]{:S(2)}, u32[]{:S(2)}) %collective-permute-start.64) | collective-permute-done | bytes 524320 | tf_op jit(solution)/shard_map/ppermute | solution.py:1047
  284.1 1.3 collective-permute-start.69
  286.0 1.2 collective-permute-done.67.refs_3_
  287.2 6.0 %collective-permute-done.68.refs_2_ = bf16[272,512]{1,0:T(8,128)(2,1)S(1)} collective-permute-done((bf16[272,512]{1,0:T(8,128)(2,1)S(1)}, bf16[272,512]{1,0:T(8,128)(2,1)S(1)}, u32[]{:S(2)}, u32[]{:S(2)}) %collective-permute-start.68) | collective-permute-done | bytes 278560 | tf_op jit(solution)/shard_map/ppermute | solution.py:1047
  293.8 5.0 %collective-permute-done.69.refs_3_ = bf16[4,64,512]{2,1,0:T(8,128)(2,1)S(1)} collective-permute-done((bf16[4,64,512]{2,1,0:T(8,128)(2,1)S(1)}, bf16[4,64,512]{2,1,0:T(8,128)(2,1)S(1)}, u32[]{:S(2)}, u32[]{:S(2)}) %collective-permute-start.69) | collective-permute-done | bytes 262176 | tf_op jit(solution)/shard_map/ppermute | solution.py:1047
  300.0 1.2 multiply_reduce_fusion.1
  301.2 3.1 collective-permute-done.70.refs_2_
  (369 shorter events, 58.1 us)
Async XLA Ops:
  5.1 10.0 %collective-permute-start = (bf16[1,272,512]{2,1,0:T(8,128)(2,1)S(1)}, bf16[1,272,512]{2,1,0:T(8,128)(2,1)S(1)}, u32[]{:S(2)}, u32[]{:S(2)}) collective-permute-start(bf16[1,272,512]{2,1,0:T(8,128)(2,1)S(1)} %pack_first.1.refs_3_.refs_6_), channel_id=1, source_target_pairs={{0,16},{4,12},{8,24},{12,4},{16,0},{20,28},{24,8},{28,20},{1,17},{... | collective-permute-start | bytes 835592 | tf_op jit(solution)/shard_map/ppermute | solution.py:960
  15.1 10.0 %collective-permute-start.2 = (bf16[1,272,512]{2,1,0:T(8,128)(2,1)S(1)}, bf16[1,272,512]{2,1,0:T(8,128)(2,1)S(1)}, u32[]{:S(2)}, u32[]{:S(2)}) collective-permute-start(bf16[1,272,512]{2,1,0:T(8,128)(2,1)S(1)} %gate.5.refs_0_.refs_5_.refs_8_), channel_id=1, source_target_pairs={{0,16},{4,12},{8,24},{12,4},{16,0},{20,28},{24,8},{28,20},{1,17},{... | collective-permute-start | bytes 835592 | tf_op jit(solution)/shard_map/ppermute | solution.py:960
  17.8 10.3 %collective-permute-start.7 = (bf16[1,8,64,512]{3,2,1,0:T(8,128)(2,1)S(1)}, bf16[1,8,64,512]{3,2,1,0:T(8,128)(2,1)S(1)}, u32[]{:S(2)}, u32[]{:S(2)}) collective-permute-start(bf16[1,8,64,512]{3,2,1,0:T(8,128)(2,1)S(1)} %pack_ffn.2.refs_0_.refs_4_), channel_id=1, source_target_pairs={{0,8},{4,20},{8,0},{12,28},{16,24},{20,4},{24,16},{28,12},{1,9},{5... | collective-permute-start | bytes 1572872 | tf_op jit(solution)/shard_map/ppermute | solution.py:960
  18.6 8.7 %collective-permute-start.5 = (bf16[1,272,512]{2,1,0:T(8,128)(2,1)S(1)}, bf16[1,272,512]{2,1,0:T(8,128)(2,1)S(1)}, u32[]{:S(2)}, u32[]{:S(2)}) collective-permute-start(bf16[1,272,512]{2,1,0:T(8,128)(2,1)S(1)} %gate.5.refs_0_.refs_5_.refs_8_), channel_id=1, source_target_pairs={{0,4},{4,0},{8,12},{12,8},{16,20},{20,16},{24,28},{28,24},{1,5},{5... | collective-permute-start | bytes 835592 | tf_op jit(solution)/shard_map/ppermute | solution.py:960
  19.1 8.2 %collective-permute-start.4 = (bf16[1,272,512]{2,1,0:T(8,128)(2,1)S(1)}, bf16[1,272,512]{2,1,0:T(8,128)(2,1)S(1)}, u32[]{:S(2)}, u32[]{:S(2)}) collective-permute-start(bf16[1,272,512]{2,1,0:T(8,128)(2,1)S(1)} %collective-permute-done.refs_0_.refs_4_.refs_7_), channel_id=1, source_target_pairs={{0,4},{4,0},{8,12},{12,8},{16,20},{20,16},{24,28},{28,24},{1,5},{5... | collective-permute-start | bytes 835592 | tf_op jit(solution)/shard_map/ppermute | solution.py:960
  25.2 9.2 %collective-permute-start.9 = (bf16[1,8,64,512]{3,2,1,0:T(8,128)(2,1)S(1)}, bf16[1,8,64,512]{3,2,1,0:T(8,128)(2,1)S(1)}, u32[]{:S(2)}, u32[]{:S(2)}) collective-permute-start(bf16[1,8,64,512]{3,2,1,0:T(8,128)(2,1)S(1)} %pack_ffn.2.refs_0_.refs_4_), channel_id=1, source_target_pairs={{0,16},{4,12},{8,24},{12,4},{16,0},{20,28},{24,8},{28,20},{1,17},{... | collective-permute-start | bytes 1572872 | tf_op jit(solution)/shard_map/ppermute | solution.py:960
  29.0 11.2 %collective-permute-start.10 = (bf16[1,8,64,512]{3,2,1,0:T(8,128)(2,1)}, bf16[1,8,64,512]{3,2,1,0:T(8,128)(2,1)}, u32[]{:S(2)}, u32[]{:S(2)}) collective-permute-start(bf16[1,8,64,512]{3,2,1,0:T(8,128)(2,1)} %gate.6.refs_0_.refs_6_), channel_id=1, source_target_pairs={{0,16},{4,12},{8,24},{12,4},{16,0},{20,28},{24,8},{28,20},{1,17},{... | collective-permute-start | bytes 1572872 | tf_op jit(solution)/shard_map/ppermute | solution.py:960
  30.8 30.1 %collective-permute-start.11 = (bf16[1,8,64,512]{3,2,1,0:T(8,128)(2,1)S(1)}, bf16[1,8,64,512]{3,2,1,0:T(8,128)(2,1)S(1)}, u32[]{:S(2)}, u32[]{:S(2)}) collective-permute-start(bf16[1,8,64,512]{3,2,1,0:T(8,128)(2,1)S(1)} %pack_ffn.2.refs_0_.refs_4_), channel_id=1, source_target_pairs={{0,4},{4,0},{8,12},{12,8},{16,20},{20,16},{24,28},{28,24},{1,5},{5... | collective-permute-start | bytes 1572872 | tf_op jit(solution)/shard_map/ppermute | solution.py:960
  34.4 28.5 %collective-permute-start.12 = (bf16[1,8,64,512]{3,2,1,0:T(8,128)(2,1)S(1)}, bf16[1,8,64,512]{3,2,1,0:T(8,128)(2,1)S(1)}, u32[]{:S(2)}, u32[]{:S(2)}) collective-permute-start(bf16[1,8,64,512]{3,2,1,0:T(8,128)(2,1)S(1)} %collective-permute-done.9.refs_5_), channel_id=1, source_target_pairs={{0,4},{4,0},{8,12},{12,8},{16,20},{20,16},{24,28},{28,24},{1,5},{5... | collective-permute-start | bytes 1572872 | tf_op jit(solution)/shard_map/ppermute | solution.py:960
  34.4 23.7 %collective-permute-start.8 = (bf16[8,128,512]{2,1,0:T(8,128)(2,1)S(1)}, bf16[8,128,512]{2,1,0:T(8,128)(2,1)S(1)}, u32[]{:S(2)}, u32[]{:S(2)}) collective-permute-start(bf16[8,128,512]{2,1,0:T(8,128)(2,1)S(1)} %get-tuple-element.87.refs_0_.refs_2_.refs_4_), channel_id=1, source_target_pairs={{0,4},{4,0},{8,12},{12,8},{16,20},{20,16},{24,28},{28,24},{1,5},{5... | collective-permute-start | bytes 3145736 | tf_op jit(solution)/shard_map/ppermute | solution.py:960
  35.0 28.0 %collective-permute-start.13 = (bf16[1,8,64,512]{3,2,1,0:T(8,128)(2,1)}, bf16[1,8,64,512]{3,2,1,0:T(8,128)(2,1)S(1)}, u32[]{:S(2)}, u32[]{:S(2)}) collective-permute-start(bf16[1,8,64,512]{3,2,1,0:T(8,128)(2,1)} %gate.6.refs_0_.refs_6_), channel_id=1, source_target_pairs={{0,4},{4,0},{8,12},{12,8},{16,20},{20,16},{24,28},{28,24},{1,5},{5... | collective-permute-start | bytes 1572872 | tf_op jit(solution)/shard_map/ppermute | solution.py:960
  40.2 23.7 %collective-permute-start.14 = (bf16[1,8,64,512]{3,2,1,0:T(8,128)(2,1)}, bf16[1,8,64,512]{3,2,1,0:T(8,128)(2,1)S(1)}, u32[]{:S(2)}, u32[]{:S(2)}) collective-permute-start(bf16[1,8,64,512]{3,2,1,0:T(8,128)(2,1)} %collective-permute-done.10.refs_7_), channel_id=1, source_target_pairs={{0,4},{4,0},{8,12},{12,8},{16,20},{20,16},{24,28},{28,24},{1,5},{5... | collective-permute-start | bytes 1572872 | tf_op jit(solution)/shard_map/ppermute | solution.py:960
  58.1 19.5 %collective-permute-start.16 = (bf16[1,8,64,512]{3,2,1,0:T(8,128)(2,1)S(1)}, bf16[1,8,64,512]{3,2,1,0:T(8,128)(2,1)S(1)}, u32[]{:S(2)}, u32[]{:S(2)}) collective-permute-start(bf16[1,8,64,512]{3,2,1,0:T(8,128)(2,1)S(1)} %pack_attn.1.refs_0_.refs_6_), channel_id=1, source_target_pairs={{0,8},{4,20},{8,0},{12,28},{16,24},{20,4},{24,16},{28,12},{1,9},{5... | collective-permute-start | bytes 1572872 | tf_op jit(solution)/shard_map/ppermute | solution.py:960
  60.9 18.9 %collective-permute-start.19 = (bf16[1,8,64,512]{3,2,1,0:T(8,128)(2,1)S(1)}, bf16[1,8,64,512]{3,2,1,0:T(8,128)(2,1)S(1)}, u32[]{:S(2)}, u32[]{:S(2)}) collective-permute-start(bf16[1,8,64,512]{3,2,1,0:T(8,128)(2,1)S(1)} %pack_attn.1.refs_0_.refs_6_), channel_id=1, source_target_pairs={{0,16},{4,12},{8,24},{12,4},{16,0},{20,28},{24,8},{28,20},{1,17},{... | collective-permute-start | bytes 1572872 | tf_op jit(solution)/shard_map/ppermute | solution.py:960
  62.9 22.9 %collective-permute-start.21 = (bf16[1,8,64,512]{3,2,1,0:T(8,128)(2,1)S(1)}, bf16[1,8,64,512]{3,2,1,0:T(8,128)(2,1)S(1)}, u32[]{:S(2)}, u32[]{:S(2)}) collective-permute-start(bf16[1,8,64,512]{3,2,1,0:T(8,128)(2,1)S(1)} %pack_attn.1.refs_0_.refs_6_), channel_id=1, source_target_pairs={{0,4},{4,0},{8,12},{12,8},{16,20},{20,16},{24,28},{28,24},{1,5},{5... | collective-permute-start | bytes 1572872 | tf_op jit(solution)/shard_map/ppermute | solution.py:960
  62.9 13.4 %collective-permute-start.15 = (bf16[2,128,512]{2,1,0:T(8,128)(2,1)S(1)}, bf16[2,128,512]{2,1,0:T(8,128)(2,1)S(1)}, u32[]{:S(2)}, u32[]{:S(2)}) collective-permute-start(bf16[2,128,512]{2,1,0:T(8,128)(2,1)S(1)} %get-tuple-element.92), channel_id=1, source_target_pairs={{0,8},{4,20},{8,0},{12,28},{16,24},{20,4},{24,16},{28,12},{1,9},{5... | collective-permute-start | bytes 786440 | tf_op jit(solution)/shard_map/ppermute | solution.py:960
  63.9 18.7 %collective-permute-start.17 = (bf16[1,8,64,512]{3,2,1,0:T(8,128)(2,1)S(1)}, bf16[1,8,64,512]{3,2,1,0:T(8,128)(2,1)S(1)}, u32[]{:S(2)}, u32[]{:S(2)}) collective-permute-start(bf16[1,8,64,512]{3,2,1,0:T(8,128)(2,1)S(1)} %pack_ffn.3.refs_0_.refs_4_), channel_id=1, source_target_pairs={{0,8},{4,20},{8,0},{12,28},{16,24},{20,4},{24,16},{28,12},{1,9},{5... | collective-permute-start | bytes 1572872 | tf_op jit(solution)/shard_map/ppermute | solution.py:960
  77.7 12.3 %collective-permute-start.20 = (bf16[1,8,64,512]{3,2,1,0:T(8,128)(2,1)S(1)}, bf16[1,8,64,512]{3,2,1,0:T(8,128)(2,1)S(1)}, u32[]{:S(2)}, u32[]{:S(2)}) collective-permute-start(bf16[1,8,64,512]{3,2,1,0:T(8,128)(2,1)S(1)} %gate.7.refs_0_.refs_8_), channel_id=1, source_target_pairs={{0,16},{4,12},{8,24},{12,4},{16,0},{20,28},{24,8},{28,20},{1,17},{... | collective-permute-start | bytes 1572872 | tf_op jit(solution)/shard_map/ppermute | solution.py:960
  79.2 9.1 %collective-permute-start.18 = (bf16[1,128,512]{2,1,0:T(8,128)(2,1)S(1)}, bf16[1,128,512]{2,1,0:T(8,128)(2,1)S(1)}, u32[]{:S(2)}, u32[]{:S(2)}) collective-permute-start(bf16[1,128,512]{2,1,0:T(8,128)(2,1)S(1)} %get-tuple-element.94), channel_id=1, source_target_pairs={{0,16},{4,12},{8,24},{12,4},{16,0},{20,28},{24,8},{28,20},{1,17},{... | collective-permute-start | bytes 393224 | tf_op jit(solution)/shard_map/ppermute | solution.py:960
  79.8 10.5 %collective-permute-start.22 = (bf16[1,8,64,512]{3,2,1,0:T(8,128)(2,1)S(1)}, bf16[1,8,64,512]{3,2,1,0:T(8,128)(2,1)S(1)}, u32[]{:S(2)}, u32[]{:S(2)}) collective-permute-start(bf16[1,8,64,512]{3,2,1,0:T(8,128)(2,1)S(1)} %collective-permute-done.19.refs_7_), channel_id=1, source_target_pairs={{0,4},{4,0},{8,12},{12,8},{16,20},{20,16},{24,28},{28,24},{1,5},{5... | collective-permute-start | bytes 1572872 | tf_op jit(solution)/shard_map/ppermute | solution.py:960
  82.6 11.4 %collective-permute-start.25 = (bf16[1,8,64,512]{3,2,1,0:T(8,128)(2,1)S(1)}, bf16[1,8,64,512]{3,2,1,0:T(8,128)(2,1)S(1)}, u32[]{:S(2)}, u32[]{:S(2)}) collective-permute-start(bf16[1,8,64,512]{3,2,1,0:T(8,128)(2,1)S(1)} %pack_ffn.3.refs_0_.refs_4_), channel_id=1, source_target_pairs={{0,16},{4,12},{8,24},{12,4},{16,0},{20,28},{24,8},{28,20},{1,17},{... | collective-permute-start | bytes 1572872 | tf_op jit(solution)/shard_map/ppermute | solution.py:960
  85.8 8.4 %collective-permute-start.23 = (bf16[1,8,64,512]{3,2,1,0:T(8,128)(2,1)S(1)}, bf16[1,8,64,512]{3,2,1,0:T(8,128)(2,1)S(1)}, u32[]{:S(2)}, u32[]{:S(2)}) collective-permute-start(bf16[1,8,64,512]{3,2,1,0:T(8,128)(2,1)S(1)} %gate.7.refs_0_.refs_8_), channel_id=1, source_target_pairs={{0,4},{4,0},{8,12},{12,8},{16,20},{20,16},{24,28},{28,24},{1,5},{5... | collective-permute-start | bytes 1572872 | tf_op jit(solution)/shard_map/ppermute | solution.py:960
  88.3 11.2 %collective-permute-start.26 = (bf16[1,8,64,512]{3,2,1,0:T(8,128)(2,1)S(1)}, bf16[1,8,64,512]{3,2,1,0:T(8,128)(2,1)S(1)}, u32[]{:S(2)}, u32[]{:S(2)}) collective-permute-start(bf16[1,8,64,512]{3,2,1,0:T(8,128)(2,1)S(1)} %gate.8.refs_0_.refs_6_), channel_id=1, source_target_pairs={{0,16},{4,12},{8,24},{12,4},{16,0},{20,28},{24,8},{28,20},{1,17},{... | collective-permute-start | bytes 1572872 | tf_op jit(solution)/shard_map/ppermute | solution.py:960
  89.9 9.7 %collective-permute-start.24 = (bf16[1,8,64,512]{3,2,1,0:T(8,128)(2,1)S(1)}, bf16[1,8,64,512]{3,2,1,0:T(8,128)(2,1)S(1)}, u32[]{:S(2)}, u32[]{:S(2)}) collective-permute-start(bf16[1,8,64,512]{3,2,1,0:T(8,128)(2,1)S(1)} %collective-permute-done.20.refs_9_), channel_id=1, source_target_pairs={{0,4},{4,0},{8,12},{12,8},{16,20},{20,16},{24,28},{28,24},{1,5},{5... | collective-permute-start | bytes 1572872 | tf_op jit(solution)/shard_map/ppermute | solution.py:960
  90.3 16.4 %collective-permute-start.27 = (bf16[1,8,64,512]{3,2,1,0:T(8,128)(2,1)S(1)}, bf16[1,8,64,512]{3,2,1,0:T(8,128)(2,1)S(1)}, u32[]{:S(2)}, u32[]{:S(2)}) collective-permute-start(bf16[1,8,64,512]{3,2,1,0:T(8,128)(2,1)S(1)} %pack_ffn.3.refs_0_.refs_4_), channel_id=1, source_target_pairs={{0,4},{4,0},{8,12},{12,8},{16,20},{20,16},{24,28},{28,24},{1,5},{5... | collective-permute-start | bytes 1572872 | tf_op jit(solution)/shard_map/ppermute | solution.py:960
  94.0 12.8 %collective-permute-start.29 = (bf16[1,8,64,512]{3,2,1,0:T(8,128)(2,1)S(1)}, bf16[1,8,64,512]{3,2,1,0:T(8,128)(2,1)S(1)}, u32[]{:S(2)}, u32[]{:S(2)}) collective-permute-start(bf16[1,8,64,512]{3,2,1,0:T(8,128)(2,1)S(1)} %gate.8.refs_0_.refs_6_), channel_id=1, source_target_pairs={{0,4},{4,0},{8,12},{12,8},{16,20},{20,16},{24,28},{28,24},{1,5},{5... | collective-permute-start | bytes 1572872 | tf_op jit(solution)/shard_map/ppermute | solution.py:960
  94.2 12.5 %collective-permute-start.28 = (bf16[1,8,64,512]{3,2,1,0:T(8,128)(2,1)S(1)}, bf16[1,8,64,512]{3,2,1,0:T(8,128)(2,1)S(1)}, u32[]{:S(2)}, u32[]{:S(2)}) collective-permute-start(bf16[1,8,64,512]{3,2,1,0:T(8,128)(2,1)S(1)} %collective-permute-done.25.refs_5_), channel_id=1, source_target_pairs={{0,4},{4,0},{8,12},{12,8},{16,20},{20,16},{24,28},{28,24},{1,5},{5... | collective-permute-start | bytes 1572872 | tf_op jit(solution)/shard_map/ppermute | solution.py:960
  114.0 15.7 %collective-permute-start.31 = (bf16[8,8,64,512]{3,2,1,0:T(8,128)(2,1)}, bf16[8,8,64,512]{3,2,1,0:T(8,128)(2,1)}, u32[]{:S(2)}, u32[]{:S(2)}) collective-permute-start(bf16[8,8,64,512]{3,2,1,0:T(8,128)(2,1)} %get-tuple-element.109.refs_2_.refs_4_), channel_id=1, source_target_pairs={{0,4},{4,0},{8,12},{12,8},{16,20},{20,16},{24,28},{28,24},{1,5},{5... | collective-permute-start | bytes 12582920 | tf_op jit(solution)/shard_map/ppermute | solution.py:960
  126.2 22.8 %collective-permute-start.33 = (bf16[8,4,64,512]{3,2,1,0:T(8,128)(2,1)S(1)}, bf16[8,4,64,512]{3,2,1,0:T(8,128)(2,1)S(1)}, u32[]{:S(2)}, u32[]{:S(2)}) collective-permute-start(bf16[8,4,64,512]{3,2,1,0:T(8,128)(2,1)S(1)} %get-tuple-element.116.refs_2_.refs_4_), channel_id=1, source_target_pairs={{0,4},{4,0},{8,12},{12,8},{16,20},{20,16},{24,28},{28,24},{1,5},{5... | collective-permute-start | bytes 6291464 | tf_op jit(solution)/shard_map/ppermute | solution.py:960
  129.2 19.9 %collective-permute-start.34 = (bf16[8,4,64,512]{3,2,1,0:T(8,128)(2,1)S(1)}, bf16[8,4,64,512]{3,2,1,0:T(8,128)(2,1)S(1)}, u32[]{:S(2)}, u32[]{:S(2)}) collective-permute-start(bf16[8,4,64,512]{3,2,1,0:T(8,128)(2,1)S(1)} %get-tuple-element.117.refs_6_.refs_8_), channel_id=1, source_target_pairs={{0,4},{4,0},{8,12},{12,8},{16,20},{20,16},{24,28},{28,24},{1,5},{5... | collective-permute-start | bytes 6291464 | tf_op jit(solution)/shard_map/ppermute | solution.py:960
  132.3 14.9 %collective-permute-start.32 = (bf16[2,8,64,512]{3,2,1,0:T(8,128)(2,1)S(1)}, bf16[2,8,64,512]{3,2,1,0:T(8,128)(2,1)S(1)}, u32[]{:S(2)}, u32[]{:S(2)}) collective-permute-start(bf16[2,8,64,512]{3,2,1,0:T(8,128)(2,1)S(1)} %get-tuple-element.114), channel_id=1, source_target_pairs={{0,8},{4,20},{8,0},{12,28},{16,24},{20,4},{24,16},{28,12},{1,9},{5... | collective-permute-start | bytes 3145736 | tf_op jit(solution)/shard_map/ppermute | solution.py:960
  142.8 26.9 %collective-permute-start.38 = (bf16[8,4,64,512]{3,2,1,0:T(8,128)(2,1)S(1)}, bf16[8,4,64,512]{3,2,1,0:T(8,128)(2,1)S(1)}, u32[]{:S(2)}, u32[]{:S(2)}) collective-permute-start(bf16[8,4,64,512]{3,2,1,0:T(8,128)(2,1)S(1)} %get-tuple-element.124.refs_2_.refs_4_), channel_id=1, source_target_pairs={{0,4},{4,0},{8,12},{12,8},{16,20},{20,16},{24,28},{28,24},{1,5},{5... | collective-permute-start | bytes 6291464 | tf_op jit(solution)/shard_map/ppermute | solution.py:960
  142.9 7.4 %collective-permute-start.35 = (bf16[1,128,512]{2,1,0:T(8,128)(2,1)S(1)}, bf16[1,128,512]{2,1,0:T(8,128)(2,1)S(1)}, u32[]{:S(2)}, u32[]{:S(2)}) collective-permute-start(bf16[1,128,512]{2,1,0:T(8,128)(2,1)S(1)} %get-tuple-element.108.refs_1_.refs_3_), channel_id=1, source_target_pairs={{0,8},{4,20},{8,0},{12,28},{16,24},{20,4},{24,16},{28,12},{1,9},{5... | collective-permute-start | bytes 393224 | tf_op jit(solution)/shard_map/ppermute | solution.py:960
  147.4 14.8 %collective-permute-start.36 = (bf16[1,8,64,512]{3,2,1,0:T(8,128)(2,1)S(1)}, bf16[1,8,64,512]{3,2,1,0:T(8,128)(2,1)S(1)}, u32[]{:S(2)}, u32[]{:S(2)}) collective-permute-start(bf16[1,8,64,512]{3,2,1,0:T(8,128)(2,1)S(1)} %get-tuple-element.121), channel_id=1, source_target_pairs={{0,16},{4,12},{8,24},{12,4},{16,0},{20,28},{24,8},{28,20},{1,17},{... | collective-permute-start | bytes 1572872 | tf_op jit(solution)/shard_map/ppermute | solution.py:960
  149.6 18.0 %collective-permute-start.37 = (bf16[2,8,64,512]{3,2,1,0:T(8,128)(2,1)S(1)}, bf16[2,8,64,512]{3,2,1,0:T(8,128)(2,1)S(1)}, u32[]{:S(2)}, u32[]{:S(2)}) collective-permute-start(bf16[2,8,64,512]{3,2,1,0:T(8,128)(2,1)S(1)} %get-tuple-element.122), channel_id=1, source_target_pairs={{0,8},{4,20},{8,0},{12,28},{16,24},{20,4},{24,16},{28,12},{1,9},{5... | collective-permute-start | bytes 3145736 | tf_op jit(solution)/shard_map/ppermute | solution.py:960
  160.0 27.8 %collective-permute-start.42 = (bf16[8,4,64,512]{3,2,1,0:T(8,128)(2,1)S(1)}, bf16[8,4,64,512]{3,2,1,0:T(8,128)(2,1)S(1)}, u32[]{:S(2)}, u32[]{:S(2)}) collective-permute-start(bf16[8,4,64,512]{3,2,1,0:T(8,128)(2,1)S(1)} %get-tuple-element.134.refs_2_.refs_4_), channel_id=1, source_target_pairs={{0,4},{4,0},{8,12},{12,8},{16,20},{20,16},{24,28},{28,24},{1,5},{5... | collective-permute-start | bytes 6291464 | tf_op jit(solution)/shard_map/ppermute | solution.py:960
  160.1 22.5 %collective-permute-start.43 = (bf16[1,128,512]{2,1,0:T(8,128)(2,1)S(1)}, bf16[1,128,512]{2,1,0:T(8,128)(2,1)S(1)}, u32[]{:S(2)}, u32[]{:S(2)}) collective-permute-start(bf16[1,128,512]{2,1,0:T(8,128)(2,1)S(1)} %get-tuple-element.108.refs_1_.refs_3_), channel_id=1, source_target_pairs={{0,16},{4,12},{8,24},{12,4},{16,0},{20,28},{24,8},{28,20},{1,17},{... | collective-permute-start | bytes 393224 | tf_op jit(solution)/shard_map/ppermute | solution.py:960
  162.3 19.9 %collective-permute-start.39 = (bf16[8,64,512]{2,1,0:T(8,128)(2,1)S(1)}, bf16[8,64,512]{2,1,0:T(8,128)(2,1)S(1)}, u32[]{:S(2)}, u32[]{:S(2)}) collective-permute-start(bf16[8,64,512]{2,1,0:T(8,128)(2,1)S(1)} %bitcast.41), channel_id=1, source_target_pairs={{0,1},{3,2},{4,5},{7,6},{8,9},{11,10},{12,13},{15,14},{16,17},{19,... | collective-permute-start | bytes 1572872 | tf_op jit(solution)/shard_map/ppermute | solution.py:1047
  167.8 15.3 %collective-permute-start.40 = (bf16[1,8,64,512]{3,2,1,0:T(8,128)(2,1)S(1)}, bf16[1,8,64,512]{3,2,1,0:T(8,128)(2,1)S(1)}, u32[]{:S(2)}, u32[]{:S(2)}) collective-permute-start(bf16[1,8,64,512]{3,2,1,0:T(8,128)(2,1)S(1)} %get-tuple-element.131), channel_id=1, source_target_pairs={{0,16},{4,12},{8,24},{12,4},{16,0},{20,28},{24,8},{28,20},{1,17},{... | collective-permute-start | bytes 1572872 | tf_op jit(solution)/shard_map/ppermute | solution.py:960
  170.0 17.2 %collective-permute-start.41 = (bf16[2,4,64,512]{3,2,1,0:T(8,128)(2,1)S(1)}, bf16[2,4,64,512]{3,2,1,0:T(8,128)(2,1)S(1)}, u32[]{:S(2)}, u32[]{:S(2)}) collective-permute-start(bf16[2,4,64,512]{3,2,1,0:T(8,128)(2,1)S(1)} %get-tuple-element.132), channel_id=1, source_target_pairs={{0,8},{4,20},{8,0},{12,28},{16,24},{20,4},{24,16},{28,12},{1,9},{5... | collective-permute-start | bytes 1572872 | tf_op jit(solution)/shard_map/ppermute | solution.py:960
  183.1 12.1 %collective-permute-start.46 = (bf16[1,128,512]{2,1,0:T(8,128)(2,1)S(1)}, bf16[1,128,512]{2,1,0:T(8,128)(2,1)S(1)}, u32[]{:S(2)}, u32[]{:S(2)}) collective-permute-start(bf16[1,128,512]{2,1,0:T(8,128)(2,1)S(1)} %collective-permute-done.43.refs_4_), channel_id=1, source_target_pairs={{0,4},{4,0},{8,12},{12,8},{16,20},{20,16},{24,28},{28,24},{1,5},{5... | collective-permute-start | bytes 393224 | tf_op jit(solution)/shard_map/ppermute | solution.py:960
  187.2 8.6 %collective-permute-start.47 = (bf16[1,128,512]{2,1,0:T(8,128)(2,1)S(1)}, bf16[1,128,512]{2,1,0:T(8,128)(2,1)S(1)}, u32[]{:S(2)}, u32[]{:S(2)}) collective-permute-start(bf16[1,128,512]{2,1,0:T(8,128)(2,1)S(1)} %gate.9.refs_0_.refs_5_), channel_id=1, source_target_pairs={{0,4},{4,0},{8,12},{12,8},{16,20},{20,16},{24,28},{28,24},{1,5},{5... | collective-permute-start | bytes 393224 | tf_op jit(solution)/shard_map/ppermute | solution.py:960
  187.2 9.2 %collective-permute-start.48 = (bf16[1,128,512]{2,1,0:T(8,128)(2,1)S(1)}, bf16[1,128,512]{2,1,0:T(8,128)(2,1)S(1)}, u32[]{:S(2)}, u32[]{:S(2)}) collective-permute-start(bf16[1,128,512]{2,1,0:T(8,128)(2,1)S(1)} %collective-permute-done.44.refs_6_), channel_id=1, source_target_pairs={{0,4},{4,0},{8,12},{12,8},{16,20},{20,16},{24,28},{28,24},{1,5},{5... | collective-permute-start | bytes 393224 | tf_op jit(solution)/shard_map/ppermute | solution.py:960
  187.8 21.3 %collective-permute-start.49 = (bf16[8,64,512]{2,1,0:T(8,128)(2,1)S(1)}, bf16[8,64,512]{2,1,0:T(8,128)(2,1)S(1)}, u32[]{:S(2)}, u32[]{:S(2)}) collective-permute-start(bf16[8,64,512]{2,1,0:T(8,128)(2,1)S(1)} %add.44.refs_0_.refs_1_), channel_id=1, source_target_pairs={{1,2},{2,1},{5,6},{6,5},{9,10},{10,9},{13,14},{14,13},{17,18},{18,... | collective-permute-start | bytes 1572872 | tf_op jit(solution)/shard_map/ppermute | solution.py:1047
  188.9 20.5 %collective-permute-start.50 = (bf16[8,64,512]{2,1,0:T(8,128)(2,1)S(1)}, bf16[8,64,512]{2,1,0:T(8,128)(2,1)S(1)}, u32[]{:S(2)}, u32[]{:S(2)}) collective-permute-start(bf16[8,64,512]{2,1,0:T(8,128)(2,1)S(1)} %bitcast.52), channel_id=1, source_target_pairs={{0,1},{3,2},{4,5},{7,6},{8,9},{11,10},{12,13},{15,14},{16,17},{19,... | collective-permute-start | bytes 1572872 | tf_op jit(solution)/shard_map/ppermute | solution.py:1047
  195.2 14.3 %collective-permute-start.51 = (bf16[1,4,64,512]{3,2,1,0:T(8,128)(2,1)S(1)}, bf16[1,4,64,512]{3,2,1,0:T(8,128)(2,1)S(1)}, u32[]{:S(2)}, u32[]{:S(2)}) collective-permute-start(bf16[1,4,64,512]{3,2,1,0:T(8,128)(2,1)S(1)} %get-tuple-element.138), channel_id=1, source_target_pairs={{0,16},{4,12},{8,24},{12,4},{16,0},{20,28},{24,8},{28,20},{1,17},{... | collective-permute-start | bytes 786440 | tf_op jit(solution)/shard_map/ppermute | solution.py:960
  195.8 14.5 %collective-permute-start.52 = (bf16[2,4,64,512]{3,2,1,0:T(8,128)(2,1)S(1)}, bf16[2,4,64,512]{3,2,1,0:T(8,128)(2,1)S(1)}, u32[]{:S(2)}, u32[]{:S(2)}) collective-permute-start(bf16[2,4,64,512]{3,2,1,0:T(8,128)(2,1)S(1)} %get-tuple-element.139), channel_id=1, source_target_pairs={{0,8},{4,20},{8,0},{12,28},{16,24},{20,4},{24,16},{28,12},{1,9},{5... | collective-permute-start | bytes 1572872 | tf_op jit(solution)/shard_map/ppermute | solution.py:960
  197.6 19.8 %collective-permute-start.53 = (bf16[512,512]{1,0:T(8,128)(2,1)S(1)}, bf16[512,512]{1,0:T(8,128)(2,1)S(1)}, u32[]{:S(2)}, u32[]{:S(2)}) collective-permute-start(bf16[512,512]{1,0:T(8,128)(2,1)S(1)} %embed_grads.1.refs_0_.refs_1_), channel_id=1, source_target_pairs={{0,1},{3,2},{4,5},{7,6},{8,9},{11,10},{12,13},{15,14},{16,17},{19,... | collective-permute-start | bytes 1572872 | tf_op jit(solution)/shard_map/ppermute | solution.py:1047
  220.6 21.0 %collective-permute-start.54 = (bf16[8,272,512]{2,1,0:T(8,128)(2,1)S(1)}, bf16[8,272,512]{2,1,0:T(8,128)(2,1)}, u32[]{:S(2)}, u32[]{:S(2)}) collective-permute-start(bf16[8,272,512]{2,1,0:T(8,128)(2,1)S(1)} %enc_weight_grads.1.refs_0_.refs_2_.refs_4_), channel_id=1, source_target_pairs={{0,4},{4,0},{8,12},{12,8},{16,20},{20,16},{24,28},{28,24},{1,5},{5... | collective-permute-start | bytes 6684680 | tf_op jit(solution)/shard_map/ppermute | solution.py:960
  220.7 25.4 %collective-permute-start.56 = (bf16[4,64,512]{2,1,0:T(8,128)(2,1)}, bf16[4,64,512]{2,1,0:T(8,128)(2,1)S(1)}, u32[]{:S(2)}, u32[]{:S(2)}) collective-permute-start(bf16[4,64,512]{2,1,0:T(8,128)(2,1)} %bitcast.58), channel_id=1, source_target_pairs={{0,1},{3,2},{4,5},{7,6},{8,9},{11,10},{12,13},{15,14},{16,17},{19,... | collective-permute-start | bytes 786440 | tf_op jit(solution)/shard_map/ppermute | solution.py:1047
  225.1 27.5 %collective-permute-start.57 = (bf16[8,64,512]{2,1,0:T(8,128)(2,1)}, bf16[8,64,512]{2,1,0:T(8,128)(2,1)S(1)}, u32[]{:S(2)}, u32[]{:S(2)}) collective-permute-start(bf16[8,64,512]{2,1,0:T(8,128)(2,1)} %copy-done.23), channel_id=1, source_target_pairs={{1,2},{2,1},{5,6},{6,5},{9,10},{10,9},{13,14},{14,13},{17,18},{18,... | collective-permute-start | bytes 1572872 | tf_op jit(solution)/shard_map/ppermute | solution.py:1047
  225.8 27.8 %collective-permute-start.58 = (bf16[8,64,512]{2,1,0:T(8,128)(2,1)}, bf16[8,64,512]{2,1,0:T(8,128)(2,1)S(1)}, u32[]{:S(2)}, u32[]{:S(2)}) collective-permute-start(bf16[8,64,512]{2,1,0:T(8,128)(2,1)} %copy-done.21), channel_id=1, source_target_pairs={{1,0},{2,3},{5,4},{6,7},{9,8},{10,11},{13,12},{14,15},{17,16},{18,... | collective-permute-start | bytes 1572872 | tf_op jit(solution)/shard_map/ppermute | solution.py:1047
  227.1 18.2 %collective-permute-start.55 = (bf16[1,4,64,512]{3,2,1,0:T(8,128)(2,1)}, bf16[1,4,64,512]{3,2,1,0:T(8,128)(2,1)S(1)}, u32[]{:S(2)}, u32[]{:S(2)}) collective-permute-start(bf16[1,4,64,512]{3,2,1,0:T(8,128)(2,1)} %copy-done.45), channel_id=1, source_target_pairs={{0,16},{4,12},{8,24},{12,4},{16,0},{20,28},{24,8},{28,20},{1,17},{... | collective-permute-start | bytes 786440 | tf_op jit(solution)/shard_map/ppermute | solution.py:960
  241.6 14.5 %collective-permute-start.59 = (bf16[512,512]{1,0:T(8,128)(2,1)S(1)}, bf16[512,512]{1,0:T(8,128)(2,1)S(1)}, u32[]{:S(2)}, u32[]{:S(2)}) collective-permute-start(bf16[512,512]{1,0:T(8,128)(2,1)S(1)} %copy-done.26), channel_id=1, source_target_pairs={{1,2},{2,1},{5,6},{6,5},{9,10},{10,9},{13,14},{14,13},{17,18},{18,... | collective-permute-start | bytes 1572872 | tf_op jit(solution)/shard_map/ppermute | solution.py:1047
  245.3 12.5 %collective-permute-start.60 = (bf16[2,272,512]{2,1,0:T(8,128)(2,1)S(1)}, bf16[2,272,512]{2,1,0:T(8,128)(2,1)S(1)}, u32[]{:S(2)}, u32[]{:S(2)}) collective-permute-start(bf16[2,272,512]{2,1,0:T(8,128)(2,1)S(1)} %get-tuple-element.151), channel_id=1, source_target_pairs={{0,8},{4,20},{8,0},{12,28},{16,24},{20,4},{24,16},{28,12},{1,9},{5... | collective-permute-start | bytes 1671176 | tf_op jit(solution)/shard_map/ppermute | solution.py:960
  246.2 12.9 %collective-permute-start.61 = (bf16[4,64,512]{2,1,0:T(8,128)(2,1)S(1)}, bf16[4,64,512]{2,1,0:T(8,128)(2,1)S(1)}, u32[]{:S(2)}, u32[]{:S(2)}) collective-permute-start(bf16[4,64,512]{2,1,0:T(8,128)(2,1)S(1)} %bitcast.60), channel_id=1, source_target_pairs={{0,1},{3,2},{4,5},{7,6},{8,9},{11,10},{12,13},{15,14},{16,17},{19,... | collective-permute-start | bytes 786440 | tf_op jit(solution)/shard_map/ppermute | solution.py:1047
  253.6 16.8 %collective-permute-start.63 = (bf16[8,64,512]{2,1,0:T(8,128)(2,1)S(1)}, bf16[8,64,512]{2,1,0:T(8,128)(2,1)S(1)}, u32[]{:S(2)}, u32[]{:S(2)}) collective-permute-start(bf16[8,64,512]{2,1,0:T(8,128)(2,1)S(1)} %add.52.refs_0_.refs_2_), channel_id=1, source_target_pairs={{1,0},{2,3},{5,4},{6,7},{9,8},{10,11},{13,12},{14,15},{17,16},{18,... | collective-permute-start | bytes 1572872 | tf_op jit(solution)/shard_map/ppermute | solution.py:1047
  256.2 25.4 %collective-permute-start.64 = (bf16[512,512]{1,0:T(8,128)(2,1)S(1)}, bf16[512,512]{1,0:T(8,128)(2,1)S(1)}, u32[]{:S(2)}, u32[]{:S(2)}) collective-permute-start(bf16[512,512]{1,0:T(8,128)(2,1)S(1)} %add.53.refs_0_.refs_2_), channel_id=1, source_target_pairs={{1,0},{2,3},{5,4},{6,7},{9,8},{10,11},{13,12},{14,15},{17,16},{18,... | collective-permute-start | bytes 1572872 | tf_op jit(solution)/shard_map/ppermute | solution.py:1047
  258.0 24.8 %collective-permute-start.65 = (bf16[1,272,512]{2,1,0:T(8,128)(2,1)S(1)}, bf16[1,272,512]{2,1,0:T(8,128)(2,1)S(1)}, u32[]{:S(2)}, u32[]{:S(2)}) collective-permute-start(bf16[1,272,512]{2,1,0:T(8,128)(2,1)S(1)} %get-tuple-element.153), channel_id=1, source_target_pairs={{0,16},{4,12},{8,24},{12,4},{16,0},{20,28},{24,8},{28,20},{1,17},{... | collective-permute-start | bytes 835592 | tf_op jit(solution)/shard_map/ppermute | solution.py:960
  259.1 24.9 %collective-permute-start.66 = (bf16[4,64,512]{2,1,0:T(8,128)(2,1)S(1)}, bf16[4,64,512]{2,1,0:T(8,128)(2,1)S(1)}, u32[]{:S(2)}, u32[]{:S(2)}) collective-permute-start(bf16[4,64,512]{2,1,0:T(8,128)(2,1)S(1)} %add.54.refs_0_.refs_1_), channel_id=1, source_target_pairs={{1,2},{2,1},{5,6},{6,5},{9,10},{10,9},{13,14},{14,13},{17,18},{18,... | collective-permute-start | bytes 786440 | tf_op jit(solution)/shard_map/ppermute | solution.py:1047
  259.9 27.3 %collective-permute-start.67 = (bf16[4,64,512]{2,1,0:T(8,128)(2,1)S(1)}, bf16[4,64,512]{2,1,0:T(8,128)(2,1)S(1)}, u32[]{:S(2)}, u32[]{:S(2)}) collective-permute-start(bf16[4,64,512]{2,1,0:T(8,128)(2,1)S(1)} %add.55.refs_0_.refs_2_), channel_id=1, source_target_pairs={{1,0},{2,3},{5,4},{6,7},{9,8},{10,11},{13,12},{14,15},{17,16},{18,... | collective-permute-start | bytes 786440 | tf_op jit(solution)/shard_map/ppermute | solution.py:1047
  282.8 10.4 %collective-permute-start.68 = (bf16[272,512]{1,0:T(8,128)(2,1)S(1)}, bf16[272,512]{1,0:T(8,128)(2,1)S(1)}, u32[]{:S(2)}, u32[]{:S(2)}) collective-permute-start(bf16[272,512]{1,0:T(8,128)(2,1)S(1)} %bitcast.54), channel_id=1, source_target_pairs={{0,1},{1,0},{2,3},{3,2},{4,5},{5,4},{6,7},{7,6},{8,9},{9,8},{10,11... | collective-permute-start | bytes 835592 | tf_op jit(solution)/shard_map/ppermute | solution.py:1047
  284.1 14.7 %collective-permute-start.69 = (bf16[4,64,512]{2,1,0:T(8,128)(2,1)S(1)}, bf16[4,64,512]{2,1,0:T(8,128)(2,1)S(1)}, u32[]{:S(2)}, u32[]{:S(2)}) collective-permute-start(bf16[4,64,512]{2,1,0:T(8,128)(2,1)S(1)} %add.57.refs_0_.refs_2_), channel_id=1, source_target_pairs={{1,0},{2,3},{5,4},{6,7},{9,8},{10,11},{13,12},{14,15},{17,16},{18,... | collective-permute-start | bytes 786440 | tf_op jit(solution)/shard_map/ppermute | solution.py:1047
  293.3 10.9 %collective-permute-start.70 = (bf16[272,512]{1,0:T(8,128)(2,1)S(1)}, bf16[272,512]{1,0:T(8,128)(2,1)S(1)}, u32[]{:S(2)}, u32[]{:S(2)}) collective-permute-start(bf16[272,512]{1,0:T(8,128)(2,1)S(1)} %add.58.refs_0_.refs_1_), channel_id=1, source_target_pairs={{0,2},{1,3},{2,0},{3,1},{4,6},{5,7},{6,4},{7,5},{8,10},{9,11},{10,... | collective-permute-start | bytes 835592 | tf_op jit(solution)/shard_map/ppermute | solution.py:1047
  (109 other events, 781.5 us)
